TPU v7x, 32 devices: a whole 2x2x4 slice. The times are simulated.
32 devices in a mesh: gx: 8 (over z, core), gy: 4 (over y, x).
Axes of the slice: x: 2, y: 2, z: 4, core: 2. Of those that a mesh axis runs over, the one named last changes fastest.
Arguments:
- adjoint_fields: float32 [6, 64, 128, 128], P(None, 'gx', 'gy'), may hold values from -6 to 6
- forward_e: bfloat16 [4, 3, 64, 128, 128], P(None, None, 'gx', 'gy'), may hold values from -6 to 6
- permittivity: float32 [64, 128, 128], P('gx', 'gy'), may hold values from 1 to 12
- design_mask: int32 [64, 128, 128], P('gx', 'gy'), may hold values 0 or 1
- band_offsets: int32 [9], replicated, may hold values from -16 to 16, as said below
- filter_taps: float32 [9], replicated, may hold values from 0.05 to 0.5
Outputs:
- filtered: float32 [64, 128, 128], P('gx', 'gy')
- adjoint_e: float32 [3, 64, 128, 128], P(None, 'gx', 'gy')
Inputs may be any that keep to these rules, and one draw needn't show every extreme that they name: `band_offsets`: the offsets are distinct; both -16 and 16 occur.
All inputs are finite; a program needn't handle non-finite values. No bound on the sum of `design_mask` on one device may be relied on, other than what follows from the above.
Results may differ from a plain program's by a relative error of at most 0.0003.
Values sent between devices are 32-bit elements; how exact they have to be, the bound alone decides.
No kernel may reach another device: no remote copies, remote signals or barrier semaphores. Data moves between devices by JAX's collectives and lax.ppermute only.
A program may use at most 64 MiB of HBM per device.

v0:
```python
import jax
import jax.numpy as jnp
from jax import lax
from jax.sharding import PartitionSpec as P

ITERS = 4


courant = 0.5


def with_halo(cells, sides, width):
    for axis, dim in sides:
        count = lax.axis_size(axis)
        ends = count - 1
        head = lax.slice_in_dim(cells, 0, width, axis=dim)
        tail = lax.slice_in_dim(cells, cells.shape[dim] - width, cells.shape[dim], axis=dim)
        cells = jnp.concatenate(
            [
                lax.ppermute(tail, axis, [(i, (i + 1) % count) for i in range(ends)]),
                cells,
                lax.ppermute(head, axis, [((i + 1) % count, i) for i in range(ends)]),
            ],
            axis=dim,
        )
    return cells


def blank_plane(quantity, along):
    return jnp.zeros_like(lax.index_in_dim(quantity, 0, along, keepdims=False))


def forward_diff(quantity, along, border):
    remainder = lax.slice_in_dim(quantity, 1, quantity.shape[along], axis=along)
    joined = jnp.concatenate([remainder, jnp.expand_dims(border, along)], along)
    return joined - quantity


def backward_diff(quantity, along, border):
    remainder = lax.slice_in_dim(quantity, 0, quantity.shape[along] - 1, axis=along)
    joined = jnp.concatenate([jnp.expand_dims(border, along), remainder], along)
    return quantity - joined


def update_magnetic(electric, magnetic, after_x, after_y):
    elec_x, elec_y, elec_z = electric
    magn_x, magn_y, magn_z = magnetic
    magn_x = magn_x - courant * (
        forward_diff(elec_z, 1, after_y[1]) - forward_diff(elec_y, 2, blank_plane(elec_y, 2))
    )
    magn_y = magn_y - courant * (
        forward_diff(elec_x, 2, blank_plane(elec_x, 2)) - forward_diff(elec_z, 0, after_x[1])
    )
    magn_z = magn_z - courant * (
        forward_diff(elec_y, 0, after_x[0]) - forward_diff(elec_x, 1, after_y[0])
    )
    return (magn_x, magn_y, magn_z)


def update_electric(electric, magnetic, factor, before_x, before_y):
    elec_x, elec_y, elec_z = electric
    magn_x, magn_y, magn_z = magnetic
    elec_x = elec_x + factor * (
        backward_diff(magn_z, 1, before_y[1]) - backward_diff(magn_y, 2, blank_plane(magn_y, 2))
    )
    elec_y = elec_y + factor * (
        backward_diff(magn_x, 2, blank_plane(magn_x, 2)) - backward_diff(magn_z, 0, before_x[1])
    )
    elec_z = elec_z + factor * (
        backward_diff(magn_y, 0, before_x[0]) - backward_diff(magn_x, 1, before_y[0])
    )
    return (elec_x, elec_y, elec_z)


def intersection(stored, electric):
    stored = stored.astype(jnp.float32)
    return stored[0] * electric[0] + stored[1] * electric[1] + stored[2] * electric[2]


def apply_band(pencil, band_offsets, filter_taps):
    total = pencil.shape[0]
    reach = total // 4
    padded = jnp.pad(pencil, ((reach, reach), (0, 0)))
    result = jnp.zeros(pencil.shape, jnp.float32)
    for index in range(band_offsets.shape[0]):
        start = reach + band_offsets[index]
        result = result + filter_taps[index] * lax.dynamic_slice_in_dim(padded, start, total, 0)
    return result


def shards(adjoint_fields, forward_e, permittivity, design_mask, band_offsets, filter_taps):
    width_x, width_y, width_z = permittivity.shape
    gradient = jnp.zeros(permittivity.shape, jnp.float32)
    margin = ITERS
    block = jnp.concatenate([adjoint_fields, permittivity[None]], 0)
    extended = with_halo(block, (("gx", 1), ("gy", 2)), margin)
    total_x = width_x * lax.axis_size("gx")
    total_y = width_y * lax.axis_size("gy")
    place_x = (
        lax.axis_index("gx") * width_x - margin + jnp.arange(width_x + 2 * margin, dtype=jnp.int32)
    )
    place_y = (
        lax.axis_index("gy") * width_y - margin + jnp.arange(width_y + 2 * margin, dtype=jnp.int32)
    )
    valid_x = (place_x >= 0) & (place_x < total_x)
    valid_y = (place_y >= 0) & (place_y < total_y)
    inside = (valid_x[:, None, None] & valid_y[None, :, None]).astype(jnp.float32)
    factor = courant / jnp.where(inside > 0.5, extended[6], 1.0)
    electric = (extended[0], extended[1], extended[2])
    magnetic = (extended[3], extended[4], extended[5])
    for turn in range(ITERS):
        blanks_x = (blank_plane(electric[1], 0), blank_plane(electric[2], 0))
        blanks_y = (blank_plane(electric[0], 1), blank_plane(electric[2], 1))
        magnetic = update_magnetic(electric, magnetic, blanks_x, blanks_y)
        magnetic = tuple((component * inside for component in magnetic))
        electric = update_electric(electric, magnetic, factor, blanks_x, blanks_y)
        electric = tuple((component * inside for component in electric))
        cropped = tuple(
            (
                component[margin : margin + width_x, margin : margin + width_y]
                for component in electric
            )
        )
        gradient = gradient + intersection(forward_e[turn], cropped)
    final_e = jnp.stack(
        [component[margin : margin + width_x, margin : margin + width_y] for component in electric]
    )
    masked = gradient * design_mask.astype(jnp.float32)
    columns = masked.reshape(width_x, width_y * width_z)
    lines = apply_band(
        lax.all_to_all(columns, "gx", split_axis=1, concat_axis=0, tiled=True),
        band_offsets,
        filter_taps,
    )
    returned = lax.all_to_all(lines, "gx", split_axis=0, concat_axis=1, tiled=True)
    filtered = returned.reshape(width_x, width_y, width_z)
    return (filtered, final_e)


def solution(mesh):
    return jax.shard_map(
        shards,
        mesh=mesh,
        in_specs=(
            P(None, "gx", "gy", None),
            P(None, None, "gx", "gy", None),
            P("gx", "gy", None),
            P("gx", "gy", None),
            P(),
            P(),
        ),
        out_specs=(P("gx", "gy", None), P(None, "gx", "gy", None)),
        check_vma=False,
    )
```

profile of v0, /device:TPU:0, one launch (start us, length us, event | category | flops | bytes accessed | tf_op | source)
XLA Modules:
  0.0 74.4 jit_solution(5370488144277874593)
XLA Ops:
  0.6 1.3 %fusion = (f32[7,4,32,128]{3,2,1,0:T(8,128)S(1)}, f32[7,4,32,128]{3,2,1,0:T(8,128)S(1)}) fusion(f32[6,8,32,128]{3,2,1,0:T(8,128)} %param.6, f32[1,8,32,128]{3,2,1,0:T(8,128)} %bitcast.194), kind=kLoop, calls=%fused_computation.3 | loop fusion | flops 229376 | bytes 1835008 | tf_op jit(solution)/shard_map/concatenate | solution.py:95
  2.0 2.4 %collective-permute-start = (f32[7,4,32,128]{3,2,1,0:T(8,128)S(1)}, f32[7,4,32,128]{3,2,1,0:T(8,128)S(1)}, u32[]{:S(2)}, u32[]{:S(2)}) collective-permute-start(f32[7,4,32,128]{3,2,1,0:T(8,128)S(1)} %get-tuple-element.20), channel_id=1, source_target_pairs={{0,4},{4,8},{8,12},{12,16},{16,20},{20,24},{24,28},{1,5},{5,9},{9,... | collective-permute-start | bytes 1376264 | tf_op jit(solution)/shard_map/ppermute | solution.py:20
  4.4 1.3 %collective-permute-start.1 = (f32[7,4,32,128]{3,2,1,0:T(8,128)S(1)}, f32[7,4,32,128]{3,2,1,0:T(8,128)S(1)}, u32[]{:S(2)}, u32[]{:S(2)}) collective-permute-start(f32[7,4,32,128]{3,2,1,0:T(8,128)S(1)} %get-tuple-element.21), channel_id=1, source_target_pairs={{4,0},{8,4},{12,8},{16,12},{20,16},{24,20},{28,24},{5,1},{9,5},{13... | collective-permute-start | bytes 1376264 | tf_op jit(solution)/shard_map/ppermute | solution.py:22
  5.9 4.4 %collective-permute-done.1 = f32[7,4,32,128]{3,2,1,0:T(8,128)S(1)} collective-permute-done((f32[7,4,32,128]{3,2,1,0:T(8,128)S(1)}, f32[7,4,32,128]{3,2,1,0:T(8,128)S(1)}, u32[]{:S(2)}, u32[]{:S(2)}) %collective-permute-start.1) | collective-permute-done | bytes 458784 | tf_op jit(solution)/shard_map/ppermute | solution.py:22
  10.2 0.9 %pad_maximum_fusion.6 = (f32[7,16,4,128]{3,2,1,0:T(4,128)S(1)}, f32[7,16,4,128]{3,2,1,0:T(4,128)S(1)}) fusion(f32[7,4,32,128]{3,2,1,0:T(8,128)S(1)} %collective-permute-done.1, f32[7,4,32,128]{3,2,1,0:T(8,128)S(1)} %collective-permute-done, f32[1,8,32,128]{3,2,1,0:T(8,128)} %bitcast.195, f32[6,8,32,128]{3,2,1,0:T(8,128)S(1)} %copy-done), kind=kLoop, calls=%fused_computation.53 | loop fusion | flops 344064 | bytes 2293760 | tf_op jit(solution)/shard_map/slice | solution.py:17
  11.1 3.4 %collective-permute-start.2 = (f32[7,16,4,128]{3,2,1,0:T(4,128)S(1)}, f32[7,16,4,128]{3,2,1,0:T(4,128)S(1)}, u32[]{:S(2)}, u32[]{:S(2)}) collective-permute-start(f32[7,16,4,128]{3,2,1,0:T(4,128)S(1)} %get-tuple-element.18), channel_id=1, source_target_pairs={{0,1},{1,2},{2,3},{4,5},{5,6},{6,7},{8,9},{9,10},{10,11},{12,13},{... | collective-permute-start | bytes 688136 | tf_op jit(solution)/shard_map/ppermute | solution.py:20
  14.5 1.3 %collective-permute-start.3 = (f32[7,16,4,128]{3,2,1,0:T(4,128)S(1)}, f32[7,16,4,128]{3,2,1,0:T(4,128)S(1)}, u32[]{:S(2)}, u32[]{:S(2)}) collective-permute-start(f32[7,16,4,128]{3,2,1,0:T(4,128)S(1)} %get-tuple-element.19), channel_id=1, source_target_pairs={{1,0},{2,1},{3,2},{5,4},{6,5},{7,6},{9,8},{10,9},{11,10},{13,12},{... | collective-permute-start | bytes 688136 | tf_op jit(solution)/shard_map/ppermute | solution.py:22
  16.1 2.0 %collective-permute-done.2 = f32[7,16,4,128]{3,2,1,0:T(4,128)S(1)} collective-permute-done((f32[7,16,4,128]{3,2,1,0:T(4,128)S(1)}, f32[7,16,4,128]{3,2,1,0:T(4,128)S(1)}, u32[]{:S(2)}, u32[]{:S(2)}) %collective-permute-start.2) | collective-permute-done | bytes 229408 | tf_op jit(solution)/shard_map/ppermute | solution.py:20
  18.1 4.4 %collective-permute-done.3 = f32[7,16,4,128]{3,2,1,0:T(4,128)S(1)} collective-permute-done((f32[7,16,4,128]{3,2,1,0:T(4,128)S(1)}, f32[7,16,4,128]{3,2,1,0:T(4,128)S(1)}, u32[]{:S(2)}, u32[]{:S(2)}) %collective-permute-start.3) | collective-permute-done | bytes 229408 | tf_op jit(solution)/shard_map/ppermute | solution.py:22
  22.5 0.4 pad_maximum_fusion
  23.7 0.4 add_multiply_fusion.8
  25.2 0.5 add_multiply_fusion.5
  26.5 0.5 add_multiply_fusion.2
  27.8 0.5 copy-done.3
  28.3 0.5 fusion.34
  28.9 0.7 copy.10
  29.6 12.9 %all-to-all-start = ((f32[8,8,512]{2,0,1:T(8,128)}), f32[8,8,512]{2,0,1:T(8,128)S(1)}, u32[]{:S(2)}, u32[]{:S(2)}) async-start(f32[8,8,512]{2,0,1:T(8,128)} %copy.10), calls=%async_computation | async-start | bytes 262144 | tf_op jit(solution)/shard_map/all_to_all | solution.py:131
  42.6 0.7 fusion.62
  54.6 0.7 fusion.61
  55.2 6.6 %fusion.18 = f32[8,8,512]{2,1,0:T(8,128)} fusion(s32[]{:T(128)S(6)} %select_n.32, f32[64,512]{1,0:T(8,128)S(1)} %bitcast.200, s32[]{:T(128)S(6)} %select_n.33, s32[]{:T(128)S(6)} %select_n.34, s32[]{:T(128)S(6)} %select_n.35, s32[]{:T(128)S(6)} %select_n.36, s32[]{:T(128)S(6)} %select_n.37, s32[]{:T(128)S(6)} %select_n.38, s32[]{:T(128)S(6)} %select_n.39, ...), kind=kLoop, calls=%fused_computation.67 | loop fusion | flops 557056 | bytes 262216 | tf_op jit(solution)/shard_map/all_to_all | solution.py:135
  61.8 5.1 %all-to-all-start.1 = ((f32[8,8,512]{2,1,0:T(8,128)}), f32[8,8,512]{2,1,0:T(8,128)S(1)}, u32[]{:S(2)}, u32[]{:S(2)}) async-start(f32[8,8,512]{2,1,0:T(8,128)} %fusion.18), calls=%async_computation.1 | async-start | bytes 262144 | tf_op jit(solution)/shard_map/all_to_all | solution.py:135
  66.9 0.8 %pad_maximum_fusion.2 = f32[3,8,32,128]{3,2,1,0:T(8,128)} fusion(f32[1,8,32,128]{3,2,1,0:T(8,128)S(1)} %bitcast.199, f32[1,8,32,128]{3,2,1,0:T(8,128)S(1)} %bitcast.198, f32[1,8,32,128]{3,2,1,0:T(8,128)S(1)} %bitcast.197), kind=kLoop, calls=%fused_computation.5 | loop fusion | flops 196608 | bytes 786432 | tf_op jit(solution)/shard_map/stack | solution.py:125
  67.7 6.0 %all-to-all-done.1 = f32[8,8,512]{2,1,0:T(8,128)S(1)} async-done(((f32[8,8,512]{2,1,0:T(8,128)}), f32[8,8,512]{2,1,0:T(8,128)S(1)}, u32[]{:S(2)}, u32[]{:S(2)}) %all-to-all-start.1) | async-done | bytes 131104 | tf_op jit(solution)/shard_map/all_to_all | solution.py:135
  73.8 0.7 reshape.158
  (57 shorter events, 3.8 us)
Async XLA Ops:
  0.6 9.6 %copy-start = (f32[6,8,32,128]{3,2,1,0:T(8,128)S(1)}, f32[6,8,32,128]{3,2,1,0:T(8,128)}, u32[]{:S(2)}) copy-start(f32[6,8,32,128]{3,2,1,0:T(8,128)} %param.6) | copy-start | bytes 2359300
  0.6 15.2 %copy-start.2 = (bf16[4,3,8,32,128]{4,3,2,1,0:T(8,128)(2,1)S(1)}, bf16[4,3,8,32,128]{4,3,2,1,0:T(8,128)(2,1)}, u32[]{:S(2)}) copy-start(bf16[4,3,8,32,128]{4,3,2,1,0:T(8,128)(2,1)} %param.7) | copy-start | bytes 2359300
  2.0 3.9 %collective-permute-start = (f32[7,4,32,128]{3,2,1,0:T(8,128)S(1)}, f32[7,4,32,128]{3,2,1,0:T(8,128)S(1)}, u32[]{:S(2)}, u32[]{:S(2)}) collective-permute-start(f32[7,4,32,128]{3,2,1,0:T(8,128)S(1)} %get-tuple-element.20), channel_id=1, source_target_pairs={{0,4},{4,8},{8,12},{12,16},{16,20},{20,24},{24,28},{1,5},{5,9},{9,... | collective-permute-start | bytes 1376264 | tf_op jit(solution)/shard_map/ppermute | solution.py:20
  4.4 5.9 %collective-permute-start.1 = (f32[7,4,32,128]{3,2,1,0:T(8,128)S(1)}, f32[7,4,32,128]{3,2,1,0:T(8,128)S(1)}, u32[]{:S(2)}, u32[]{:S(2)}) collective-permute-start(f32[7,4,32,128]{3,2,1,0:T(8,128)S(1)} %get-tuple-element.21), channel_id=1, source_target_pairs={{4,0},{8,4},{12,8},{16,12},{20,16},{24,20},{28,24},{5,1},{9,5},{13... | collective-permute-start | bytes 1376264 | tf_op jit(solution)/shard_map/ppermute | solution.py:22
  5.9 16.6 %copy-start.1 = (f32[8,32,128]{2,1,0:T(8,128)S(1)}, f32[8,32,128]{2,1,0:T(8,128)}, u32[]{:S(2)}) copy-start(f32[8,32,128]{2,1,0:T(8,128)} %param.8) | copy-start | bytes 393220
  11.1 6.9 %collective-permute-start.2 = (f32[7,16,4,128]{3,2,1,0:T(4,128)S(1)}, f32[7,16,4,128]{3,2,1,0:T(4,128)S(1)}, u32[]{:S(2)}, u32[]{:S(2)}) collective-permute-start(f32[7,16,4,128]{3,2,1,0:T(4,128)S(1)} %get-tuple-element.18), channel_id=1, source_target_pairs={{0,1},{1,2},{2,3},{4,5},{5,6},{6,7},{8,9},{9,10},{10,11},{12,13},{... | collective-permute-start | bytes 688136 | tf_op jit(solution)/shard_map/ppermute | solution.py:20
  14.5 7.9 %collective-permute-start.3 = (f32[7,16,4,128]{3,2,1,0:T(4,128)S(1)}, f32[7,16,4,128]{3,2,1,0:T(4,128)S(1)}, u32[]{:S(2)}, u32[]{:S(2)}) collective-permute-start(f32[7,16,4,128]{3,2,1,0:T(4,128)S(1)} %get-tuple-element.19), channel_id=1, source_target_pairs={{1,0},{2,1},{3,2},{5,4},{6,5},{7,6},{9,8},{10,9},{11,10},{13,12},{... | collective-permute-start | bytes 688136 | tf_op jit(solution)/shard_map/ppermute | solution.py:22
  27.4 0.9 %copy-start.3 = (s32[8,32,128]{2,1,0:T(8,128)S(1)}, s32[8,32,128]{2,1,0:T(8,128)}, u32[]{:S(2)}) copy-start(s32[8,32,128]{2,1,0:T(8,128)} %param.9) | copy-start | bytes 393220
  28.3 14.2 %copy-start.4 = (s32[9]{0:T(128)S(1)}, s32[9]{0:T(128)}, u32[]{:S(2)}) copy-start(s32[9]{0:T(128)} %param.10) | copy-start | bytes 112
  28.3 26.2 %copy-start.5 = (f32[9]{0:T(128)S(1)}, f32[9]{0:T(128)}, u32[]{:S(2)}) copy-start(f32[9]{0:T(128)} %param.11) | copy-start | bytes 112
  29.6 25.6 %all-to-all-start = ((f32[8,8,512]{2,0,1:T(8,128)}), f32[8,8,512]{2,0,1:T(8,128)S(1)}, u32[]{:S(2)}, u32[]{:S(2)}) async-start(f32[8,8,512]{2,0,1:T(8,128)} %copy.10), calls=%async_computation | async-start | bytes 262144 | tf_op jit(solution)/shard_map/all_to_all | solution.py:131
  61.8 11.9 %all-to-all-start.1 = ((f32[8,8,512]{2,1,0:T(8,128)}), f32[8,8,512]{2,1,0:T(8,128)S(1)}, u32[]{:S(2)}, u32[]{:S(2)}) async-start(f32[8,8,512]{2,1,0:T(8,128)} %fusion.18), calls=%async_computation.1 | async-start | bytes 262144 | tf_op jit(solution)/shard_map/all_to_all | solution.py:135
where the time goes:
time: 75.1 us; the launch traced here: 74.4 us
  starting transfers between devices  26.4 us (35%)
  waiting for transfers between devices  16.8 us (22%)
  other arithmetic  13.6 us (18%)
  between operations  12.4 us (17%)
  local copies, waits for them, and re-layouts  5.28 us (7%)
    all_to_all x1, starting transfers between devices, shards(): lax.all_to_all(columns, 'gx', split_axis=1, concat_axis=0, tiled=True)  12.9 us
    ppermute x2, waiting for transfers between devices, with_halo(): lax.ppermute(head, axis, [((i + 1) % count, i) for i in range(ends)])  8.79 us
    all_to_all x1, other arithmetic, shards(): lax.all_to_all(lines, 'gx', split_axis=0, concat_axis=1, tiled=True)  6.56 us
    all_to_all x1, waiting for transfers between devices, shards(): lax.all_to_all(lines, 'gx', split_axis=0, concat_axis=1, tiled=True)  6.01 us
    ppermute x2, starting transfers between devices, with_halo(): lax.ppermute(tail, axis, [(i, (i + 1) % count) for i in range(ends)])  5.79 us
    all_to_all x1, starting transfers between devices, shards(): lax.all_to_all(lines, 'gx', split_axis=0, concat_axis=1, tiled=True)  5.09 us
    ppermute x2, starting transfers between devices, with_halo(): lax.ppermute(head, axis, [((i + 1) % count, i) for i in range(ends)])  2.58 us
    ppermute x2, waiting for transfers between devices, with_halo(): lax.ppermute(tail, axis, [(i, (i + 1) % count) for i in range(ends)])  1.99 us
  transfers between devices with their start and end apart: 6, of which 4 were waited for; matrix products, arithmetic and copies ran while one was open for 3% of the time, Pallas kernels for 0%

commit v1 on v0

v1 whole, which is shorter than its diff:
```python
import functools
import jax
import jax.numpy as jnp
from jax import lax
from jax.experimental import pallas as pl
from jax.experimental.pallas import tpu as pltpu
from jax.sharding import PartitionSpec as P

ITERS = 4
COURANT = 0.5
BOTH = ("gx", "gy")
SUB = 8


def swaps(count_x, count_y, partner, idle):
    pairs = []
    for x in range(count_x):
        for y in range(count_y):
            to = partner(x, y)
            if to is None:
                to = idle(x, y)
            pairs.append((x * count_y + y, to[0] * count_y + to[1]))
    assert sorted(b for _, b in pairs) == sorted(a for a, _ in pairs)
    return pairs


class Routes:
    def __init__(self, count_x, count_y):
        self.count_x, self.count_y = count_x, count_y
        half = max(count_y // 2, 1)

        def outward_x(x):
            to = x + 1 if x % 2 else x - 1
            return to if 0 <= to < count_x else None

        def side_b(y):
            to = y + 1 if y % 2 else y - 1
            return to if 0 <= to < count_y else None

        def far_y(x, y):
            return (x, (y + half) % count_y)

        def out_partner(x, y):
            return None if outward_x(x) is None else (outward_x(x), y)

        def b_partner(x, y):
            return None if side_b(y) is None else (x, side_b(y))

        def diag_a(x, y):
            return None if outward_x(x) is None else (outward_x(x), y ^ 1)

        def diag_b(x, y):
            if outward_x(x) is None:
                return None
            return (outward_x(x), y if side_b(y) is None else side_b(y))

        def pair_b(x, y):
            to = (x // 2 + (1 if (x // 2) % 2 else -1)) * 2 + x % 2
            return (to, y) if 0 <= to < count_x else None

        make = functools.partial(swaps, count_x, count_y)
        core = lambda x, y: (x ^ 1, y)
        self.core = make(core, None)
        self.out_x = make(out_partner, far_y)
        self.side_a = make(lambda x, y: (x, y ^ 1), None)
        self.side_b = make(b_partner, core)
        self.diag_a = make(diag_a, lambda x, y: (x, y ^ 1))
        self.diag_b = make(diag_b, far_y)
        self.pair_a = make(lambda x, y: (x ^ 2, y), None)
        self.pair_b = make(pair_b, core)


def depths(margin):
    return (margin, margin, margin, margin - 1, margin, margin, margin - 1)


def pack(margin, fields, perm, out_x, in_x, side_a, side_b, diag_a, diag_b):
    width, rows = perm.shape[0], perm.shape[1]
    core = lax.rem(lax.axis_index("gx"), 2)
    odd = lax.rem(lax.axis_index("gy"), 2)
    low = lax.broadcasted_iota(jnp.int32, (SUB, perm.shape[2]), 0) < SUB // 2

    def plane_of(k, x, where):
        return fields[k, x, where] if k < 6 else perm[x, where]

    at = 0
    for k, depth in enumerate(depths(margin)):
        for j in range(depth):
            out_x[at + j] = plane_of(k, core * (width - depth) + j, slice(None))
            in_x[at + j] = plane_of(k, (1 - core) * (width - depth) + j, slice(None))
        at += depth

    def edge(k, x, x2, upper):
        where = pl.ds(pl.multiple_of(upper * (rows - SUB), SUB), SUB)
        first, second = plane_of(k, x, where), plane_of(k, x2, where)
        up = upper == 1
        first = jnp.where(up, pltpu.roll(first, SUB // 2, 0), first)
        second = jnp.where(up, second, pltpu.roll(second, SUB // 2, 0))
        return jnp.where(low, first, second)

    for k in range(7):
        for j in range(width // 2):
            side_a[k, j] = edge(k, j, j + width // 2, 1 - odd)
            side_b[k, j] = edge(k, j, j + width // 2, odd)
        for j in range(margin // 2):
            x = core * (width - margin) + j
            diag_a[k, j] = edge(k, x, x + margin // 2, 1 - odd)
            diag_b[k, j] = edge(k, x, x + margin // 2, odd)


def steps(margin, count_x, count_y, fields, perm, forward, mask, out_x, in_x, side_a, side_b, diag_a, diag_b, core_a, core_b,
          masked, final, ext, factor, own_sem, forward_buf, forward_sem):
    width, rows, lanes = perm.shape
    at_x, at_y = lax.axis_index("gx"), lax.axis_index("gy")
    core, odd = lax.rem(at_x, 2), lax.rem(at_y, 2)
    half = SUB // 2
    own = pltpu.make_async_copy(fields, ext.at[:, pl.ds(margin, width), pl.ds(0, rows)], own_sem)
    own.start()
    load_forward = pltpu.make_async_copy(forward, forward_buf, forward_sem)
    load_forward.start()

    scale = COURANT * COURANT
    low = lax.broadcasted_iota(jnp.int32, (SUB, lanes), 0) < half
    has_out = jnp.where(core == 0, at_x > 0, at_x < count_x - 1)
    has_after, has_before = at_y < count_y - 1, at_y > 0
    out_at = core * (width + margin)
    in_at = (1 - core) * (width + margin)

    def put(k, x, where, value, valid):
        if k < 6:
            ext[k, x, where] = value if valid is None else jnp.where(valid, value, 0.0)
        else:
            value = scale / value
            factor[x, where] = value if valid is None else jnp.where(valid, value, 0.0)

    body, tail = pl.ds(0, rows), pl.ds(rows, SUB)
    for x in range(width):
        factor[margin + x, body] = scale / perm[x]
    at = 0
    for k, depth in enumerate(depths(margin)):
        for j in range(depth):
            put(k, out_at + (1 - core) * (margin - depth) + j, body, out_x[at + j], has_out)
            put(k, in_at + core * (margin - depth) + j, body, in_x[at + j], None)
        at += depth

    def tail_tile(first, second, upper):
        after = jnp.where(odd == 0, first, second)
        before = jnp.where(odd == 0, second, first)
        if isinstance(upper, int):
            after = pltpu.roll(after, half, 0) if upper else after
            before = before if upper else pltpu.roll(before, half, 0)
        else:
            after = jnp.where(upper == 1, pltpu.roll(after, half, 0), after)
            before = jnp.where(upper == 1, before, pltpu.roll(before, half, 0))
        return jnp.where(low, after, before)

    valid_tail = jnp.where(low, jnp.where(has_after, 1, 0), jnp.where(has_before, 1, 0)) > 0
    valid_corner = valid_tail & jnp.broadcast_to(has_out, (SUB, lanes))
    for k in range(7):
        for j in range(width // 2):
            put(k, margin + j, tail, tail_tile(side_a[k, j], side_b[k, j], 0), valid_tail)
            put(k, margin + j + width // 2, tail, tail_tile(side_a[k, j], side_b[k, j], 1), valid_tail)
        for j in range(margin // 2):
            put(k, out_at + j, tail, tail_tile(diag_a[k, j], diag_b[k, j], 0), valid_corner)
            put(k, out_at + j + margin // 2, tail, tail_tile(diag_a[k, j], diag_b[k, j], 1), valid_corner)
        for j in range(margin):
            tile = core * (width // 2 - margin) + j
            put(k, in_at + j, tail, tail_tile(core_a[k, tile], core_b[k, tile], core), valid_tail)

    lane = lax.broadcasted_iota(jnp.int32, (rows + SUB, lanes), 1)
    first_lane, last_lane = lane == 0, lane == lanes - 1
    before_rows = jnp.where(low | jnp.broadcast_to(has_before, (SUB, lanes)), 1.0, 0.0)
    before_x = jnp.where(at_x > 0, 1.0, 0.0)

    def next_y(f):
        return pltpu.roll(f, rows + SUB - 1, 0)

    def last_y(f):
        return pltpu.roll(f, 1, 0)

    def next_z(f):
        return jnp.where(last_lane, 0.0, pltpu.roll(f, lanes - 1, 1))

    def last_z(f):
        return jnp.where(first_lane, 0.0, pltpu.roll(f, 1, 1))

    own.wait()
    load_forward.wait()
    for turn in range(margin):
        last = turn == margin - 1
        held_y = held_z = None
        for i in range(turn, width + 2 * margin - 1 - turn):
            ex, ey, ez = ext[0, i], ext[1, i], ext[2, i]
            ey_x, ez_x = ext[1, i + 1], ext[2, i + 1]
            hx, hy, hz = ext[3, i], ext[4, i], ext[5, i]
            if turn == 0:
                hx, hy, hz = hx * (1 / COURANT), hy * (1 / COURANT), hz * (1 / COURANT)
            hx = hx - ((next_y(ez) - ez) - (next_z(ey) - ey))
            hy = hy - ((next_z(ex) - ex) - (ez_x - ez))
            hz = hz - ((ey_x - ey) - (next_y(ex) - ex))

            def clear(h):
                h = jnp.concatenate([h[:rows], h[rows:] * before_rows], 0)
                return h * before_x if i < margin else h

            hx, hy, hz = clear(hx), clear(hy), clear(hz)
            if not last:
                ext[3, i], ext[4, i], ext[5, i] = hx, hy, hz
            if i > turn:
                c = factor[i]
                ex = ex + c * ((hz - last_y(hz)) - (hy - last_z(hy)))
                ey = ey + c * ((hx - last_z(hx)) - (hz - held_z))
                ez = ez + c * ((hy - held_y) - (hx - last_y(hx)))
                if not last:
                    ext[0, i], ext[1, i], ext[2, i] = ex, ey, ez
                if margin <= i < margin + width:
                    x = i - margin
                    own_e = (ex[:rows], ey[:rows], ez[:rows])
                    total = sum(forward_buf[turn, a, x].astype(jnp.float32) * own_e[a] for a in range(3))
                    if turn > 0:
                        total = total + masked[x]
                    if last:
                        total = total * mask[x].astype(jnp.float32)
                        for a in range(3):
                            final[a, x] = own_e[a]
                    masked[x] = total
            held_y, held_z = hy, hz


def band(rounds, total, offsets, taps, *refs):
    *blocks, out, line = refs
    width = out.shape[0]
    at_x = lax.axis_index("gx")
    core = lax.rem(at_x, 2)
    for p in range(2 * rounds + 1):
        for x in range(width):
            line[(2 * p + core) * width + x] = blocks[2 * p][x]
            line[(2 * p + 1 - core) * width + x] = blocks[2 * p + 1][x]
    origin = (2 * rounds + core) * width
    for x in range(width):
        result = None
        for b in range(offsets.shape[0]):
            place = at_x * width + x + offsets[b]
            inside = (place >= 0) & (place < total)
            weight = jnp.where(inside, taps[b], 0.0)
            term = weight * line[origin + x + offsets[b]]
            result = term if result is None else result + term
        out[x] = result


def shards(routes, adjoint_fields, forward_e, permittivity, design_mask, band_offsets, filter_taps):
    width, rows, lanes = permittivity.shape
    margin = ITERS
    f32 = jnp.float32
    planes = sum(depths(margin))
    shape = jax.ShapeDtypeStruct
    vmem = pl.BlockSpec(memory_space=pltpu.VMEM)
    smem = pl.BlockSpec(memory_space=pltpu.SMEM)
    anywhere = pl.BlockSpec(memory_space=pl.ANY)
    params = pltpu.CompilerParams(vmem_limit_bytes=24 * 1024 * 1024)
    strip = shape((planes, rows, lanes), f32)
    edge = shape((7, width // 2, SUB, lanes), f32)
    corner = shape((7, margin // 2, SUB, lanes), f32)
    out_x, in_x, side_a, side_b, diag_a, diag_b = pl.pallas_call(
        functools.partial(pack, margin),
        out_shape=(strip, strip, edge, edge, corner, corner),
        in_specs=[vmem] * 2,
        out_specs=(vmem,) * 6,
        compiler_params=params,
        name="pack_borders",
    )(adjoint_fields, permittivity)

    def move(value, pairs):
        return lax.ppermute(value, BOTH, pairs)

    out_x = move(out_x, routes.out_x)
    side_a = move(side_a, routes.side_a)
    side_b = move(side_b, routes.side_b)
    diag_a = move(diag_a, routes.diag_a)
    diag_b = move(diag_b, routes.diag_b)
    in_x = move(in_x, routes.core)
    core_a = move(side_a, routes.core)
    core_b = move(side_b, routes.core)
    masked, final = pl.pallas_call(
        functools.partial(steps, margin, routes.count_x, routes.count_y),
        out_shape=(shape((width, rows, lanes), f32), shape((3, width, rows, lanes), f32)),
        in_specs=[anywhere, vmem, anywhere, vmem] + [vmem] * 8,
        out_specs=(vmem, vmem),
        scratch_shapes=[
            pltpu.VMEM((6, width + 2 * margin, rows + SUB, lanes), f32),
            pltpu.VMEM((width + 2 * margin, rows + SUB, lanes), f32),
            pltpu.SemaphoreType.DMA,
            pltpu.VMEM(forward_e.shape, forward_e.dtype),
            pltpu.SemaphoreType.DMA,
        ],
        compiler_params=params,
        name="yee_steps",
    )(adjoint_fields, permittivity, forward_e, design_mask, out_x, in_x, side_a, side_b, diag_a, diag_b, core_a, core_b)

    total = width * routes.count_x
    rounds = -(-(total // 4) // (2 * width))
    odd_pair = lax.rem(lax.axis_index("gx") // 2, 2) == 1
    near = {0: (masked, move(masked, routes.core))}
    via_a, via_b = masked, masked
    for r in range(1, rounds + 1):
        via_a, via_b = move(via_b, routes.pair_a), move(via_a, routes.pair_b)
        core_via_a, core_via_b = move(via_a, routes.core), move(via_b, routes.core)
        near[r] = (via_a, core_via_a, via_b, core_via_b)
    blocks = []
    for p in range(-rounds, rounds + 1):
        if p == 0:
            blocks += list(near[0])
        else:
            a, core_a, b, core_b = near[abs(p)]
            flip = odd_pair if p > 0 else ~odd_pair
            blocks += [jnp.where(flip, b, a), jnp.where(flip, core_b, core_a)]
    filtered = pl.pallas_call(
        functools.partial(band, rounds, total),
        out_shape=shape((width, rows, lanes), f32),
        in_specs=[smem, smem] + [vmem] * len(blocks),
        out_specs=vmem,
        scratch_shapes=[pltpu.VMEM((len(blocks) * width, rows, lanes), f32)],
        compiler_params=params,
        name="band_filter",
    )(band_offsets, filter_taps, *blocks)
    return filtered, final


def solution(mesh):
    routes = Routes(mesh.shape["gx"], mesh.shape["gy"])
    return jax.shard_map(
        functools.partial(shards, routes),
        mesh=mesh,
        in_specs=(
            P(None, "gx", "gy", None),
            P(None, None, "gx", "gy", None),
            P("gx", "gy", None),
            P("gx", "gy", None),
            P(),
            P(),
        ),
        out_specs=(P("gx", "gy", None), P(None, "gx", "gy", None)),
        check_vma=False,
    )
```

time: 75.1 us -> 35.6 us (0.47)
  the two profiles are of different devices: /device:TPU:0 before, /device:TPU:11 now
where the time goes in v1:
time: 35.6 us; the launch traced here: 35.4 us
  waiting for transfers between devices  13.3 us (37%)
  starting transfers between devices  12.4 us (35%)
  Pallas kernels  6.2 us (17%)
  local copies, waits for them, and re-layouts  2.7 us (8%)
  between operations  0.73 us (2%)
    ppermute x13, waiting for transfers between devices, move(): return lax.ppermute(value, BOTH, pairs)  13.3 us
    ppermute x13, starting transfers between devices, move(): return lax.ppermute(value, BOTH, pairs)  12.4 us
    pallas_call x1, Pallas kernels, shards(): pl.pallas_call(functools.partial(steps, margin, routes.count_x, routes.co...  4.66 us
    unnamed x12, local copies, waits for them, and re-layouts  2.7 us
    pallas_call x1, Pallas kernels, shards(): pl.pallas_call(functools.partial(band, rounds, total), out_shape=shape((w...  1.4 us
  transfers between devices with their start and end apart: 13, of which 6 were waited for; matrix products, arithmetic and copies ran while one was open for 0% of the time, Pallas kernels for 0%

profile of v1, /device:TPU:11, one launch (start us, length us, event | category | flops | bytes accessed | tf_op | source)
XLA Modules:
  0.0 35.4 jit_solution(6918261203352087110)
XLA Ops:
  0.6 1.1 %copy-done = f32[6,8,32,128]{3,2,1,0:T(8,128)S(1)} copy-done((f32[6,8,32,128]{3,2,1,0:T(8,128)S(1)}, f32[6,8,32,128]{3,2,1,0:T(8,128)}, u32[]{:S(2)}) %copy-start) | copy-done | bytes 786456
  1.8 0.9 %copy-done.2 = f32[8,32,128]{2,1,0:T(8,128)S(1)} copy-done((f32[8,32,128]{2,1,0:T(8,128)S(1)}, f32[8,32,128]{2,1,0:T(8,128)}, u32[]{:S(2)}) %copy-start.2) | copy-done | bytes 131096
  2.7 0.1 pack_borders.1
  2.8 1.9 %collective-permute-start = (f32[26,32,128]{2,1,0:T(8,128)S(1)}, f32[26,32,128]{2,1,0:T(8,128)S(1)}, u32[]{:S(2)}, u32[]{:S(2)}) collective-permute-start(f32[26,32,128]{2,1,0:T(8,128)S(1)} %get-tuple-element.10), channel_id=1, source_target_pairs={{0,2},{1,3},{2,0},{3,1},{4,8},{5,9},{6,10},{7,11},{8,4},{9,5},{10,... | collective-permute-start | bytes 1277960 | tf_op jit(solution)/shard_map/ppermute | solution.py:274
  4.7 0.3 collective-permute-start.2
  5.0 2.2 %collective-permute-start.3 = (f32[7,4,8,128]{3,2,1,0:T(8,128)S(1)}, f32[7,4,8,128]{3,2,1,0:T(8,128)S(1)}, u32[]{:S(2)}, u32[]{:S(2)}) collective-permute-start(f32[7,4,8,128]{3,2,1,0:T(8,128)S(1)} %get-tuple-element.13), channel_id=1, source_target_pairs={{0,4},{1,2},{2,1},{3,7},{4,0},{5,6},{6,5},{7,3},{8,12},{9,10},{10,... | collective-permute-start | bytes 344072 | tf_op jit(solution)/shard_map/ppermute | solution.py:274
  7.2 0.7 %collective-permute-start.4 = (f32[7,2,8,128]{3,2,1,0:T(8,128)S(1)}, f32[7,2,8,128]{3,2,1,0:T(8,128)S(1)}, u32[]{:S(2)}, u32[]{:S(2)}) collective-permute-start(f32[7,2,8,128]{3,2,1,0:T(8,128)S(1)} %get-tuple-element.14), channel_id=1, source_target_pairs={{0,1},{1,0},{2,3},{3,2},{4,9},{5,8},{6,11},{7,10},{8,5},{9,4},{10,... | collective-permute-start | bytes 172040 | tf_op jit(solution)/shard_map/ppermute | solution.py:274
  7.9 1.0 %collective-permute-done.2.side_a = f32[7,4,8,128]{3,2,1,0:T(8,128)S(1)} collective-permute-done((f32[7,4,8,128]{3,2,1,0:T(8,128)S(1)}, f32[7,4,8,128]{3,2,1,0:T(8,128)S(1)}, u32[]{:S(2)}, u32[]{:S(2)}) %collective-permute-start.2) | collective-permute-done | bytes 114720 | tf_op jit(solution)/shard_map/ppermute | solution.py:274
  8.9 1.4 %collective-permute-start.6 = (f32[7,4,8,128]{3,2,1,0:T(8,128)S(1)}, f32[7,4,8,128]{3,2,1,0:T(8,128)S(1)}, u32[]{:S(2)}, u32[]{:S(2)}) collective-permute-start(f32[7,4,8,128]{3,2,1,0:T(8,128)S(1)} %collective-permute-done.2.side_a), channel_id=1, source_target_pairs={{0,4},{1,5},{2,6},{3,7},{4,0},{5,1},{6,2},{7,3},{8,12},{9,13},{10,... | collective-permute-start | bytes 344072 | tf_op jit(solution)/shard_map/ppermute | solution.py:274
  10.3 3.3 %collective-permute-done.3.side_b = f32[7,4,8,128]{3,2,1,0:T(8,128)S(1)} collective-permute-done((f32[7,4,8,128]{3,2,1,0:T(8,128)S(1)}, f32[7,4,8,128]{3,2,1,0:T(8,128)S(1)}, u32[]{:S(2)}, u32[]{:S(2)}) %collective-permute-start.3) | collective-permute-done | bytes 114720 | tf_op jit(solution)/shard_map/ppermute | solution.py:274
  13.6 1.4 %collective-permute-start.7 = (f32[7,4,8,128]{3,2,1,0:T(8,128)S(1)}, f32[7,4,8,128]{3,2,1,0:T(8,128)S(1)}, u32[]{:S(2)}, u32[]{:S(2)}) collective-permute-start(f32[7,4,8,128]{3,2,1,0:T(8,128)S(1)} %collective-permute-done.3.side_b), channel_id=1, source_target_pairs={{0,4},{1,5},{2,6},{3,7},{4,0},{5,1},{6,2},{7,3},{8,12},{9,13},{10,... | collective-permute-start | bytes 344072 | tf_op jit(solution)/shard_map/ppermute | solution.py:274
  15.0 1.1 %collective-permute-start.5 = (f32[7,2,8,128]{3,2,1,0:T(8,128)S(1)}, f32[7,2,8,128]{3,2,1,0:T(8,128)S(1)}, u32[]{:S(2)}, u32[]{:S(2)}) collective-permute-start(f32[7,2,8,128]{3,2,1,0:T(8,128)S(1)} %get-tuple-element.15), channel_id=1, source_target_pairs={{0,2},{1,3},{2,0},{3,1},{4,8},{5,10},{6,9},{7,11},{8,4},{9,6},{10,... | collective-permute-start | bytes 172040 | tf_op jit(solution)/shard_map/ppermute | solution.py:274
  16.1 4.3 %collective-permute-done.5.diag_b = f32[7,2,8,128]{3,2,1,0:T(8,128)S(1)} collective-permute-done((f32[7,2,8,128]{3,2,1,0:T(8,128)S(1)}, f32[7,2,8,128]{3,2,1,0:T(8,128)S(1)}, u32[]{:S(2)}, u32[]{:S(2)}) %collective-permute-start.5) | collective-permute-done | bytes 57376 | tf_op jit(solution)/shard_map/ppermute | solution.py:274
  20.4 4.7 %yee_steps.1 = (f32[8,32,128]{2,1,0:T(8,128)S(1)}, f32[3,8,32,128]{3,2,1,0:T(8,128)}) custom-call(f32[6,8,32,128]{3,2,1,0:T(8,128)S(1)} %copy-done, f32[8,32,128]{2,1,0:T(8,128)S(1)} %copy-done.2, bf16[4,3,8,32,128]{4,3,2,1,0:T(8,128)(2,1)S(1)} %copy-done.1, s32[8,32,128]{2,1,0:T(8,128)S(1)} %copy-done.3, f32[26,32,128]{2,1,0:T(8,128)S(1)} %collective-permute-done.out_x, ...), custom_call_target="tpu_custom_call" | custom-call | tf_op jit(solution)/shard_map/yee_steps/pallas_call | solution.py:284
  25.1 1.4 %collective-permute-start.8 = (f32[8,32,128]{2,1,0:T(8,128)S(1)}, f32[8,32,128]{2,1,0:T(8,128)S(1)}, u32[]{:S(2)}, u32[]{:S(2)}) collective-permute-start(f32[8,32,128]{2,1,0:T(8,128)S(1)} %get-tuple-element.16.refs_2_), channel_id=1, source_target_pairs={{0,4},{1,5},{2,6},{3,7},{4,0},{5,1},{6,2},{7,3},{8,16},{9,17},{10,... | collective-permute-start | bytes 393224 | tf_op jit(solution)/shard_map/ppermute | solution.py:274
  26.4 0.3 collective-permute-start.12
  26.7 3.5 %collective-permute-done.8 = f32[8,32,128]{2,1,0:T(8,128)S(1)} collective-permute-done((f32[8,32,128]{2,1,0:T(8,128)S(1)}, f32[8,32,128]{2,1,0:T(8,128)S(1)}, u32[]{:S(2)}, u32[]{:S(2)}) %collective-permute-start.8) | collective-permute-done | bytes 131104 | tf_op jit(solution)/shard_map/ppermute | solution.py:274
  30.3 0.8 %collective-permute-start.10 = (f32[8,32,128]{2,1,0:T(8,128)S(1)}, f32[8,32,128]{2,1,0:T(8,128)S(1)}, u32[]{:S(2)}, u32[]{:S(2)}) collective-permute-start(f32[8,32,128]{2,1,0:T(8,128)S(1)} %collective-permute-done.8), channel_id=1, source_target_pairs={{0,4},{1,5},{2,6},{3,7},{4,0},{5,1},{6,2},{7,3},{8,12},{9,13},{10,... | collective-permute-start | bytes 393224 | tf_op jit(solution)/shard_map/ppermute | solution.py:274
  31.0 0.2 collective-permute-done.9
  31.2 1.1 %collective-permute-start.11 = (f32[8,32,128]{2,1,0:T(8,128)S(1)}, f32[8,32,128]{2,1,0:T(8,128)S(1)}, u32[]{:S(2)}, u32[]{:S(2)}) collective-permute-start(f32[8,32,128]{2,1,0:T(8,128)S(1)} %collective-permute-done.9), channel_id=1, source_target_pairs={{0,4},{1,5},{2,6},{3,7},{4,0},{5,1},{6,2},{7,3},{8,12},{9,13},{10,... | collective-permute-start | bytes 393224 | tf_op jit(solution)/shard_map/ppermute | solution.py:274
  32.4 1.0 %collective-permute-done.11 = f32[8,32,128]{2,1,0:T(8,128)S(1)} collective-permute-done((f32[8,32,128]{2,1,0:T(8,128)S(1)}, f32[8,32,128]{2,1,0:T(8,128)S(1)}, u32[]{:S(2)}, u32[]{:S(2)}) %collective-permute-start.11) | collective-permute-done | bytes 131104 | tf_op jit(solution)/shard_map/ppermute | solution.py:274
  33.4 0.6 %copy-done.4 = s32[9]{0:T(128)S(1)} copy-done((s32[9]{0:T(128)S(1)}, s32[9]{0:T(128)}, u32[]{:S(2)}) %copy-start.4) | copy-done | bytes 60
  34.0 0.0 copy-done.5
  34.0 1.4 %band_filter.1 = f32[8,32,128]{2,1,0:T(8,128)} custom-call(s32[9]{0:T(128)S(1)} %copy-done.4, f32[9]{0:T(128)S(1)} %copy-done.5, f32[8,32,128]{2,1,0:T(8,128)S(1)} %get-tuple-element.21.refs_0_, f32[8,32,128]{2,1,0:T(8,128)S(1)} %get-tuple-element.19.refs_1_, f32[8,32,128]{2,1,0:T(8,128)S(1)} %get-tuple-element.16.refs_2_, ...), custom_call_target="tpu_custom_call" | custom-call | tf_op jit(solution)/shard_map/band_filter/pallas_call | solution.py:317
  (19 shorter events, 0.1 us)
Async XLA Ops:
  0.6 1.1 %copy-start = (f32[6,8,32,128]{3,2,1,0:T(8,128)S(1)}, f32[6,8,32,128]{3,2,1,0:T(8,128)}, u32[]{:S(2)}) copy-start(f32[6,8,32,128]{3,2,1,0:T(8,128)} %fields.3) | copy-start | bytes 2359300
  1.8 0.9 %copy-start.2 = (f32[8,32,128]{2,1,0:T(8,128)S(1)}, f32[8,32,128]{2,1,0:T(8,128)}, u32[]{:S(2)}) copy-start(f32[8,32,128]{2,1,0:T(8,128)} %perm.3) | copy-start | bytes 393220
  2.7 17.7 %copy-start.1 = (bf16[4,3,8,32,128]{4,3,2,1,0:T(8,128)(2,1)S(1)}, bf16[4,3,8,32,128]{4,3,2,1,0:T(8,128)(2,1)}, u32[]{:S(2)}) copy-start(bf16[4,3,8,32,128]{4,3,2,1,0:T(8,128)(2,1)} %forward.1) | copy-start | bytes 2359300
  2.7 17.7 %copy-start.3 = (s32[8,32,128]{2,1,0:T(8,128)S(1)}, s32[8,32,128]{2,1,0:T(8,128)}, u32[]{:S(2)}) copy-start(s32[8,32,128]{2,1,0:T(8,128)} %mask.1) | copy-start | bytes 393220
  2.8 17.5 %collective-permute-start = (f32[26,32,128]{2,1,0:T(8,128)S(1)}, f32[26,32,128]{2,1,0:T(8,128)S(1)}, u32[]{:S(2)}, u32[]{:S(2)}) collective-permute-start(f32[26,32,128]{2,1,0:T(8,128)S(1)} %get-tuple-element.10), channel_id=1, source_target_pairs={{0,2},{1,3},{2,0},{3,1},{4,8},{5,9},{6,10},{7,11},{8,4},{9,5},{10,... | collective-permute-start | bytes 1277960 | tf_op jit(solution)/shard_map/ppermute | solution.py:274
  4.7 15.6 %collective-permute-start.1 = (f32[26,32,128]{2,1,0:T(8,128)S(1)}, f32[26,32,128]{2,1,0:T(8,128)S(1)}, u32[]{:S(2)}, u32[]{:S(2)}) collective-permute-start(f32[26,32,128]{2,1,0:T(8,128)S(1)} %get-tuple-element.11), channel_id=1, source_target_pairs={{0,4},{1,5},{2,6},{3,7},{4,0},{5,1},{6,2},{7,3},{8,12},{9,13},{10,... | collective-permute-start | bytes 1277960 | tf_op jit(solution)/shard_map/ppermute | solution.py:274
  4.7 4.2 %collective-permute-start.2 = (f32[7,4,8,128]{3,2,1,0:T(8,128)S(1)}, f32[7,4,8,128]{3,2,1,0:T(8,128)S(1)}, u32[]{:S(2)}, u32[]{:S(2)}) collective-permute-start(f32[7,4,8,128]{3,2,1,0:T(8,128)S(1)} %get-tuple-element.12), channel_id=1, source_target_pairs={{0,1},{1,0},{2,3},{3,2},{4,5},{5,4},{6,7},{7,6},{8,9},{9,8},{10,11... | collective-permute-start | bytes 344072 | tf_op jit(solution)/shard_map/ppermute | solution.py:274
  5.0 8.6 %collective-permute-start.3 = (f32[7,4,8,128]{3,2,1,0:T(8,128)S(1)}, f32[7,4,8,128]{3,2,1,0:T(8,128)S(1)}, u32[]{:S(2)}, u32[]{:S(2)}) collective-permute-start(f32[7,4,8,128]{3,2,1,0:T(8,128)S(1)} %get-tuple-element.13), channel_id=1, source_target_pairs={{0,4},{1,2},{2,1},{3,7},{4,0},{5,6},{6,5},{7,3},{8,12},{9,10},{10,... | collective-permute-start | bytes 344072 | tf_op jit(solution)/shard_map/ppermute | solution.py:274
  7.2 7.8 %collective-permute-start.4 = (f32[7,2,8,128]{3,2,1,0:T(8,128)S(1)}, f32[7,2,8,128]{3,2,1,0:T(8,128)S(1)}, u32[]{:S(2)}, u32[]{:S(2)}) collective-permute-start(f32[7,2,8,128]{3,2,1,0:T(8,128)S(1)} %get-tuple-element.14), channel_id=1, source_target_pairs={{0,1},{1,0},{2,3},{3,2},{4,9},{5,8},{6,11},{7,10},{8,5},{9,4},{10,... | collective-permute-start | bytes 172040 | tf_op jit(solution)/shard_map/ppermute | solution.py:274
  8.9 11.4 %collective-permute-start.6 = (f32[7,4,8,128]{3,2,1,0:T(8,128)S(1)}, f32[7,4,8,128]{3,2,1,0:T(8,128)S(1)}, u32[]{:S(2)}, u32[]{:S(2)}) collective-permute-start(f32[7,4,8,128]{3,2,1,0:T(8,128)S(1)} %collective-permute-done.2.side_a), channel_id=1, source_target_pairs={{0,4},{1,5},{2,6},{3,7},{4,0},{5,1},{6,2},{7,3},{8,12},{9,13},{10,... | collective-permute-start | bytes 344072 | tf_op jit(solution)/shard_map/ppermute | solution.py:274
  13.6 6.8 %collective-permute-start.7 = (f32[7,4,8,128]{3,2,1,0:T(8,128)S(1)}, f32[7,4,8,128]{3,2,1,0:T(8,128)S(1)}, u32[]{:S(2)}, u32[]{:S(2)}) collective-permute-start(f32[7,4,8,128]{3,2,1,0:T(8,128)S(1)} %collective-permute-done.3.side_b), channel_id=1, source_target_pairs={{0,4},{1,5},{2,6},{3,7},{4,0},{5,1},{6,2},{7,3},{8,12},{9,13},{10,... | collective-permute-start | bytes 344072 | tf_op jit(solution)/shard_map/ppermute | solution.py:274
  15.0 5.4 %collective-permute-start.5 = (f32[7,2,8,128]{3,2,1,0:T(8,128)S(1)}, f32[7,2,8,128]{3,2,1,0:T(8,128)S(1)}, u32[]{:S(2)}, u32[]{:S(2)}) collective-permute-start(f32[7,2,8,128]{3,2,1,0:T(8,128)S(1)} %get-tuple-element.15), channel_id=1, source_target_pairs={{0,2},{1,3},{2,0},{3,1},{4,8},{5,10},{6,9},{7,11},{8,4},{9,6},{10,... | collective-permute-start | bytes 172040 | tf_op jit(solution)/shard_map/ppermute | solution.py:274
  25.1 5.2 %collective-permute-start.8 = (f32[8,32,128]{2,1,0:T(8,128)S(1)}, f32[8,32,128]{2,1,0:T(8,128)S(1)}, u32[]{:S(2)}, u32[]{:S(2)}) collective-permute-start(f32[8,32,128]{2,1,0:T(8,128)S(1)} %get-tuple-element.16.refs_2_), channel_id=1, source_target_pairs={{0,4},{1,5},{2,6},{3,7},{4,0},{5,1},{6,2},{7,3},{8,16},{9,17},{10,... | collective-permute-start | bytes 393224 | tf_op jit(solution)/shard_map/ppermute | solution.py:274
  26.4 4.8 %collective-permute-start.9 = (f32[8,32,128]{2,1,0:T(8,128)S(1)}, f32[8,32,128]{2,1,0:T(8,128)S(1)}, u32[]{:S(2)}, u32[]{:S(2)}) collective-permute-start(f32[8,32,128]{2,1,0:T(8,128)S(1)} %get-tuple-element.16.refs_2_), channel_id=1, source_target_pairs={{0,8},{1,9},{2,10},{3,11},{4,12},{5,13},{6,14},{7,15},{8,0},{9,1},... | collective-permute-start | bytes 393224 | tf_op jit(solution)/shard_map/ppermute | solution.py:274
  26.4 6.9 %collective-permute-start.12 = (f32[8,32,128]{2,1,0:T(8,128)S(1)}, f32[8,32,128]{2,1,0:T(8,128)S(1)}, u32[]{:S(2)}, u32[]{:S(2)}) collective-permute-start(f32[8,32,128]{2,1,0:T(8,128)S(1)} %get-tuple-element.16.refs_2_), channel_id=1, source_target_pairs={{0,4},{1,5},{2,6},{3,7},{4,0},{5,1},{6,2},{7,3},{8,12},{9,13},{10,... | collective-permute-start | bytes 393224 | tf_op jit(solution)/shard_map/ppermute | solution.py:274
  30.3 2.1 %collective-permute-start.10 = (f32[8,32,128]{2,1,0:T(8,128)S(1)}, f32[8,32,128]{2,1,0:T(8,128)S(1)}, u32[]{:S(2)}, u32[]{:S(2)}) collective-permute-start(f32[8,32,128]{2,1,0:T(8,128)S(1)} %collective-permute-done.8), channel_id=1, source_target_pairs={{0,4},{1,5},{2,6},{3,7},{4,0},{5,1},{6,2},{7,3},{8,12},{9,13},{10,... | collective-permute-start | bytes 393224 | tf_op jit(solution)/shard_map/ppermute | solution.py:274
  31.2 2.1 %collective-permute-start.11 = (f32[8,32,128]{2,1,0:T(8,128)S(1)}, f32[8,32,128]{2,1,0:T(8,128)S(1)}, u32[]{:S(2)}, u32[]{:S(2)}) collective-permute-start(f32[8,32,128]{2,1,0:T(8,128)S(1)} %collective-permute-done.9), channel_id=1, source_target_pairs={{0,4},{1,5},{2,6},{3,7},{4,0},{5,1},{6,2},{7,3},{8,12},{9,13},{10,... | collective-permute-start | bytes 393224 | tf_op jit(solution)/shard_map/ppermute | solution.py:274
  33.4 0.7 %copy-start.4 = (s32[9]{0:T(128)S(1)}, s32[9]{0:T(128)}, u32[]{:S(2)}) copy-start(s32[9]{0:T(128)} %offsets.1) | copy-start | bytes 112
  33.4 0.7 %copy-start.5 = (f32[9]{0:T(128)S(1)}, f32[9]{0:T(128)}, u32[]{:S(2)}) copy-start(f32[9]{0:T(128)} %taps.1) | copy-start | bytes 112

commit v2 on v1

v2 whole, which is shorter than its diff:
```python
import functools
import jax
import jax.numpy as jnp
from jax import lax
from jax.experimental import pallas as pl
from jax.experimental.pallas import tpu as pltpu
from jax.sharding import PartitionSpec as P

ITERS = 4
COURANT = 0.5
BOTH = ("gx", "gy")
SUB = 8


def swaps(count_x, count_y, partner, idle):
    pairs = []
    for x in range(count_x):
        for y in range(count_y):
            to = partner(x, y)
            if to is None:
                to = idle(x, y)
            pairs.append((x * count_y + y, to[0] * count_y + to[1]))
    assert sorted(b for _, b in pairs) == sorted(a for a, _ in pairs)
    return pairs


class Routes:
    def __init__(self, count_x, count_y):
        self.count_x, self.count_y = count_x, count_y
        half = max(count_y // 2, 1)

        def outward_x(x):
            to = x + 1 if x % 2 else x - 1
            return to if 0 <= to < count_x else None

        def side_b(y):
            to = y + 1 if y % 2 else y - 1
            return to if 0 <= to < count_y else None

        def far_y(x, y):
            return (x, (y + half) % count_y)

        def out_partner(x, y):
            return None if outward_x(x) is None else (outward_x(x), y)

        def b_partner(x, y):
            return None if side_b(y) is None else (x, side_b(y))

        def pair_b(x, y):
            to = (x // 2 + (1 if (x // 2) % 2 else -1)) * 2 + x % 2
            return (to, y) if 0 <= to < count_x else None

        make = functools.partial(swaps, count_x, count_y)
        core = lambda x, y: (x ^ 1, y)
        self.core = make(core, None)
        self.out_x = make(out_partner, far_y)
        self.side_a = make(lambda x, y: (x, y ^ 1), None)
        self.side_b = make(b_partner, core)
        self.pair_a = make(lambda x, y: (x ^ 2, y), None)
        self.pair_b = make(pair_b, core)


def depths(margin):
    return (margin, margin, margin, margin - 1, margin, margin, margin - 1)


def edge_tile(low, first, second, upper):
    up = upper == 1
    first = jnp.where(up, pltpu.roll(first, SUB // 2, 0), first)
    second = jnp.where(up, second, pltpu.roll(second, SUB // 2, 0))
    return jnp.where(low, first, second)


def tail_tile(low, odd, from_a, from_b, upper):
    after = jnp.where(odd == 0, from_a, from_b)
    before = jnp.where(odd == 0, from_b, from_a)
    if upper:
        after = pltpu.roll(after, SUB // 2, 0)
    else:
        before = pltpu.roll(before, SUB // 2, 0)
    return jnp.where(low, after, before)


def low_half(lanes):
    return lax.broadcasted_iota(jnp.int32, (SUB, lanes), 0) < SUB // 2


def position():
    at_x, at_y = lax.axis_index("gx"), lax.axis_index("gy")
    return at_x, at_y, lax.rem(at_x, 2), lax.rem(at_y, 2)


def pack(margin, fields, perm, ext, out_x, in_x, side_a, side_b, sems):
    width, rows, lanes = perm.shape
    _, _, core, odd = position()
    low = low_half(lanes)
    own = (pl.ds(margin, width), pl.ds(0, rows))
    loads = [pltpu.make_async_copy(fields.at[k], ext.at[(k, *own)], sems.at[k]) for k in range(6)]
    loads.append(pltpu.make_async_copy(perm, ext.at[(6, *own)], sems.at[6]))
    for load in loads:
        load.start()
    at = 0
    for k, depth in enumerate(depths(margin)):
        loads[k].wait()
        for j in range(depth):
            out_x[at + j] = ext[k, margin + core * (width - depth) + j, 0:rows]
            in_x[at + j] = ext[k, margin + (1 - core) * (width - depth) + j, 0:rows]
        at += depth

        def edge(x, x2, upper):
            where = pl.ds(pl.multiple_of(upper * (rows - SUB), SUB), SUB)
            return edge_tile(low, ext[k, margin + x, where], ext[k, margin + x2, where], upper)

        for j in range(width // 2):
            side_a[k, j] = edge(j, j + width // 2, 1 - odd)
            side_b[k, j] = edge(j, j + width // 2, odd)


def tails(margin, count_y, ext_in, side_a, side_b, ext, inner, outer):
    del ext_in
    width, rows, lanes = ext.shape[1] - 2 * margin, ext.shape[2] - SUB, ext.shape[3]
    _, at_y, core, odd = position()
    low = low_half(lanes)
    valid = jnp.where(low, jnp.where(at_y < count_y - 1, 1, 0), jnp.where(at_y > 0, 1, 0)) > 0
    for k in range(7):
        for x in range(width):
            j, upper = x % (width // 2), x // (width // 2)
            tile = tail_tile(low, odd, side_a[k, j], side_b[k, j], upper)
            ext[k, margin + x, rows:] = jnp.where(valid, tile, 1.0 if k == 6 else 0.0)
        for j in range(margin):
            inner[k, j] = ext[k, margin + (1 - core) * (width - margin) + j, rows:]
            outer[k, j] = ext[k, margin + core * (width - margin) + j, rows:]


def steps(margin, reach, count_x, count_y, ext_in, forward, mask, out_x, in_x, inner, outer, offsets, taps,
          ext, masked, final, weights, table, table_sems):
    del ext_in
    width, rows, lanes = mask.shape
    high = rows + SUB
    at_x, at_y, core, odd = position()
    load_offsets = pltpu.make_async_copy(offsets, table[0], table_sems.at[0])
    load_taps = pltpu.make_async_copy(taps, table[1], table_sems.at[1])
    load_offsets.start()
    load_taps.start()

    scale = COURANT * COURANT
    low = low_half(lanes)
    has_out = jnp.where(core == 0, at_x > 0, at_x < count_x - 1)
    has_after, has_before = at_y < count_y - 1, at_y > 0
    valid_y = jnp.where(low, jnp.where(has_after, 1, 0), jnp.where(has_before, 1, 0)) > 0
    valid_corner = valid_y & jnp.broadcast_to(has_out, (SUB, lanes))
    out_at = core * (width + margin)
    in_at = (1 - core) * (width + margin)

    def put(k, x, where, value, valid):
        if k == 6:
            value = scale / value
        ext[k, x, where] = value if valid is None else jnp.where(valid, value, 0.0)

    body, tail = pl.ds(0, rows), pl.ds(rows, SUB)
    for x in range(margin, margin + width):
        put(6, x, body, ext[6, x, 0:rows], None)
        put(6, x, tail, ext[6, x, rows:], valid_y)
    at = 0
    for k, depth in enumerate(depths(margin)):
        for j in range(depth):
            put(k, out_at + (1 - core) * (margin - depth) + j, body, out_x[at + j], has_out)
            put(k, in_at + core * (margin - depth) + j, body, in_x[at + j], None)
        at += depth
    for k in range(7):
        for j in range(margin):
            put(k, out_at + j, tail, outer[k, j], valid_corner if k == 6 else has_out)
            put(k, in_at + j, tail, inner[k, j], valid_y if k == 6 else None)

    lane = lax.broadcasted_iota(jnp.int32, (high, lanes), 1)
    first_lane = lane == 0
    before_rows = jnp.where(low | jnp.broadcast_to(has_before, (SUB, lanes)), 1.0, 0.0)
    before_x = jnp.where(at_x > 0, 1.0, 0.0)

    gap = lax.broadcasted_iota(jnp.int32, (lanes, lanes), 0) - lax.broadcasted_iota(jnp.int32, (lanes, lanes), 1)
    ahead = jnp.where(gap == 1, 1.0, 0.0) - jnp.where(gap == 0, 1.0, 0.0)
    ahead = jnp.concatenate([ahead, ahead], 0).astype(jnp.bfloat16)

    def ahead_z(k, first, end):
        f = ext[k, first:end].reshape((end - first) * high, lanes)
        main = f.astype(jnp.bfloat16)
        rest = (f - main.astype(jnp.float32)).astype(jnp.bfloat16)
        return jnp.dot(jnp.concatenate([main, rest], 1), ahead, preferred_element_type=jnp.float32)

    def next_y(f):
        return pltpu.roll(f, high - 1, 0)

    def last_y(f):
        return pltpu.roll(f, 1, 0)

    def last_z(f):
        return jnp.where(first_lane, 0.0, pltpu.roll(f, 1, 1))

    for turn in range(margin):
        last = turn == margin - 1
        first, end = turn, width + 2 * margin - 1 - turn
        ahead_x, ahead_y = ahead_z(0, first, end), ahead_z(1, first, end)
        held_y = held_z = None
        for i in range(first, end):
            ex, ey, ez = ext[0, i], ext[1, i], ext[2, i]
            ey_x, ez_x = ext[1, i + 1], ext[2, i + 1]
            hx, hy, hz = ext[3, i], ext[4, i], ext[5, i]
            if turn == 0:
                hx, hy, hz = hx * (1 / COURANT), hy * (1 / COURANT), hz * (1 / COURANT)
            here = slice((i - first) * high, (i - first + 1) * high)
            hx = hx - ((next_y(ez) - ez) - ahead_y[here])
            hy = hy - (ahead_x[here] - (ez_x - ez))
            hz = hz - ((ey_x - ey) - (next_y(ex) - ex))

            def clear(h):
                h = jnp.concatenate([h[:rows], h[rows:] * before_rows], 0)
                return h * before_x if i < margin else h

            hx, hy, hz = clear(hx), clear(hy), clear(hz)
            if not last:
                ext[3, i], ext[4, i], ext[5, i] = hx, hy, hz
            if i > first:
                c = ext[6, i]
                ex = ex + c * ((hz - last_y(hz)) - (hy - last_z(hy)))
                ey = ey + c * ((hx - last_z(hx)) - (hz - held_z))
                ez = ez + c * ((hy - held_y) - (hx - last_y(hx)))
                if not last:
                    ext[0, i], ext[1, i], ext[2, i] = ex, ey, ez
                if margin <= i < margin + width:
                    x = i - margin
                    own_e = (ex[:rows], ey[:rows], ez[:rows])
                    total = sum(forward[turn, a, x].astype(jnp.float32) * own_e[a] for a in range(3))
                    if turn > 0:
                        total = total + masked[x]
                    if last:
                        total = total * mask[x].astype(jnp.float32)
                        for a in range(3):
                            final[a, x] = own_e[a]
                    masked[x] = total
            held_y, held_z = hy, hz

    load_offsets.wait()
    load_taps.wait()
    distance = lax.broadcasted_iota(jnp.int32, weights.shape, 0) - reach
    total = jnp.zeros(weights.shape, jnp.float32)
    for b in range(offsets.shape[0]):
        total = total + jnp.where(distance == table[0][b], table[1][b], 0.0)
    weights[...] = total


def band(rounds, reach, count_x, weights, own, other, *refs):
    *near, out = refs
    width, rows, lanes = out.shape
    at_x, _, core, _ = position()
    pair = at_x // 2
    even = lax.rem(pair, 2) == 0

    def value(k, x, where):
        def of_pair(p, same):
            if p == 0:
                return (own if same else other)[x, where]
            a, b, core_a, core_b = near[4 * (abs(p) - 1) : 4 * abs(p)]
            first, second = (a, b) if same else (core_a, core_b)
            found = jnp.where(even == (p > 0), first[x, where], second[x, where])
            return jnp.where((pair + p >= 0) & (pair + p < count_x // 2), found, 0.0)

        if k % 2 == 0:
            return of_pair(k // 2, True)
        return jnp.where(core == 0, of_pair((k - 1) // 2, False), of_pair((k + 1) // 2, False))

    for r in range(rows // SUB):
        where = slice(r * SUB, (r + 1) * SUB)
        line = {}
        sums = [None] * width
        for d in range(-reach, reach + 1):
            weight = jnp.broadcast_to(weights[d + reach : d + reach + 1], (SUB, lanes))
            for x in range(width):
                at = x + d
                if at not in line:
                    line[at] = value(at // width, at % width, where)
                term = weight * line[at]
                sums[x] = term if sums[x] is None else sums[x] + term
        for x in range(width):
            out[x, where] = sums[x]


def shards(routes, adjoint_fields, forward_e, permittivity, design_mask, band_offsets, filter_taps):
    width, rows, lanes = permittivity.shape
    margin = ITERS
    f32 = jnp.float32
    planes = sum(depths(margin))
    shape = jax.ShapeDtypeStruct
    vmem = pl.BlockSpec(memory_space=pltpu.VMEM)
    hbm = pl.BlockSpec(memory_space=pltpu.HBM)
    params = pltpu.CompilerParams(vmem_limit_bytes=24 * 1024 * 1024)
    block = shape((width, rows, lanes), f32)
    ext = shape((7, width + 2 * margin, rows + SUB, lanes), f32)
    strip = shape((planes, rows, lanes), f32)
    edge = shape((7, width // 2, SUB, lanes), f32)
    inner = shape((7, margin, SUB, lanes), f32)
    cells, out_x, in_x, side_a, side_b = pl.pallas_call(
        functools.partial(pack, margin),
        out_shape=(ext, strip, strip, edge, edge),
        in_specs=[hbm] * 2,
        out_specs=(vmem,) * 5,
        scratch_shapes=[pltpu.SemaphoreType.DMA((7,))],
        compiler_params=params,
        name="pack_borders",
    )(pltpu.with_memory_space_constraint(adjoint_fields, pltpu.HBM), pltpu.with_memory_space_constraint(permittivity, pltpu.HBM))

    def move(value, pairs):
        return lax.ppermute(value, BOTH, pairs)

    in_x = move(in_x, routes.core)
    side_b = move(side_b, routes.side_b)
    out_x = move(out_x, routes.out_x)
    side_a = move(side_a, routes.side_a)
    cells, inner, outer = pl.pallas_call(
        functools.partial(tails, margin, routes.count_y),
        out_shape=(ext, inner, inner),
        in_specs=[vmem] * 3,
        out_specs=(vmem,) * 3,
        input_output_aliases={0: 0},
        compiler_params=params,
        name="join_sides",
    )(cells, side_a, side_b)
    outer = move(outer, routes.out_x)
    inner = move(inner, routes.core)
    reach = width * routes.count_x // 4
    rounds = -(-reach // (2 * width))
    _, masked, final, weights = pl.pallas_call(
        functools.partial(steps, margin, reach, routes.count_x, routes.count_y),
        out_shape=(ext, block, shape((3, width, rows, lanes), f32), shape((-(-(2 * reach + 1) // SUB) * SUB, lanes), f32)),
        in_specs=[vmem] * 7 + [hbm] * 2,
        out_specs=(vmem,) * 4,
        input_output_aliases={0: 0},
        scratch_shapes=[
            (pltpu.SMEM(band_offsets.shape, band_offsets.dtype), pltpu.SMEM(filter_taps.shape, filter_taps.dtype)),
            pltpu.SemaphoreType.DMA((2,)),
        ],
        compiler_params=params,
        name="yee_steps",
    )(cells, forward_e, design_mask, out_x, in_x, inner, outer, band_offsets, filter_taps)

    other = move(masked, routes.core)
    via_a, via_b = masked, masked
    near = []
    for _ in range(rounds):
        via_a, via_b = move(via_b, routes.pair_a), move(via_a, routes.pair_b)
        near += [via_a, via_b, move(via_a, routes.core), move(via_b, routes.core)]
    filtered = pl.pallas_call(
        functools.partial(band, rounds, reach, routes.count_x),
        out_shape=block,
        in_specs=[vmem] * (3 + len(near)),
        out_specs=vmem,
        compiler_params=params,
        name="band_filter",
    )(weights, masked, other, *near)
    return filtered, final


def solution(mesh):
    routes = Routes(mesh.shape["gx"], mesh.shape["gy"])
    return jax.shard_map(
        functools.partial(shards, routes),
        mesh=mesh,
        in_specs=(
            P(None, "gx", "gy", None),
            P(None, None, "gx", "gy", None),
            P("gx", "gy", None),
            P("gx", "gy", None),
            P(),
            P(),
        ),
        out_specs=(P("gx", "gy", None), P(None, "gx", "gy", None)),
        check_vma=False,
    )
```

time: 35.6 us -> 30 us (0.84)
  local copies, waits for them, and re-layouts: 2.7 us -> 0.02 us
  starting transfers between devices: 12.4 us -> 10.8 us
  waiting for transfers between devices: 13.3 us -> 12.7 us
  Pallas kernels: 6.2 us -> 5.69 us
    unnamed x12 -> x8, local copies, waits for them, and re-layouts: 2.7 us -> 0.02 us
    ppermute x13 -> x11, starting transfers between devices: 12.4 us -> 10.8 us  [move(): return lax.ppermute(value, BOTH, pairs)]
    ppermute x13 -> x11, waiting for transfers between devices: 13.3 us -> 12.7 us  [move(): return lax.ppermute(value, BOTH, pairs)]
    pallas_call x3 -> x4, Pallas kernels: 6.2 us -> 5.69 us  [the longest x1 3.21 us: shards(): pl.pallas_call(functools.partial(steps, margin, reach, routes.count_x, ro...]
  transfers between devices with their start and end apart: 13 -> 11, of which waited for: 6 -> 6; matrix products, arithmetic and copies ran while one was open for 0% -> 0% of each run, Pallas kernels for 0% -> 0%
where the time goes in v2:
time: 30 us; the launch traced here: 29.9 us
  waiting for transfers between devices  12.7 us (42%)
  starting transfers between devices  10.8 us (36%)
  Pallas kernels  5.69 us (19%)
  between operations  0.72 us (2%)
    ppermute x11, waiting for transfers between devices, move(): return lax.ppermute(value, BOTH, pairs)  12.7 us
    ppermute x11, starting transfers between devices, move(): return lax.ppermute(value, BOTH, pairs)  10.8 us
    pallas_call x1, Pallas kernels, shards(): pl.pallas_call(functools.partial(steps, margin, reach, routes.count_x, ro...  3.21 us
    pallas_call x1, Pallas kernels, shards(): pl.pallas_call(functools.partial(pack, margin), out_shape=(ext, strip, st...  1.39 us
    pallas_call x1, Pallas kernels, shards(): pl.pallas_call(functools.partial(band, rounds, reach, routes.count_x), ou...  1.01 us
  transfers between devices with their start and end apart: 11, of which 6 were waited for; matrix products, arithmetic and copies ran while one was open for 0% of the time, Pallas kernels for 0%

profile of v2, /device:TPU:11, one launch (start us, length us, event | category | flops | bytes accessed | tf_op | source)
XLA Modules:
  0.0 29.9 jit_solution(14431606178799315174)
XLA Ops:
  0.7 1.4 %pack_borders.1 = (f32[7,16,40,128]{3,2,1,0:T(8,128)S(1)}, f32[26,32,128]{2,1,0:T(8,128)S(1)}, f32[26,32,128]{2,1,0:T(8,128)S(1)}, f32[7,4,8,128]{3,2,1,0:T(8,128)S(1)}, f32[7,4,8,128]{3,2,1,0:T(8,128)S(1)}) custom-call(f32[6,8,32,128]{3,2,1,0:T(8,128)} %fields.1, f32[8,32,128]{2,1,0:T(8,128)} %perm.1), custom_call_target="tpu_custom_call" | custom-call | tf_op jit(solution)/shard_map/pack_borders/pallas_call | solution.py:301
  2.1 1.9 %collective-permute-start.2 = (f32[26,32,128]{2,1,0:T(8,128)S(1)}, f32[26,32,128]{2,1,0:T(8,128)S(1)}, u32[]{:S(2)}, u32[]{:S(2)}) collective-permute-start(f32[26,32,128]{2,1,0:T(8,128)S(1)} %get-tuple-element.17), channel_id=1, source_target_pairs={{0,2},{1,3},{2,0},{3,1},{4,8},{5,9},{6,10},{7,11},{8,4},{9,5},{10,... | collective-permute-start | bytes 1277960 | tf_op jit(solution)/shard_map/ppermute | solution.py:312
  4.0 0.0 collective-permute-start.3
  4.0 0.3 collective-permute-start
  4.3 2.2 %collective-permute-start.1 = (f32[7,4,8,128]{3,2,1,0:T(8,128)S(1)}, f32[7,4,8,128]{3,2,1,0:T(8,128)S(1)}, u32[]{:S(2)}, u32[]{:S(2)}) collective-permute-start(f32[7,4,8,128]{3,2,1,0:T(8,128)S(1)} %get-tuple-element.15), channel_id=1, source_target_pairs={{0,4},{1,2},{2,1},{3,7},{4,0},{5,6},{6,5},{7,3},{8,12},{9,10},{10,... | collective-permute-start | bytes 344072 | tf_op jit(solution)/shard_map/ppermute | solution.py:312
  6.4 1.8 %collective-permute-done.side_a = f32[7,4,8,128]{3,2,1,0:T(8,128)S(1)} collective-permute-done((f32[7,4,8,128]{3,2,1,0:T(8,128)S(1)}, f32[7,4,8,128]{3,2,1,0:T(8,128)S(1)}, u32[]{:S(2)}, u32[]{:S(2)}) %collective-permute-start) | collective-permute-done | bytes 114720 | tf_op jit(solution)/shard_map/ppermute | solution.py:312
  8.2 3.4 %collective-permute-done.1.side_b = f32[7,4,8,128]{3,2,1,0:T(8,128)S(1)} collective-permute-done((f32[7,4,8,128]{3,2,1,0:T(8,128)S(1)}, f32[7,4,8,128]{3,2,1,0:T(8,128)S(1)}, u32[]{:S(2)}, u32[]{:S(2)}) %collective-permute-start.1) | collective-permute-done | bytes 114720 | tf_op jit(solution)/shard_map/ppermute | solution.py:312
  11.6 0.1 join_sides.1
  11.7 1.4 %collective-permute-start.4 = (f32[7,4,8,128]{3,2,1,0:T(8,128)S(1)}, f32[7,4,8,128]{3,2,1,0:T(8,128)S(1)}, u32[]{:S(2)}, u32[]{:S(2)}) collective-permute-start(f32[7,4,8,128]{3,2,1,0:T(8,128)S(1)} %get-tuple-element.19), channel_id=1, source_target_pairs={{0,4},{1,5},{2,6},{3,7},{4,0},{5,1},{6,2},{7,3},{8,12},{9,13},{10,... | collective-permute-start | bytes 344072 | tf_op jit(solution)/shard_map/ppermute | solution.py:312
  13.1 1.3 %collective-permute-start.5 = (f32[7,4,8,128]{3,2,1,0:T(8,128)S(1)}, f32[7,4,8,128]{3,2,1,0:T(8,128)S(1)}, u32[]{:S(2)}, u32[]{:S(2)}) collective-permute-start(f32[7,4,8,128]{3,2,1,0:T(8,128)S(1)} %get-tuple-element.20), channel_id=1, source_target_pairs={{0,2},{1,3},{2,0},{3,1},{4,8},{5,9},{6,10},{7,11},{8,4},{9,5},{10,... | collective-permute-start | bytes 344072 | tf_op jit(solution)/shard_map/ppermute | solution.py:312
  14.4 0.0 collective-permute-done.4.inner
  14.4 3.0 %collective-permute-done.5.outer = f32[7,4,8,128]{3,2,1,0:T(8,128)S(1)} collective-permute-done((f32[7,4,8,128]{3,2,1,0:T(8,128)S(1)}, f32[7,4,8,128]{3,2,1,0:T(8,128)S(1)}, u32[]{:S(2)}, u32[]{:S(2)}) %collective-permute-start.5) | collective-permute-done | bytes 114720 | tf_op jit(solution)/shard_map/ppermute | solution.py:312
  17.4 3.2 %yee_steps.1 = (f32[7,16,40,128]{3,2,1,0:T(8,128)S(1)}, f32[8,32,128]{2,1,0:T(8,128)S(1)}, f32[3,8,32,128]{3,2,1,0:T(8,128)}, f32[40,128]{1,0:T(8,128)S(1)}) custom-call(f32[7,16,40,128]{3,2,1,0:T(8,128)S(1)} %get-tuple-element.16.ext_in, bf16[4,3,8,32,128]{4,3,2,1,0:T(8,128)(2,1)S(1)} %copy-done, ...), custom_call_target="tpu_custom_call", output_to_operand_aliasing={{0}: (0, {})} | custom-call | tf_op jit(solution)/shard_map/yee_steps/pallas_call | solution.py:331
  20.6 1.4 %collective-permute-start.8 = (f32[8,32,128]{2,1,0:T(8,128)S(1)}, f32[8,32,128]{2,1,0:T(8,128)S(1)}, u32[]{:S(2)}, u32[]{:S(2)}) collective-permute-start(f32[8,32,128]{2,1,0:T(8,128)S(1)} %get-tuple-element.22.own), channel_id=1, source_target_pairs={{0,4},{1,5},{2,6},{3,7},{4,0},{5,1},{6,2},{7,3},{8,16},{9,17},{10,... | collective-permute-start | bytes 393224 | tf_op jit(solution)/shard_map/ppermute | solution.py:312
  22.0 0.0 collective-permute-start.7
  22.0 0.3 %collective-permute-start.6 = (f32[8,32,128]{2,1,0:T(8,128)S(1)}, f32[8,32,128]{2,1,0:T(8,128)S(1)}, u32[]{:S(2)}, u32[]{:S(2)}) collective-permute-start(f32[8,32,128]{2,1,0:T(8,128)S(1)} %get-tuple-element.22.own), channel_id=1, source_target_pairs={{0,4},{1,5},{2,6},{3,7},{4,0},{5,1},{6,2},{7,3},{8,12},{9,13},{10,... | collective-permute-start | bytes 393224 | tf_op jit(solution)/shard_map/ppermute | solution.py:312
  22.3 3.4 %collective-permute-done.8.refs_1_ = f32[8,32,128]{2,1,0:T(8,128)S(1)} collective-permute-done((f32[8,32,128]{2,1,0:T(8,128)S(1)}, f32[8,32,128]{2,1,0:T(8,128)S(1)}, u32[]{:S(2)}, u32[]{:S(2)}) %collective-permute-start.8) | collective-permute-done | bytes 131104 | tf_op jit(solution)/shard_map/ppermute | solution.py:312
  25.7 0.8 %collective-permute-start.10 = (f32[8,32,128]{2,1,0:T(8,128)S(1)}, f32[8,32,128]{2,1,0:T(8,128)S(1)}, u32[]{:S(2)}, u32[]{:S(2)}) collective-permute-start(f32[8,32,128]{2,1,0:T(8,128)S(1)} %collective-permute-done.8.refs_1_), channel_id=1, source_target_pairs={{0,4},{1,5},{2,6},{3,7},{4,0},{5,1},{6,2},{7,3},{8,12},{9,13},{10,... | collective-permute-start | bytes 393224 | tf_op jit(solution)/shard_map/ppermute | solution.py:312
  26.6 0.1 collective-permute-done.7.refs_0_
  26.7 1.2 %collective-permute-start.9 = (f32[8,32,128]{2,1,0:T(8,128)S(1)}, f32[8,32,128]{2,1,0:T(8,128)S(1)}, u32[]{:S(2)}, u32[]{:S(2)}) collective-permute-start(f32[8,32,128]{2,1,0:T(8,128)S(1)} %collective-permute-done.7.refs_0_), channel_id=1, source_target_pairs={{0,4},{1,5},{2,6},{3,7},{4,0},{5,1},{6,2},{7,3},{8,12},{9,13},{10,... | collective-permute-start | bytes 393224 | tf_op jit(solution)/shard_map/ppermute | solution.py:312
  27.9 0.0 collective-permute-done.6.other
  27.9 0.0 collective-permute-done.10.refs_3_
  27.9 1.0 %collective-permute-done.9.refs_2_ = f32[8,32,128]{2,1,0:T(8,128)S(1)} collective-permute-done((f32[8,32,128]{2,1,0:T(8,128)S(1)}, f32[8,32,128]{2,1,0:T(8,128)S(1)}, u32[]{:S(2)}, u32[]{:S(2)}) %collective-permute-start.9) | collective-permute-done | bytes 131104 | tf_op jit(solution)/shard_map/ppermute | solution.py:312
  28.9 1.0 %band_filter.1 = f32[8,32,128]{2,1,0:T(8,128)} custom-call(f32[40,128]{1,0:T(8,128)S(1)} %get-tuple-element.21.weights, f32[8,32,128]{2,1,0:T(8,128)S(1)} %get-tuple-element.22.own, f32[8,32,128]{2,1,0:T(8,128)S(1)} %collective-permute-done.6.other, f32[8,32,128]{2,1,0:T(8,128)S(1)} %collective-permute-done.7.refs_0_, ...), custom_call_target="tpu_custom_call" | custom-call | tf_op jit(solution)/shard_map/band_filter/pallas_call | solution.py:351
  (10 shorter events, 0.0 us)
Async XLA Ops:
  0.6 16.7 %copy-start.3 = (f32[9]{0:T(128)S(1)}, f32[9]{0:T(128)}, u32[]{:S(2)}) copy-start(f32[9]{0:T(128)} %taps.1) | copy-start | bytes 112
  0.6 16.7 %copy-start.2 = (s32[9]{0:T(128)S(1)}, s32[9]{0:T(128)}, u32[]{:S(2)}) copy-start(s32[9]{0:T(128)} %offsets.1) | copy-start | bytes 112
  0.7 16.7 %copy-start.1 = (s32[8,32,128]{2,1,0:T(8,128)S(1)}, s32[8,32,128]{2,1,0:T(8,128)}, u32[]{:S(2)}) copy-start(s32[8,32,128]{2,1,0:T(8,128)} %mask.1) | copy-start | bytes 393220
  0.7 16.7 %copy-start = (bf16[4,3,8,32,128]{4,3,2,1,0:T(8,128)(2,1)S(1)}, bf16[4,3,8,32,128]{4,3,2,1,0:T(8,128)(2,1)}, u32[]{:S(2)}) copy-start(bf16[4,3,8,32,128]{4,3,2,1,0:T(8,128)(2,1)} %forward.1) | copy-start | bytes 2359300
  2.1 15.3 %collective-permute-start.2 = (f32[26,32,128]{2,1,0:T(8,128)S(1)}, f32[26,32,128]{2,1,0:T(8,128)S(1)}, u32[]{:S(2)}, u32[]{:S(2)}) collective-permute-start(f32[26,32,128]{2,1,0:T(8,128)S(1)} %get-tuple-element.17), channel_id=1, source_target_pairs={{0,2},{1,3},{2,0},{3,1},{4,8},{5,9},{6,10},{7,11},{8,4},{9,5},{10,... | collective-permute-start | bytes 1277960 | tf_op jit(solution)/shard_map/ppermute | solution.py:312
  4.0 13.3 %collective-permute-start.3 = (f32[26,32,128]{2,1,0:T(8,128)S(1)}, f32[26,32,128]{2,1,0:T(8,128)S(1)}, u32[]{:S(2)}, u32[]{:S(2)}) collective-permute-start(f32[26,32,128]{2,1,0:T(8,128)S(1)} %get-tuple-element.18), channel_id=1, source_target_pairs={{0,4},{1,5},{2,6},{3,7},{4,0},{5,1},{6,2},{7,3},{8,12},{9,13},{10,... | collective-permute-start | bytes 1277960 | tf_op jit(solution)/shard_map/ppermute | solution.py:312
  4.0 4.2 %collective-permute-start = (f32[7,4,8,128]{3,2,1,0:T(8,128)S(1)}, f32[7,4,8,128]{3,2,1,0:T(8,128)S(1)}, u32[]{:S(2)}, u32[]{:S(2)}) collective-permute-start(f32[7,4,8,128]{3,2,1,0:T(8,128)S(1)} %get-tuple-element.14), channel_id=1, source_target_pairs={{0,1},{1,0},{2,3},{3,2},{4,5},{5,4},{6,7},{7,6},{8,9},{9,8},{10,11... | collective-permute-start | bytes 344072 | tf_op jit(solution)/shard_map/ppermute | solution.py:312
  4.3 7.4 %collective-permute-start.1 = (f32[7,4,8,128]{3,2,1,0:T(8,128)S(1)}, f32[7,4,8,128]{3,2,1,0:T(8,128)S(1)}, u32[]{:S(2)}, u32[]{:S(2)}) collective-permute-start(f32[7,4,8,128]{3,2,1,0:T(8,128)S(1)} %get-tuple-element.15), channel_id=1, source_target_pairs={{0,4},{1,2},{2,1},{3,7},{4,0},{5,6},{6,5},{7,3},{8,12},{9,10},{10,... | collective-permute-start | bytes 344072 | tf_op jit(solution)/shard_map/ppermute | solution.py:312
  11.7 2.7 %collective-permute-start.4 = (f32[7,4,8,128]{3,2,1,0:T(8,128)S(1)}, f32[7,4,8,128]{3,2,1,0:T(8,128)S(1)}, u32[]{:S(2)}, u32[]{:S(2)}) collective-permute-start(f32[7,4,8,128]{3,2,1,0:T(8,128)S(1)} %get-tuple-element.19), channel_id=1, source_target_pairs={{0,4},{1,5},{2,6},{3,7},{4,0},{5,1},{6,2},{7,3},{8,12},{9,13},{10,... | collective-permute-start | bytes 344072 | tf_op jit(solution)/shard_map/ppermute | solution.py:312
  13.1 4.2 %collective-permute-start.5 = (f32[7,4,8,128]{3,2,1,0:T(8,128)S(1)}, f32[7,4,8,128]{3,2,1,0:T(8,128)S(1)}, u32[]{:S(2)}, u32[]{:S(2)}) collective-permute-start(f32[7,4,8,128]{3,2,1,0:T(8,128)S(1)} %get-tuple-element.20), channel_id=1, source_target_pairs={{0,2},{1,3},{2,0},{3,1},{4,8},{5,9},{6,10},{7,11},{8,4},{9,5},{10,... | collective-permute-start | bytes 344072 | tf_op jit(solution)/shard_map/ppermute | solution.py:312
  20.6 5.1 %collective-permute-start.8 = (f32[8,32,128]{2,1,0:T(8,128)S(1)}, f32[8,32,128]{2,1,0:T(8,128)S(1)}, u32[]{:S(2)}, u32[]{:S(2)}) collective-permute-start(f32[8,32,128]{2,1,0:T(8,128)S(1)} %get-tuple-element.22.own), channel_id=1, source_target_pairs={{0,4},{1,5},{2,6},{3,7},{4,0},{5,1},{6,2},{7,3},{8,16},{9,17},{10,... | collective-permute-start | bytes 393224 | tf_op jit(solution)/shard_map/ppermute | solution.py:312
  22.0 4.7 %collective-permute-start.7 = (f32[8,32,128]{2,1,0:T(8,128)S(1)}, f32[8,32,128]{2,1,0:T(8,128)S(1)}, u32[]{:S(2)}, u32[]{:S(2)}) collective-permute-start(f32[8,32,128]{2,1,0:T(8,128)S(1)} %get-tuple-element.22.own), channel_id=1, source_target_pairs={{0,8},{1,9},{2,10},{3,11},{4,12},{5,13},{6,14},{7,15},{8,0},{9,1},... | collective-permute-start | bytes 393224 | tf_op jit(solution)/shard_map/ppermute | solution.py:312
  22.0 5.9 %collective-permute-start.6 = (f32[8,32,128]{2,1,0:T(8,128)S(1)}, f32[8,32,128]{2,1,0:T(8,128)S(1)}, u32[]{:S(2)}, u32[]{:S(2)}) collective-permute-start(f32[8,32,128]{2,1,0:T(8,128)S(1)} %get-tuple-element.22.own), channel_id=1, source_target_pairs={{0,4},{1,5},{2,6},{3,7},{4,0},{5,1},{6,2},{7,3},{8,12},{9,13},{10,... | collective-permute-start | bytes 393224 | tf_op jit(solution)/shard_map/ppermute | solution.py:312
  25.7 2.2 %collective-permute-start.10 = (f32[8,32,128]{2,1,0:T(8,128)S(1)}, f32[8,32,128]{2,1,0:T(8,128)S(1)}, u32[]{:S(2)}, u32[]{:S(2)}) collective-permute-start(f32[8,32,128]{2,1,0:T(8,128)S(1)} %collective-permute-done.8.refs_1_), channel_id=1, source_target_pairs={{0,4},{1,5},{2,6},{3,7},{4,0},{5,1},{6,2},{7,3},{8,12},{9,13},{10,... | collective-permute-start | bytes 393224 | tf_op jit(solution)/shard_map/ppermute | solution.py:312
  26.7 2.2 %collective-permute-start.9 = (f32[8,32,128]{2,1,0:T(8,128)S(1)}, f32[8,32,128]{2,1,0:T(8,128)S(1)}, u32[]{:S(2)}, u32[]{:S(2)}) collective-permute-start(f32[8,32,128]{2,1,0:T(8,128)S(1)} %collective-permute-done.7.refs_0_), channel_id=1, source_target_pairs={{0,4},{1,5},{2,6},{3,7},{4,0},{5,1},{6,2},{7,3},{8,12},{9,13},{10,... | collective-permute-start | bytes 393224 | tf_op jit(solution)/shard_map/ppermute | solution.py:312

commit v3 on v2

v3 whole, which is shorter than its diff:
```python
import functools
import jax
import jax.numpy as jnp
from jax import lax
from jax.experimental import pallas as pl
from jax.experimental.pallas import tpu as pltpu
from jax.sharding import PartitionSpec as P

ITERS = 4
COURANT = 0.5
BOTH = ("gx", "gy")
SUB = 8
JOIN_Y_US = 50
JOIN_X_US = 0.05
BAND_OWN_US = 2


def swaps(count_x, count_y, partner, idle):
    pairs = []
    for x in range(count_x):
        for y in range(count_y):
            to = partner(x, y)
            if to is None:
                to = idle(x, y)
            pairs.append((x * count_y + y, to[0] * count_y + to[1]))
    assert sorted(b for _, b in pairs) == sorted(a for a, _ in pairs)
    return pairs


class Routes:
    def __init__(self, count_x, count_y):
        self.count_x, self.count_y = count_x, count_y
        half = max(count_y // 2, 1)

        def outward_x(x):
            to = x + 1 if x % 2 else x - 1
            return to if 0 <= to < count_x else None

        def side_b(y):
            to = y + 1 if y % 2 else y - 1
            return to if 0 <= to < count_y else None

        def far_y(x, y):
            return (x, (y + half) % count_y)

        def out_partner(x, y):
            return None if outward_x(x) is None else (outward_x(x), y)

        def b_partner(x, y):
            return None if side_b(y) is None else (x, side_b(y))

        def ring(x, y, up):
            to = x + 2 if x % 2 == up else x - 2
            return (to, y) if 0 <= to < count_x else (x ^ 1, y)

        make = functools.partial(swaps, count_x, count_y)
        core = lambda x, y: (x ^ 1, y)
        self.core = make(core, None)
        self.out_x = make(out_partner, far_y)
        self.side_a = make(lambda x, y: (x, y ^ 1), None)
        self.side_b = make(b_partner, core)
        self.ring_1 = make(lambda x, y: ring(x, y, 1), None)
        self.ring_0 = make(lambda x, y: ring(x, y, 0), None)


def depths(margin):
    return (margin, margin, margin, margin - 1, margin, margin, margin - 1)


def edge_tile(low, first, second, upper):
    up = upper == 1
    first = jnp.where(up, pltpu.roll(first, SUB // 2, 0), first)
    second = jnp.where(up, second, pltpu.roll(second, SUB // 2, 0))
    return jnp.where(low, first, second)


def tail_tile(low, odd, from_a, from_b, upper):
    after = jnp.where(odd == 0, from_a, from_b)
    before = jnp.where(odd == 0, from_b, from_a)
    if upper:
        after = pltpu.roll(after, SUB // 2, 0)
    else:
        before = pltpu.roll(before, SUB // 2, 0)
    return jnp.where(low, after, before)


def low_half(lanes):
    return lax.broadcasted_iota(jnp.int32, (SUB, lanes), 0) < SUB // 2


def position():
    at_x, at_y = lax.axis_index("gx"), lax.axis_index("gy")
    return at_x, at_y, lax.rem(at_x, 2), lax.rem(at_y, 2)


def pack_y(margin, fields, perm, ext, side_a, side_b, sems):
    width, rows, lanes = perm.shape
    _, _, _, odd = position()
    low = low_half(lanes)
    own = (pl.ds(margin, width), pl.ds(0, rows))
    loads = [pltpu.make_async_copy(fields.at[k] if k < 6 else perm, ext.at[(k, *own)], sems.at[k]) for k in range(7)]
    for load in loads:
        load.start()
    for k in range(7):
        loads[k].wait()

        def edge(x, upper):
            where = pl.ds(pl.multiple_of(upper * (rows - SUB), SUB), SUB)
            return edge_tile(low, ext[k, margin + x, where], ext[k, margin + x + width // 2, where], upper)

        for j in range(width // 2):
            side_a[k, j] = edge(j, 1 - odd)
            side_b[k, j] = edge(j, odd)


def pack_x(margin, ext, out_x, in_x):
    width, rows = ext.shape[1] - 2 * margin, ext.shape[2] - SUB
    _, _, core, _ = position()
    at = 0
    for k, depth in enumerate(depths(margin)):
        for j in range(depth):
            out_x[at + j] = ext[k, margin + core * (width - depth) + j, 0:rows]
            in_x[at + j] = ext[k, margin + (1 - core) * (width - depth) + j, 0:rows]
        at += depth


def valid_rows(low, at_y, count_y):
    return jnp.where(low, jnp.where(at_y < count_y - 1, 1, 0), jnp.where(at_y > 0, 1, 0)) > 0


def has_outward(at_x, core, count_x):
    return jnp.where(core == 0, at_x > 0, at_x < count_x - 1)


def join_y(margin, count_y, ext_in, side_a, side_b, ext, outer):
    del ext_in
    width, rows, lanes = ext.shape[1] - 2 * margin, ext.shape[2] - SUB, ext.shape[3]
    _, at_y, core, odd = position()
    low = low_half(lanes)
    valid = valid_rows(low, at_y, count_y)
    for k in range(7):
        for x in range(width):
            j, upper = x % (width // 2), x // (width // 2)
            tile = tail_tile(low, odd, side_a[k, j], side_b[k, j], upper)
            ext[k, margin + x, rows:] = jnp.where(valid, tile, 1.0 if k == 6 else 0.0)
        for j in range(margin):
            outer[k, j] = ext[k, margin + core * (width - margin) + j, rows:]


def join_inner(margin, count_y, ext_in, ext, inner):
    del ext_in
    width, rows, lanes = ext.shape[1] - 2 * margin, ext.shape[2] - SUB, ext.shape[3]
    _, at_y, core, _ = position()
    valid = valid_rows(low_half(lanes), at_y, count_y)
    for k in range(7):
        for j in range(margin):
            inner[k, j] = ext[k, margin + (1 - core) * (width - margin) + j, rows:]
    scale = COURANT * COURANT
    for x in range(margin, margin + width):
        ext[6, x, 0:rows] = scale / ext[6, x, 0:rows]
        ext[6, x, rows:] = jnp.where(valid, scale / ext[6, x, rows:], 0.0)


def load_rest(ext_in, forward, mask, offsets, taps, ext, forward_out, mask_out, weights, table, sems):
    del ext_in, ext
    lists = [pltpu.make_async_copy(offsets, table[0], sems.at[0]), pltpu.make_async_copy(taps, table[1], sems.at[1])]
    loads = [pltpu.make_async_copy(forward, forward_out, sems.at[2]), pltpu.make_async_copy(mask, mask_out, sems.at[3])]
    for load in lists + loads:
        load.start()
    for load in lists:
        load.wait()
    distance = lax.broadcasted_iota(jnp.int32, weights.shape, 0) - weights.shape[0] // 2
    total = jnp.zeros(weights.shape, jnp.float32)
    for b in range(offsets.shape[0]):
        total = total + jnp.where(distance == table[0][b], table[1][b], 0.0)
    weights[...] = total
    for load in loads:
        load.wait()


def join_core(margin, ext_in, in_x, ext):
    del ext_in
    width, rows = ext.shape[1] - 2 * margin, ext.shape[2] - SUB
    _, _, core, _ = position()
    in_at = (1 - core) * (width + margin)
    at = 0
    for k, depth in enumerate(depths(margin)):
        for j in range(depth):
            plane = in_x[at + j]
            plane = COURANT * COURANT / plane if k == 6 else plane
            ext[k, in_at + core * (margin - depth) + j, 0:rows] = plane
        at += depth


def join_outer(margin, count_x, ext_in, out_x, ext):
    del ext_in
    width, rows = ext.shape[1] - 2 * margin, ext.shape[2] - SUB
    at_x, _, core, _ = position()
    has_out = has_outward(at_x, core, count_x)
    out_at = core * (width + margin)
    at = 0
    for k, depth in enumerate(depths(margin)):
        for j in range(depth):
            plane = out_x[at + j]
            plane = COURANT * COURANT / plane if k == 6 else plane
            ext[k, out_at + (1 - core) * (margin - depth) + j, 0:rows] = jnp.where(has_out, plane, 0.0)
        at += depth


def join_corner(margin, count_x, count_y, ext_in, outer, ext):
    del ext_in
    width, rows, lanes = ext.shape[1] - 2 * margin, ext.shape[2] - SUB, ext.shape[3]
    at_x, at_y, core, _ = position()
    has_out = has_outward(at_x, core, count_x)
    valid = valid_rows(low_half(lanes), at_y, count_y) & jnp.broadcast_to(has_out, (SUB, lanes))
    out_at = core * (width + margin)
    for k in range(7):
        for j in range(margin):
            tile = outer[k, j]
            tile = jnp.where(valid, COURANT * COURANT / tile, 0.0) if k == 6 else jnp.where(has_out, tile, 0.0)
            ext[k, out_at + j, rows:] = tile


def steps(margin, count_x, count_y, ext_in, forward, mask, inner, ext, masked, final):
    del ext_in
    width, rows, lanes = mask.shape
    high = rows + SUB
    at_x, at_y, core, _ = position()
    low = low_half(lanes)
    has_before = at_y > 0
    valid = valid_rows(low, at_y, count_y)
    in_at = (1 - core) * (width + margin)
    for k in range(7):
        for j in range(margin):
            tile = inner[k, j]
            ext[k, in_at + j, rows:] = jnp.where(valid, COURANT * COURANT / tile, 0.0) if k == 6 else tile

    lane = lax.broadcasted_iota(jnp.int32, (high, lanes), 1)
    first_lane = lane == 0
    before_rows = jnp.where(low | jnp.broadcast_to(has_before, (SUB, lanes)), 1.0, 0.0)
    before_x = jnp.where(at_x > 0, 1.0, 0.0)

    gap = lax.broadcasted_iota(jnp.int32, (lanes, lanes), 0) - lax.broadcasted_iota(jnp.int32, (lanes, lanes), 1)
    ahead = jnp.where(gap == 1, 1.0, 0.0) - jnp.where(gap == 0, 1.0, 0.0)
    ahead = jnp.concatenate([ahead, ahead], 0).astype(jnp.bfloat16)

    def ahead_z(k, first, end):
        f = ext[k, first:end].reshape((end - first) * high, lanes)
        main = f.astype(jnp.bfloat16)
        rest = (f - main.astype(jnp.float32)).astype(jnp.bfloat16)
        return jnp.dot(jnp.concatenate([main, rest], 1), ahead, preferred_element_type=jnp.float32)

    def next_y(f):
        return pltpu.roll(f, high - 1, 0)

    def last_y(f):
        return pltpu.roll(f, 1, 0)

    def last_z(f):
        return jnp.where(first_lane, 0.0, pltpu.roll(f, 1, 1))

    for turn in range(margin):
        last = turn == margin - 1
        first, end = turn, width + 2 * margin - 1 - turn
        ahead_x, ahead_y = ahead_z(0, first, end), ahead_z(1, first, end)
        held_y = held_z = None
        for i in range(first, end):
            ex, ey, ez = ext[0, i], ext[1, i], ext[2, i]
            ey_x, ez_x = ext[1, i + 1], ext[2, i + 1]
            hx, hy, hz = ext[3, i], ext[4, i], ext[5, i]
            if turn == 0:
                hx, hy, hz = hx * (1 / COURANT), hy * (1 / COURANT), hz * (1 / COURANT)
            here = slice((i - first) * high, (i - first + 1) * high)
            hx = hx - ((next_y(ez) - ez) - ahead_y[here])
            hy = hy - (ahead_x[here] - (ez_x - ez))
            hz = hz - ((ey_x - ey) - (next_y(ex) - ex))

            def clear(h):
                h = jnp.concatenate([h[:rows], h[rows:] * before_rows], 0)
                return h * before_x if i < margin else h

            hx, hy, hz = clear(hx), clear(hy), clear(hz)
            if not last:
                ext[3, i], ext[4, i], ext[5, i] = hx, hy, hz
            if i > first:
                c = ext[6, i]
                ex = ex + c * ((hz - last_y(hz)) - (hy - last_z(hy)))
                ey = ey + c * ((hx - last_z(hx)) - (hz - held_z))
                ez = ez + c * ((hy - held_y) - (hx - last_y(hx)))
                if not last:
                    ext[0, i], ext[1, i], ext[2, i] = ex, ey, ez
                if margin <= i < margin + width:
                    x = i - margin
                    own_e = (ex[:rows], ey[:rows], ez[:rows])
                    total = sum(forward[turn, a, x].astype(jnp.float32) * own_e[a] for a in range(3))
                    if turn > 0:
                        total = total + masked[x]
                    if last:
                        total = total * mask[x].astype(jnp.float32)
                        for a in range(3):
                            final[a, x] = own_e[a]
                    masked[x] = total
            held_y, held_z = hy, hz


def band_sum(reach, hop, sign, alone, weights, own, other, where, sums):
    width, _, lanes = own.shape
    _, _, core, _ = position()
    middle = weights.shape[0] // 2
    for j in range(width):
        for same in (True,) if alone else (True, False):
            plane = (own if same else other)[j, where]
            for x in range(width):
                distances = [j - x - 2 * hop * s * width + (0 if same else t * width) for s in (1, -1) for t in (1, -1)]
                if min(abs(distance) for distance in distances) > reach:
                    continue
                distance = j - x - 2 * hop * width * sign + (0 if same else (1 - 2 * core) * width)
                weight = jnp.broadcast_to(weights[pl.ds(middle + distance, 1)], (SUB, lanes))
                sums[x] = sums[x] + weight * plane
    return sums


def arrived(count_x, via_1, via_0, x, where):
    at_x, _, core, _ = position()
    first, second = via_1[x, where], via_0[x, where]
    up = core == 1
    before = jnp.where(at_x >= 2, jnp.where(up, first, second), 0.0)
    after = jnp.where(at_x < count_x - 2, jnp.where(up, second, first), 0.0)
    return before, after


def band_hop(reach, hop, count_x, up, alone, weights, own, *refs):
    *refs, send = refs
    other, via = (own, refs) if alone else (refs[0], refs[1:])
    width, rows, lanes = own.shape
    _, _, core, _ = position()
    ahead = core == up
    for r in range(rows // SUB):
        where = slice(r * SUB, (r + 1) * SUB)
        if via:
            start = [jnp.where(ahead, *arrived(count_x, *via, x, where)) for x in range(width)]
        else:
            start = [jnp.zeros((SUB, lanes), jnp.float32)] * width
        sums = band_sum(reach, hop, jnp.where(ahead, 1, -1), alone, weights, own, other, where, start)
        for x in range(width):
            send[x, where] = sums[x]


def band_own(reach, weights, own, other, final, base, stored, sem):
    store = pltpu.make_async_copy(final, stored, sem)
    store.start()
    width, rows, lanes = own.shape
    for r in range(rows // SUB):
        where = slice(r * SUB, (r + 1) * SUB)
        sums = band_sum(reach, 0, 1, False, weights, own, other, where, [jnp.zeros((SUB, lanes), jnp.float32)] * width)
        for x in range(width):
            base[x, where] = sums[x]
    store.wait()


def band_end(count_x, base, via_1, via_0, out):
    for x in range(out.shape[0]):
        before, after = arrived(count_x, via_1, via_0, x, slice(None))
        out[x] = base[x] + before + after


def shards(routes, adjoint_fields, forward_e, permittivity, design_mask, band_offsets, filter_taps):
    width, rows, lanes = permittivity.shape
    margin = ITERS
    f32 = jnp.float32
    planes = sum(depths(margin))
    shape = jax.ShapeDtypeStruct
    vmem = pl.BlockSpec(memory_space=pltpu.VMEM)
    hbm = pl.BlockSpec(memory_space=pltpu.HBM)
    params = pltpu.CompilerParams(vmem_limit_bytes=24 * 1024 * 1024)
    block = shape((width, rows, lanes), f32)
    ext = shape((7, width + 2 * margin, rows + SUB, lanes), f32)
    strip = shape((planes, rows, lanes), f32)
    edge = shape((7, width // 2, SUB, lanes), f32)
    corner = shape((7, margin, SUB, lanes), f32)
    reach = width * routes.count_x // 4
    rounds = -(-reach // (2 * width))
    distances = shape((4 * (rounds + 1) * width, lanes), f32)

    def cost(microseconds):
        return pl.CostEstimate(flops=int(microseconds * 1e9), bytes_accessed=int(microseconds * 3.6e6), transcendentals=0)

    def move(value, pairs):
        return lax.ppermute(value, BOTH, pairs)

    def from_hbm(*values):
        return [pltpu.with_memory_space_constraint(value, pltpu.HBM) for value in values]

    cells, side_a, side_b = pl.pallas_call(
        functools.partial(pack_y, margin),
        out_shape=(ext, edge, edge),
        in_specs=[hbm] * 2,
        out_specs=(vmem,) * 3,
        scratch_shapes=[pltpu.SemaphoreType.DMA((7,))],
        compiler_params=params,
        name="pack_y",
    )(*from_hbm(adjoint_fields, permittivity))
    out_x, in_x = pl.pallas_call(
        functools.partial(pack_x, margin),
        out_shape=(strip, strip),
        in_specs=[vmem],
        out_specs=(vmem,) * 2,
        compiler_params=params,
        name="pack_x",
    )(cells)
    side_b = move(side_b, routes.side_b)
    side_a = move(side_a, routes.side_a)
    in_x = move(in_x, routes.core)
    out_x = move(out_x, routes.out_x)
    cells, forward_e, design_mask, weights = pl.pallas_call(
        load_rest,
        out_shape=(ext, pltpu.VMEM(forward_e.shape, forward_e.dtype), pltpu.VMEM(design_mask.shape, design_mask.dtype), distances),
        in_specs=[vmem] + [hbm] * 4,
        out_specs=(vmem,) * 4,
        input_output_aliases={0: 0},
        scratch_shapes=[
            (pltpu.SMEM(band_offsets.shape, band_offsets.dtype), pltpu.SMEM(filter_taps.shape, filter_taps.dtype)),
            pltpu.SemaphoreType.DMA((4,)),
        ],
        compiler_params=params,
        cost_estimate=cost(JOIN_X_US),
        name="load_rest",
    )(cells, *from_hbm(forward_e, design_mask, band_offsets, filter_taps))
    cells, outer = pl.pallas_call(
        functools.partial(join_y, margin, routes.count_y),
        out_shape=(ext, corner),
        in_specs=[vmem] * 3,
        out_specs=(vmem,) * 2,
        input_output_aliases={0: 0},
        compiler_params=params,
        cost_estimate=cost(JOIN_Y_US),
        name="join_y",
    )(cells, side_a, side_b)
    outer = move(outer, routes.out_x)
    cells, inner = pl.pallas_call(
        functools.partial(join_inner, margin, routes.count_y),
        out_shape=(ext, corner),
        in_specs=[vmem],
        out_specs=(vmem,) * 2,
        input_output_aliases={0: 0},
        compiler_params=params,
        cost_estimate=cost(JOIN_X_US),
        name="join_inner",
    )(cells)
    inner = move(inner, routes.core)
    cells = pl.pallas_call(
        functools.partial(join_outer, margin, routes.count_x),
        out_shape=ext,
        in_specs=[vmem] * 2,
        out_specs=vmem,
        input_output_aliases={0: 0},
        compiler_params=params,
        cost_estimate=cost(JOIN_X_US),
        name="join_outer",
    )(cells, out_x)
    cells = pl.pallas_call(
        functools.partial(join_core, margin),
        out_shape=ext,
        in_specs=[vmem] * 2,
        out_specs=vmem,
        input_output_aliases={0: 0},
        compiler_params=params,
        cost_estimate=cost(JOIN_X_US),
        name="join_core",
    )(cells, in_x)
    cells = pl.pallas_call(
        functools.partial(join_corner, margin, routes.count_x, routes.count_y),
        out_shape=ext,
        in_specs=[vmem] * 2,
        out_specs=vmem,
        input_output_aliases={0: 0},
        compiler_params=params,
        cost_estimate=cost(JOIN_X_US),
        name="join_corner",
    )(cells, outer)
    _, masked, final = pl.pallas_call(
        functools.partial(steps, margin, routes.count_x, routes.count_y),
        out_shape=(ext, block, pltpu.VMEM((3, width, rows, lanes), f32)),
        in_specs=[vmem] * 4,
        out_specs=(vmem,) * 3,
        input_output_aliases={0: 0},
        compiler_params=params,
        name="yee_steps",
    )(cells, forward_e, design_mask, inner)

    other = move(masked, routes.core)
    via = []

    def hop_kernel(hop, up, alone):
        operands = [weights, masked] + ([] if alone else [other]) + via
        return pl.pallas_call(
            functools.partial(band_hop, reach, hop, routes.count_x, up, alone),
            out_shape=block,
            in_specs=[vmem] * len(operands),
            out_specs=vmem,
            compiler_params=params,
            name="band_hop",
        )(*operands)

    for hop in range(rounds, 0, -1):
        send_1 = hop_kernel(hop, 1, hop == rounds)
        send_0 = hop_kernel(hop, 0, False)
        via = [move(send_1, routes.ring_1), move(send_0, routes.ring_0)]
    base, final = pl.pallas_call(
        functools.partial(band_own, reach),
        out_shape=(block, shape(final.shape, f32)),
        in_specs=[vmem] * 4,
        out_specs=(vmem, hbm),
        scratch_shapes=[pltpu.SemaphoreType.DMA],
        compiler_params=params,
        cost_estimate=cost(BAND_OWN_US),
        name="band_own",
    )(weights, masked, other, final)
    filtered = pl.pallas_call(
        functools.partial(band_end, routes.count_x),
        out_shape=block,
        in_specs=[vmem] * 3,
        out_specs=vmem,
        compiler_params=params,
        name="band_end",
    )(base, *via)
    return filtered, final


def solution(mesh):
    routes = Routes(mesh.shape["gx"], mesh.shape["gy"])
    return jax.shard_map(
        functools.partial(shards, routes),
        mesh=mesh,
        in_specs=(
            P(None, "gx", "gy", None),
            P(None, None, "gx", "gy", None),
            P("gx", "gy", None),
            P("gx", "gy", None),
            P(),
            P(),
        ),
        out_specs=(P("gx", "gy", None), P(None, "gx", "gy", None)),
        check_vma=False,
    )
```

time: 30 us -> 25.2 us (0.84)
  the two profiles are of different devices: /device:TPU:11 before, /device:TPU:3 now
where the time goes in v3:
time: 25.2 us; the launch traced here: 25 us
  starting transfers between devices  9.84 us (39%)
  waiting for transfers between devices  8.19 us (32%)
  Pallas kernels  6.25 us (25%)
  between operations  0.74 us (3%)
    ppermute x9, starting transfers between devices, move(): return lax.ppermute(value, BOTH, pairs)  9.84 us
    ppermute x9, waiting for transfers between devices, move(): return lax.ppermute(value, BOTH, pairs)  8.19 us
    pallas_call x1, Pallas kernels, shards(): pl.pallas_call(functools.partial(steps, margin, routes.count_x, routes.co...  1.79 us
    pallas_call x1, Pallas kernels, shards(): pl.pallas_call(functools.partial(pack_y, margin), out_shape=(ext, edge, e...  1.31 us
    pallas_call x1, Pallas kernels, shards(): pl.pallas_call(load_rest, out_shape=(ext, pltpu.VMEM(forward_e.shape, for...  1.18 us
    pallas_call x1, Pallas kernels, shards(): pl.pallas_call(functools.partial(band_own, reach), out_shape=(block, shap...  0.75 us
    pallas_call x1, Pallas kernels, shards(): pl.pallas_call(functools.partial(band_end, routes.count_x), out_shape=blo...  0.69 us
  transfers between devices with their start and end apart: 9, of which 5 were waited for; matrix products, arithmetic and copies ran while one was open for 0% of the time, Pallas kernels for 10%

profile of v3, /device:TPU:3, one launch (start us, length us, event | category | flops | bytes accessed | tf_op | source)
XLA Modules:
  0.0 25.0 jit_solution(18247561175525738887)
XLA Ops:
  0.6 1.3 %pack_y.1 = (f32[7,16,40,128]{3,2,1,0:T(8,128)S(1)}, f32[7,4,8,128]{3,2,1,0:T(8,128)S(1)}, f32[7,4,8,128]{3,2,1,0:T(8,128)S(1)}) custom-call(f32[6,8,32,128]{3,2,1,0:T(8,128)} %fields.1, f32[8,32,128]{2,1,0:T(8,128)} %perm.1), custom_call_target="tpu_custom_call" | custom-call | tf_op jit(solution)/shard_map/pack_y/pallas_call | solution.py:394
  1.9 0.1 collective-permute-start
  2.0 2.4 %collective-permute-start.1 = (f32[7,4,8,128]{3,2,1,0:T(8,128)S(1)}, f32[7,4,8,128]{3,2,1,0:T(8,128)S(1)}, u32[]{:S(2)}, u32[]{:S(2)}) collective-permute-start(f32[7,4,8,128]{3,2,1,0:T(8,128)S(1)} %get-tuple-element.23), channel_id=1, source_target_pairs={{0,4},{1,2},{2,1},{3,7},{4,0},{5,6},{6,5},{7,3},{8,12},{9,10},{10,... | collective-permute-start | bytes 344072 | tf_op jit(solution)/shard_map/ppermute | solution.py:389
  4.4 0.1 pack_x.1
  4.5 2.5 %collective-permute-start.2 = (f32[26,32,128]{2,1,0:T(8,128)S(1)}, f32[26,32,128]{2,1,0:T(8,128)S(1)}, u32[]{:S(2)}, u32[]{:S(2)}) collective-permute-start(f32[26,32,128]{2,1,0:T(8,128)S(1)} %get-tuple-element.26), channel_id=1, source_target_pairs={{0,2},{1,3},{2,0},{3,1},{4,8},{5,9},{6,10},{7,11},{8,4},{9,5},{10,... | collective-permute-start | bytes 1277960 | tf_op jit(solution)/shard_map/ppermute | solution.py:389
  7.0 1.2 %load_rest.1 = (f32[7,16,40,128]{3,2,1,0:T(8,128)S(1)}, bf16[4,3,8,32,128]{4,3,2,1,0:T(8,128)(2,1)S(1)}, s32[8,32,128]{2,1,0:T(8,128)S(1)}, f32[64,128]{1,0:T(8,128)S(1)}) custom-call(f32[7,16,40,128]{3,2,1,0:T(8,128)S(1)} %get-tuple-element.19.ext_in.ext, bf16[4,3,8,32,128]{4,3,2,1,0:T(8,128)(2,1)} %forward.1, ...), custom_call_target="tpu_custom_call", output_to_operand_aliasing={{0}: (0, {})} | custom-call | flops 50000000 | bytes 180000 | tf_op jit(solution)/shard_map/load_rest/pallas_call | solution.py:415
  8.2 0.0 collective-permute-done.side_a
  8.2 1.3 %collective-permute-done.1.side_b = f32[7,4,8,128]{3,2,1,0:T(8,128)S(1)} collective-permute-done((f32[7,4,8,128]{3,2,1,0:T(8,128)S(1)}, f32[7,4,8,128]{3,2,1,0:T(8,128)S(1)}, u32[]{:S(2)}, u32[]{:S(2)}) %collective-permute-start.1) | collective-permute-done | bytes 114720 | tf_op jit(solution)/shard_map/ppermute | solution.py:389
  9.4 0.1 join_y.1
  9.5 2.8 %collective-permute-start.4 = (f32[7,4,8,128]{3,2,1,0:T(8,128)S(1)}, f32[7,4,8,128]{3,2,1,0:T(8,128)S(1)}, u32[]{:S(2)}, u32[]{:S(2)}) collective-permute-start(f32[7,4,8,128]{3,2,1,0:T(8,128)S(1)} %get-tuple-element.28), channel_id=1, source_target_pairs={{0,2},{1,3},{2,0},{3,1},{4,8},{5,9},{6,10},{7,11},{8,4},{9,5},{10,... | collective-permute-start | bytes 344072 | tf_op jit(solution)/shard_map/ppermute | solution.py:389
  12.4 0.1 collective-permute-start.5
  12.4 0.7 %collective-permute-done.2.out_x = f32[26,32,128]{2,1,0:T(8,128)S(1)} collective-permute-done((f32[26,32,128]{2,1,0:T(8,128)S(1)}, f32[26,32,128]{2,1,0:T(8,128)S(1)}, u32[]{:S(2)}, u32[]{:S(2)}) %collective-permute-start.2) | collective-permute-done | bytes 426016 | tf_op jit(solution)/shard_map/ppermute | solution.py:389
  13.1 0.1 join_outer.1.ext_in
  13.2 1.9 %collective-permute-done.4.outer = f32[7,4,8,128]{3,2,1,0:T(8,128)S(1)} collective-permute-done((f32[7,4,8,128]{3,2,1,0:T(8,128)S(1)}, f32[7,4,8,128]{3,2,1,0:T(8,128)S(1)}, u32[]{:S(2)}, u32[]{:S(2)}) %collective-permute-start.4) | collective-permute-done | bytes 114720 | tf_op jit(solution)/shard_map/ppermute | solution.py:389
  15.1 1.8 %yee_steps.1 = (f32[7,16,40,128]{3,2,1,0:T(8,128)S(1)}, f32[8,32,128]{2,1,0:T(8,128)S(1)}, f32[3,8,32,128]{3,2,1,0:T(8,128)S(1)}) custom-call(f32[7,16,40,128]{3,2,1,0:T(8,128)S(1)} %join_corner.1.ext_in, bf16[4,3,8,32,128]{4,3,2,1,0:T(8,128)(2,1)S(1)} %get-tuple-element.29.forward, ...), custom_call_target="tpu_custom_call", output_to_operand_aliasing={{0}: (0, {})} | custom-call | tf_op jit(solution)/shard_map/yee_steps/pallas_call | solution.py:481
  16.9 1.6 %collective-permute-start.6 = (f32[8,32,128]{2,1,0:T(8,128)S(1)}, f32[8,32,128]{2,1,0:T(8,128)S(1)}, u32[]{:S(2)}, u32[]{:S(2)}) collective-permute-start(f32[8,32,128]{2,1,0:T(8,128)S(1)} %get-tuple-element.32.own), channel_id=1, source_target_pairs={{0,4},{1,5},{2,6},{3,7},{4,0},{5,1},{6,2},{7,3},{8,12},{9,13},{10,... | collective-permute-start | bytes 393224 | tf_op jit(solution)/shard_map/ppermute | solution.py:389
  18.5 0.1 band_hop.2
  18.6 0.0 collective-permute-start.7
  18.6 0.9 %collective-permute-done.6.other.refs_0_ = f32[8,32,128]{2,1,0:T(8,128)S(1)} collective-permute-done((f32[8,32,128]{2,1,0:T(8,128)S(1)}, f32[8,32,128]{2,1,0:T(8,128)S(1)}, u32[]{:S(2)}, u32[]{:S(2)}) %collective-permute-start.6) | collective-permute-done | bytes 131104 | tf_op jit(solution)/shard_map/ppermute | solution.py:389
  19.5 0.2 band_hop.3
  19.7 0.4 %collective-permute-start.8 = (f32[8,32,128]{2,1,0:T(8,128)S(1)}, f32[8,32,128]{2,1,0:T(8,128)S(1)}, u32[]{:S(2)}, u32[]{:S(2)}) collective-permute-start(f32[8,32,128]{2,1,0:T(8,128)S(1)} %band_hop.3), channel_id=1, source_target_pairs={{0,8},{1,9},{2,10},{3,11},{4,0},{5,1},{6,2},{7,3},{8,16},{9,17},{1... | collective-permute-start | bytes 393224 | tf_op jit(solution)/shard_map/ppermute | solution.py:389
  20.1 0.8 %band_own.1 = (f32[8,32,128]{2,1,0:T(8,128)S(1)}, f32[3,8,32,128]{3,2,1,0:T(8,128)}) custom-call(f32[64,128]{1,0:T(8,128)S(1)} %get-tuple-element.20.weights, f32[8,32,128]{2,1,0:T(8,128)S(1)} %get-tuple-element.32.own, f32[8,32,128]{2,1,0:T(8,128)S(1)} %collective-permute-done.6.other.refs_0_, f32[3,8,32,128]{3,2,1,0:T(8,128)S(1)} %get-tuple-element.33.final), custom_call_target="tpu_custom_call" | custom-call | flops 2000000000 | bytes 7200000 | tf_op jit(solution)/shard_map/band_own/pallas_call | solution.py:509
  20.8 3.5 %collective-permute-done.8.via_0 = f32[8,32,128]{2,1,0:T(8,128)S(1)} collective-permute-done((f32[8,32,128]{2,1,0:T(8,128)S(1)}, f32[8,32,128]{2,1,0:T(8,128)S(1)}, u32[]{:S(2)}, u32[]{:S(2)}) %collective-permute-start.8) | collective-permute-done | bytes 131104 | tf_op jit(solution)/shard_map/ppermute | solution.py:389
  24.3 0.7 %band_end.1 = f32[8,32,128]{2,1,0:T(8,128)} custom-call(f32[8,32,128]{2,1,0:T(8,128)S(1)} %get-tuple-element.34.base, f32[8,32,128]{2,1,0:T(8,128)S(1)} %collective-permute-done.7.via_1, f32[8,32,128]{2,1,0:T(8,128)S(1)} %collective-permute-done.8.via_0), custom_call_target="tpu_custom_call" | custom-call | tf_op jit(solution)/shard_map/band_end/pallas_call | solution.py:519
  (7 shorter events, 0.1 us)
Async XLA Ops:
  1.9 6.2 %collective-permute-start = (f32[7,4,8,128]{3,2,1,0:T(8,128)S(1)}, f32[7,4,8,128]{3,2,1,0:T(8,128)S(1)}, u32[]{:S(2)}, u32[]{:S(2)}) collective-permute-start(f32[7,4,8,128]{3,2,1,0:T(8,128)S(1)} %get-tuple-element.22), channel_id=1, source_target_pairs={{0,1},{1,0},{2,3},{3,2},{4,5},{5,4},{6,7},{7,6},{8,9},{9,8},{10,11... | collective-permute-start | bytes 344072 | tf_op jit(solution)/shard_map/ppermute | solution.py:389
  2.0 7.4 %collective-permute-start.1 = (f32[7,4,8,128]{3,2,1,0:T(8,128)S(1)}, f32[7,4,8,128]{3,2,1,0:T(8,128)S(1)}, u32[]{:S(2)}, u32[]{:S(2)}) collective-permute-start(f32[7,4,8,128]{3,2,1,0:T(8,128)S(1)} %get-tuple-element.23), channel_id=1, source_target_pairs={{0,4},{1,2},{2,1},{3,7},{4,0},{5,6},{6,5},{7,3},{8,12},{9,10},{10,... | collective-permute-start | bytes 344072 | tf_op jit(solution)/shard_map/ppermute | solution.py:389
  4.5 8.6 %collective-permute-start.2 = (f32[26,32,128]{2,1,0:T(8,128)S(1)}, f32[26,32,128]{2,1,0:T(8,128)S(1)}, u32[]{:S(2)}, u32[]{:S(2)}) collective-permute-start(f32[26,32,128]{2,1,0:T(8,128)S(1)} %get-tuple-element.26), channel_id=1, source_target_pairs={{0,2},{1,3},{2,0},{3,1},{4,8},{5,9},{6,10},{7,11},{8,4},{9,5},{10,... | collective-permute-start | bytes 1277960 | tf_op jit(solution)/shard_map/ppermute | solution.py:389
  7.0 6.2 %collective-permute-start.3 = (f32[26,32,128]{2,1,0:T(8,128)S(1)}, f32[26,32,128]{2,1,0:T(8,128)S(1)}, u32[]{:S(2)}, u32[]{:S(2)}) collective-permute-start(f32[26,32,128]{2,1,0:T(8,128)S(1)} %get-tuple-element.27), channel_id=1, source_target_pairs={{0,4},{1,5},{2,6},{3,7},{4,0},{5,1},{6,2},{7,3},{8,12},{9,13},{10,... | collective-permute-start | bytes 1277960 | tf_op jit(solution)/shard_map/ppermute | solution.py:389
  9.5 5.6 %collective-permute-start.4 = (f32[7,4,8,128]{3,2,1,0:T(8,128)S(1)}, f32[7,4,8,128]{3,2,1,0:T(8,128)S(1)}, u32[]{:S(2)}, u32[]{:S(2)}) collective-permute-start(f32[7,4,8,128]{3,2,1,0:T(8,128)S(1)} %get-tuple-element.28), channel_id=1, source_target_pairs={{0,2},{1,3},{2,0},{3,1},{4,8},{5,9},{6,10},{7,11},{8,4},{9,5},{10,... | collective-permute-start | bytes 344072 | tf_op jit(solution)/shard_map/ppermute | solution.py:389
  12.4 2.8 %collective-permute-start.5 = (f32[7,4,8,128]{3,2,1,0:T(8,128)S(1)}, f32[7,4,8,128]{3,2,1,0:T(8,128)S(1)}, u32[]{:S(2)}, u32[]{:S(2)}) collective-permute-start(f32[7,4,8,128]{3,2,1,0:T(8,128)S(1)} %get-tuple-element.31), channel_id=1, source_target_pairs={{0,4},{1,5},{2,6},{3,7},{4,0},{5,1},{6,2},{7,3},{8,12},{9,13},{10,... | collective-permute-start | bytes 344072 | tf_op jit(solution)/shard_map/ppermute | solution.py:389
  16.9 2.6 %collective-permute-start.6 = (f32[8,32,128]{2,1,0:T(8,128)S(1)}, f32[8,32,128]{2,1,0:T(8,128)S(1)}, u32[]{:S(2)}, u32[]{:S(2)}) collective-permute-start(f32[8,32,128]{2,1,0:T(8,128)S(1)} %get-tuple-element.32.own), channel_id=1, source_target_pairs={{0,4},{1,5},{2,6},{3,7},{4,0},{5,1},{6,2},{7,3},{8,12},{9,13},{10,... | collective-permute-start | bytes 393224 | tf_op jit(solution)/shard_map/ppermute | solution.py:389
  18.6 2.2 %collective-permute-start.7 = (f32[8,32,128]{2,1,0:T(8,128)S(1)}, f32[8,32,128]{2,1,0:T(8,128)S(1)}, u32[]{:S(2)}, u32[]{:S(2)}) collective-permute-start(f32[8,32,128]{2,1,0:T(8,128)S(1)} %band_hop.2), channel_id=1, source_target_pairs={{0,4},{1,5},{2,6},{3,7},{4,12},{5,13},{6,14},{7,15},{8,0},{9,1},{1... | collective-permute-start | bytes 393224 | tf_op jit(solution)/shard_map/ppermute | solution.py:389
  19.7 4.7 %collective-permute-start.8 = (f32[8,32,128]{2,1,0:T(8,128)S(1)}, f32[8,32,128]{2,1,0:T(8,128)S(1)}, u32[]{:S(2)}, u32[]{:S(2)}) collective-permute-start(f32[8,32,128]{2,1,0:T(8,128)S(1)} %band_hop.3), channel_id=1, source_target_pairs={{0,8},{1,9},{2,10},{3,11},{4,0},{5,1},{6,2},{7,3},{8,16},{9,17},{1... | collective-permute-start | bytes 393224 | tf_op jit(solution)/shard_map/ppermute | solution.py:389

commit v4 on v3

--- a/solution.py
+++ b/solution.py
@@ -30,7 +30,9 @@
 class Routes:
     def __init__(self, count_x, count_y):
         self.count_x, self.count_y = count_x, count_y
-        half = max(count_y // 2, 1)
+        round_y = [y ^ (y >> 1) for y in range(count_y)]
+        if sorted(round_y) != list(range(count_y)):
+            round_y = list(range(count_y))
 
         def outward_x(x):
             to = x + 1 if x % 2 else x - 1
@@ -40,8 +42,8 @@
             to = y + 1 if y % 2 else y - 1
             return to if 0 <= to < count_y else None
 
-        def far_y(x, y):
-            return (x, (y + half) % count_y)
+        def around(x, y):
+            return (x, round_y[(round_y.index(y) + 1) % count_y])
 
         def out_partner(x, y):
             return None if outward_x(x) is None else (outward_x(x), y)
@@ -56,7 +58,7 @@
         make = functools.partial(swaps, count_x, count_y)
         core = lambda x, y: (x ^ 1, y)
         self.core = make(core, None)
-        self.out_x = make(out_partner, far_y)
+        self.out_x = make(out_partner, around)
         self.side_a = make(lambda x, y: (x, y ^ 1), None)
         self.side_b = make(b_partner, core)
         self.ring_1 = make(lambda x, y: ring(x, y, 1), None)
@@ -221,23 +223,14 @@
             ext[k, out_at + j, rows:] = tile
 
 
-def steps(margin, count_x, count_y, ext_in, forward, mask, inner, ext, masked, final):
-    del ext_in
+def steps(margin, ranges, ext, forward, mask, masked, final):
     width, rows, lanes = mask.shape
     high = rows + SUB
-    at_x, at_y, core, _ = position()
+    at_x, at_y, _, _ = position()
     low = low_half(lanes)
-    has_before = at_y > 0
-    valid = valid_rows(low, at_y, count_y)
-    in_at = (1 - core) * (width + margin)
-    for k in range(7):
-        for j in range(margin):
-            tile = inner[k, j]
-            ext[k, in_at + j, rows:] = jnp.where(valid, COURANT * COURANT / tile, 0.0) if k == 6 else tile
-
     lane = lax.broadcasted_iota(jnp.int32, (high, lanes), 1)
     first_lane = lane == 0
-    before_rows = jnp.where(low | jnp.broadcast_to(has_before, (SUB, lanes)), 1.0, 0.0)
+    before_rows = jnp.where(low | jnp.broadcast_to(at_y > 0, (SUB, lanes)), 1.0, 0.0)
     before_x = jnp.where(at_x > 0, 1.0, 0.0)
 
     gap = lax.broadcasted_iota(jnp.int32, (lanes, lanes), 0) - lax.broadcasted_iota(jnp.int32, (lanes, lanes), 1)
@@ -259,30 +252,31 @@
     def last_z(f):
         return jnp.where(first_lane, 0.0, pltpu.roll(f, 1, 1))
 
-    for turn in range(margin):
+    for turn, (first, first_e, end_h, end_e) in enumerate(ranges):
         last = turn == margin - 1
-        first, end = turn, width + 2 * margin - 1 - turn
-        ahead_x, ahead_y = ahead_z(0, first, end), ahead_z(1, first, end)
+        ahead_x, ahead_y = ahead_z(0, first, end_h), ahead_z(1, first, end_h)
         held_y = held_z = None
-        for i in range(first, end):
+        for i in range(first, end_e):
             ex, ey, ez = ext[0, i], ext[1, i], ext[2, i]
-            ey_x, ez_x = ext[1, i + 1], ext[2, i + 1]
             hx, hy, hz = ext[3, i], ext[4, i], ext[5, i]
-            if turn == 0:
-                hx, hy, hz = hx * (1 / COURANT), hy * (1 / COURANT), hz * (1 / COURANT)
-            here = slice((i - first) * high, (i - first + 1) * high)
-            hx = hx - ((next_y(ez) - ez) - ahead_y[here])
-            hy = hy - (ahead_x[here] - (ez_x - ez))
-            hz = hz - ((ey_x - ey) - (next_y(ex) - ex))
-
-            def clear(h):
-                h = jnp.concatenate([h[:rows], h[rows:] * before_rows], 0)
-                return h * before_x if i < margin else h
-
-            hx, hy, hz = clear(hx), clear(hy), clear(hz)
-            if not last:
+            if i < end_h:
+                ey_x, ez_x = ext[1, i + 1], ext[2, i + 1]
+                if turn == 0:
+                    hx, hy, hz = hx * (1 / COURANT), hy * (1 / COURANT), hz * (1 / COURANT)
+                here = slice((i - first) * high, (i - first + 1) * high)
+                hx = hx - ((next_y(ez) - ez) - ahead_y[here])
+                hy = hy - (ahead_x[here] - (ez_x - ez))
+                hz = hz - ((ey_x - ey) - (next_y(ex) - ex))
+
+                def clear(h):
+                    h = jnp.concatenate([h[:rows], h[rows:] * before_rows], 0)
+                    return h * before_x if i < margin else h
+
+                hx, hy, hz = clear(hx), clear(hy), clear(hz)
                 ext[3, i], ext[4, i], ext[5, i] = hx, hy, hz
-            if i > first:
+            if i >= first_e:
+                if held_y is None:
+                    held_y, held_z = ext[4, i - 1], ext[5, i - 1]
                 c = ext[6, i]
                 ex = ex + c * ((hz - last_y(hz)) - (hy - last_z(hy)))
                 ey = ey + c * ((hx - last_z(hx)) - (hz - held_z))
@@ -303,6 +297,46 @@
             held_y, held_z = hy, hz
 
 
+def inner_ranges(margin, width, core):
+    top = width + 2 * margin - 1
+    if core == 1:
+        return [(t, t + 1, top - margin - t, top - margin - t) for t in range(margin)]
+    return [(margin + t, margin + t + 1, top - t, top - t) for t in range(margin)]
+
+
+def outer_ranges(margin, width, core):
+    top = width + 2 * margin - 1
+    if core == 1:
+        return [(top - margin - t, top - margin - t, top - t, top - t) for t in range(margin)]
+    return [(t, t + 1, margin + t, margin + t + 1) for t in range(margin)]
+
+
+def early_steps(margin, count_y, ext_in, forward, mask, inner, ext, masked, final):
+    del ext_in
+    width, lanes = mask.shape[0], mask.shape[2]
+    rows = mask.shape[1]
+    _, at_y, core, _ = position()
+    valid = valid_rows(low_half(lanes), at_y, count_y)
+    in_at = (1 - core) * (width + margin)
+    for k in range(7):
+        for j in range(margin):
+            tile = inner[k, j]
+            ext[k, in_at + j, rows:] = jnp.where(valid, COURANT * COURANT / tile, 0.0) if k == 6 else tile
+    for c in range(2):
+        @pl.when(core == c)
+        def _():
+            steps(margin, inner_ranges(margin, width, c), ext, forward, mask, masked, final)
+
+
+def late_steps(margin, ext_in, masked_in, final_in, forward, mask, ext, masked, final):
+    del ext_in, masked_in, final_in
+    _, _, core, _ = position()
+    for c in range(2):
+        @pl.when(core == c)
+        def _():
+            steps(margin, outer_ranges(margin, mask.shape[0], c), ext, forward, mask, masked, final)
+
+
 def band_sum(reach, hop, sign, alone, weights, own, other, where, sums):
     width, _, lanes = own.shape
     _, _, core, _ = position()
@@ -449,6 +483,27 @@
     )(cells)
     inner = move(inner, routes.core)
     cells = pl.pallas_call(
+        functools.partial(join_core, margin),
+        out_shape=ext,
+        in_specs=[vmem] * 2,
+        out_specs=vmem,
+        input_output_aliases={0: 0},
+        compiler_params=params,
+        cost_estimate=cost(JOIN_X_US),
+        name="join_core",
+    )(cells, in_x)
+    fields = pltpu.VMEM((3, width, rows, lanes), f32)
+    cells, masked, final = pl.pallas_call(
+        functools.partial(early_steps, margin, routes.count_y),
+        out_shape=(ext, block, fields),
+        in_specs=[vmem] * 4,
+        out_specs=(vmem,) * 3,
+        input_output_aliases={0: 0},
+        compiler_params=params,
+        cost_estimate=cost(JOIN_X_US),
+        name="early_steps",
+    )(cells, forward_e, design_mask, inner)
+    cells = pl.pallas_call(
         functools.partial(join_outer, margin, routes.count_x),
         out_shape=ext,
         in_specs=[vmem] * 2,
@@ -458,16 +513,6 @@
         cost_estimate=cost(JOIN_X_US),
         name="join_outer",
     )(cells, out_x)
-    cells = pl.pallas_call(
-        functools.partial(join_core, margin),
-        out_shape=ext,
-        in_specs=[vmem] * 2,
-        out_specs=vmem,
-        input_output_aliases={0: 0},
-        compiler_params=params,
-        cost_estimate=cost(JOIN_X_US),
-        name="join_core",
-    )(cells, in_x)
     cells = pl.pallas_call(
         functools.partial(join_corner, margin, routes.count_x, routes.count_y),
         out_shape=ext,
@@ -479,14 +524,15 @@
         name="join_corner",
     )(cells, outer)
     _, masked, final = pl.pallas_call(
-        functools.partial(steps, margin, routes.count_x, routes.count_y),
-        out_shape=(ext, block, pltpu.VMEM((3, width, rows, lanes), f32)),
-        in_specs=[vmem] * 4,
+        functools.partial(late_steps, margin),
+        out_shape=(ext, block, fields),
+        in_specs=[vmem] * 5,
         out_specs=(vmem,) * 3,
-        input_output_aliases={0: 0},
-        compiler_params=params,
-        name="yee_steps",
-    )(cells, forward_e, design_mask, inner)
+        input_output_aliases={0: 0, 1: 1, 2: 2},
+        compiler_params=params,
+        cost_estimate=cost(JOIN_X_US),
+        name="late_steps",
+    )(cells, masked, final, forward_e, design_mask)
 
     other = move(masked, routes.core)
     via = []

time: 25.2 us -> 23.8 us (0.944)
  the two profiles are of different devices: /device:TPU:3 before, /device:TPU:0 now
where the time goes in v4:
time: 23.8 us; the launch traced here: 23.6 us
  starting transfers between devices  11.5 us (48%)
  Pallas kernels  6.8 us (29%)
  waiting for transfers between devices  4.54 us (19%)
  between operations  0.77 us (3%)
    ppermute x9, starting transfers between devices, move(): return lax.ppermute(value, BOTH, pairs)  11.5 us
    ppermute x9, waiting for transfers between devices, move(): return lax.ppermute(value, BOTH, pairs)  4.54 us
    pallas_call x1, Pallas kernels, shards(): pl.pallas_call(functools.partial(pack_y, margin), out_shape=(ext, edge, e...  1.31 us
    pallas_call x1, Pallas kernels, shards(): pl.pallas_call(functools.partial(early_steps, margin, routes.count_y), ou...  1.31 us
    pallas_call x1, Pallas kernels, shards(): pl.pallas_call(load_rest, out_shape=(ext, pltpu.VMEM(forward_e.shape, for...  1.18 us
    pallas_call x1, Pallas kernels, shards(): pl.pallas_call(functools.partial(late_steps, margin), out_shape=(ext, blo...  1 us
    pallas_call x1, Pallas kernels, shards(): pl.pallas_call(functools.partial(band_own, reach), out_shape=(block, shap...  0.75 us
    pallas_call x1, Pallas kernels, shards(): pl.pallas_call(functools.partial(band_end, routes.count_x), out_shape=blo...  0.69 us
  transfers between devices with their start and end apart: 9, of which 3 were waited for; matrix products, arithmetic and copies ran while one was open for 0% of the time, Pallas kernels for 16%

profile of v4, /device:TPU:0, one launch (start us, length us, event | category | flops | bytes accessed | tf_op | source)
XLA Modules:
  0.0 23.6 jit_solution(10617850778271121229)
XLA Ops:
  0.6 1.3 %pack_y.1 = (f32[7,16,40,128]{3,2,1,0:T(8,128)S(1)}, f32[7,4,8,128]{3,2,1,0:T(8,128)S(1)}, f32[7,4,8,128]{3,2,1,0:T(8,128)S(1)}) custom-call(f32[6,8,32,128]{3,2,1,0:T(8,128)} %fields.1, f32[8,32,128]{2,1,0:T(8,128)} %perm.1), custom_call_target="tpu_custom_call" | custom-call | tf_op jit(solution)/shard_map/pack_y/pallas_call | solution.py:428
  2.0 3.0 %collective-permute-start = (f32[7,4,8,128]{3,2,1,0:T(8,128)S(1)}, f32[7,4,8,128]{3,2,1,0:T(8,128)S(1)}, u32[]{:S(2)}, u32[]{:S(2)}) collective-permute-start(f32[7,4,8,128]{3,2,1,0:T(8,128)S(1)} %get-tuple-element.25), channel_id=1, source_target_pairs={{0,1},{1,0},{2,3},{3,2},{4,5},{5,4},{6,7},{7,6},{8,9},{9,8},{10,11... | collective-permute-start | bytes 344072 | tf_op jit(solution)/shard_map/ppermute | solution.py:423
  5.0 0.0 collective-permute-start.1
  5.0 0.1 pack_x.1
  5.0 0.6 %collective-permute-start.2 = (f32[26,32,128]{2,1,0:T(8,128)S(1)}, f32[26,32,128]{2,1,0:T(8,128)S(1)}, u32[]{:S(2)}, u32[]{:S(2)}) collective-permute-start(f32[26,32,128]{2,1,0:T(8,128)S(1)} %get-tuple-element.29), channel_id=1, source_target_pairs={{0,4},{1,5},{2,6},{3,7},{4,0},{5,1},{6,2},{7,3},{8,12},{9,13},{10,... | collective-permute-start | bytes 1277960 | tf_op jit(solution)/shard_map/ppermute | solution.py:423
  5.6 2.5 %collective-permute-start.4 = (f32[26,32,128]{2,1,0:T(8,128)S(1)}, f32[26,32,128]{2,1,0:T(8,128)S(1)}, u32[]{:S(2)}, u32[]{:S(2)}) collective-permute-start(f32[26,32,128]{2,1,0:T(8,128)S(1)} %get-tuple-element.34), channel_id=1, source_target_pairs={{0,1},{1,3},{2,0},{3,2},{4,8},{5,9},{6,10},{7,11},{8,4},{9,5},{10,... | collective-permute-start | bytes 1277960 | tf_op jit(solution)/shard_map/ppermute | solution.py:423
  8.1 1.2 %load_rest.1 = (f32[7,16,40,128]{3,2,1,0:T(8,128)S(1)}, bf16[4,3,8,32,128]{4,3,2,1,0:T(8,128)(2,1)S(1)}, s32[8,32,128]{2,1,0:T(8,128)S(1)}, f32[64,128]{1,0:T(8,128)S(1)}) custom-call(f32[7,16,40,128]{3,2,1,0:T(8,128)S(1)} %get-tuple-element.22.ext_in.ext, bf16[4,3,8,32,128]{4,3,2,1,0:T(8,128)(2,1)} %forward.1, ...), custom_call_target="tpu_custom_call", output_to_operand_aliasing={{0}: (0, {})} | custom-call | flops 50000000 | bytes 180000 | tf_op jit(solution)/shard_map/load_rest/pallas_call | solution.py:449
  9.3 0.0 collective-permute-done.side_a
  9.3 0.1 join_y.1
  9.5 0.1 collective-permute-start.3
  9.5 4.0 %collective-permute-start.5 = (f32[7,4,8,128]{3,2,1,0:T(8,128)S(1)}, f32[7,4,8,128]{3,2,1,0:T(8,128)S(1)}, u32[]{:S(2)}, u32[]{:S(2)}) collective-permute-start(f32[7,4,8,128]{3,2,1,0:T(8,128)S(1)} %get-tuple-element.35), channel_id=1, source_target_pairs={{0,1},{1,3},{2,0},{3,2},{4,8},{5,9},{6,10},{7,11},{8,4},{9,5},{10,... | collective-permute-start | bytes 344072 | tf_op jit(solution)/shard_map/ppermute | solution.py:423
  13.6 1.3 %early_steps.1 = (f32[7,16,40,128]{3,2,1,0:T(8,128)S(1)}, f32[8,32,128]{2,1,0:T(8,128)S(1)}, f32[3,8,32,128]{3,2,1,0:T(8,128)S(1)}) custom-call(f32[7,16,40,128]{3,2,1,0:T(8,128)S(1)} %join_core.1.ext_in, bf16[4,3,8,32,128]{4,3,2,1,0:T(8,128)(2,1)S(1)} %get-tuple-element.30.forward, ...), custom_call_target="tpu_custom_call", output_to_operand_aliasing={{0}: (0, {})} | custom-call | flops 50000000 | bytes 180000 | tf_op jit(solution)/shard_map/early_steps/pallas_call | solution.py:496
  14.9 0.1 join_outer.1.ext_in
  15.0 0.9 %collective-permute-done.5.outer = f32[7,4,8,128]{3,2,1,0:T(8,128)S(1)} collective-permute-done((f32[7,4,8,128]{3,2,1,0:T(8,128)S(1)}, f32[7,4,8,128]{3,2,1,0:T(8,128)S(1)}, u32[]{:S(2)}, u32[]{:S(2)}) %collective-permute-start.5) | collective-permute-done | bytes 114720 | tf_op jit(solution)/shard_map/ppermute | solution.py:423
  15.9 1.0 %late_steps.1 = (f32[7,16,40,128]{3,2,1,0:T(8,128)S(1)}, f32[8,32,128]{2,1,0:T(8,128)S(1)}, f32[3,8,32,128]{3,2,1,0:T(8,128)S(1)}) custom-call(f32[7,16,40,128]{3,2,1,0:T(8,128)S(1)} %join_corner.1.ext_in, f32[8,32,128]{2,1,0:T(8,128)S(1)} %get-tuple-element.36.masked_in, ...), custom_call_target="tpu_custom_call", output_to_operand_aliasing={{0}: (0, {}), {1}: (1, {}), {2}: (2, {})} | custom-call | flops 50000000 | bytes 180000 | tf_op jit(solution)/shard_map/late_steps/pallas_call | solution.py:526
  16.9 0.1 collective-permute-start.6
  17.0 0.1 band_hop.2
  17.1 0.5 %collective-permute-start.7 = (f32[8,32,128]{2,1,0:T(8,128)S(1)}, f32[8,32,128]{2,1,0:T(8,128)S(1)}, u32[]{:S(2)}, u32[]{:S(2)}) collective-permute-start(f32[8,32,128]{2,1,0:T(8,128)S(1)} %band_hop.2), channel_id=1, source_target_pairs={{0,4},{1,5},{2,6},{3,7},{4,12},{5,13},{6,14},{7,15},{8,0},{9,1},{1... | collective-permute-start | bytes 393224 | tf_op jit(solution)/shard_map/ppermute | solution.py:423
  17.6 0.7 %collective-permute-done.6.other.refs_0_ = f32[8,32,128]{2,1,0:T(8,128)S(1)} collective-permute-done((f32[8,32,128]{2,1,0:T(8,128)S(1)}, f32[8,32,128]{2,1,0:T(8,128)S(1)}, u32[]{:S(2)}, u32[]{:S(2)}) %collective-permute-start.6) | collective-permute-done | bytes 131104 | tf_op jit(solution)/shard_map/ppermute | solution.py:423
  18.3 0.2 band_hop.3
  18.5 0.8 %collective-permute-start.8 = (f32[8,32,128]{2,1,0:T(8,128)S(1)}, f32[8,32,128]{2,1,0:T(8,128)S(1)}, u32[]{:S(2)}, u32[]{:S(2)}) collective-permute-start(f32[8,32,128]{2,1,0:T(8,128)S(1)} %band_hop.3), channel_id=1, source_target_pairs={{0,8},{1,9},{2,10},{3,11},{4,0},{5,1},{6,2},{7,3},{8,16},{9,17},{1... | collective-permute-start | bytes 393224 | tf_op jit(solution)/shard_map/ppermute | solution.py:423
  19.3 0.8 %band_own.1 = (f32[8,32,128]{2,1,0:T(8,128)S(1)}, f32[3,8,32,128]{3,2,1,0:T(8,128)}) custom-call(f32[64,128]{1,0:T(8,128)S(1)} %get-tuple-element.23.weights, f32[8,32,128]{2,1,0:T(8,128)S(1)} %get-tuple-element.38.own, f32[8,32,128]{2,1,0:T(8,128)S(1)} %collective-permute-done.6.other.refs_0_, f32[3,8,32,128]{3,2,1,0:T(8,128)S(1)} %get-tuple-element.39.final), custom_call_target="tpu_custom_call" | custom-call | flops 2000000000 | bytes 7200000 | tf_op jit(solution)/shard_map/band_own/pallas_call | solution.py:555
  20.1 2.9 %collective-permute-done.7.via_1 = f32[8,32,128]{2,1,0:T(8,128)S(1)} collective-permute-done((f32[8,32,128]{2,1,0:T(8,128)S(1)}, f32[8,32,128]{2,1,0:T(8,128)S(1)}, u32[]{:S(2)}, u32[]{:S(2)}) %collective-permute-start.7) | collective-permute-done | bytes 131104 | tf_op jit(solution)/shard_map/ppermute | solution.py:423
  22.9 0.7 %band_end.1 = f32[8,32,128]{2,1,0:T(8,128)} custom-call(f32[8,32,128]{2,1,0:T(8,128)S(1)} %get-tuple-element.40.base, f32[8,32,128]{2,1,0:T(8,128)S(1)} %collective-permute-done.7.via_1, f32[8,32,128]{2,1,0:T(8,128)S(1)} %collective-permute-done.8.via_0), custom_call_target="tpu_custom_call" | custom-call | tf_op jit(solution)/shard_map/band_end/pallas_call | solution.py:565
  (8 shorter events, 0.1 us)
Async XLA Ops:
  2.0 7.4 %collective-permute-start = (f32[7,4,8,128]{3,2,1,0:T(8,128)S(1)}, f32[7,4,8,128]{3,2,1,0:T(8,128)S(1)}, u32[]{:S(2)}, u32[]{:S(2)}) collective-permute-start(f32[7,4,8,128]{3,2,1,0:T(8,128)S(1)} %get-tuple-element.25), channel_id=1, source_target_pairs={{0,1},{1,0},{2,3},{3,2},{4,5},{5,4},{6,7},{7,6},{8,9},{9,8},{10,11... | collective-permute-start | bytes 344072 | tf_op jit(solution)/shard_map/ppermute | solution.py:423
  5.0 4.4 %collective-permute-start.1 = (f32[7,4,8,128]{3,2,1,0:T(8,128)S(1)}, f32[7,4,8,128]{3,2,1,0:T(8,128)S(1)}, u32[]{:S(2)}, u32[]{:S(2)}) collective-permute-start(f32[7,4,8,128]{3,2,1,0:T(8,128)S(1)} %get-tuple-element.26), channel_id=1, source_target_pairs={{0,4},{1,2},{2,1},{3,7},{4,0},{5,6},{6,5},{7,3},{8,12},{9,10},{10,... | collective-permute-start | bytes 344072 | tf_op jit(solution)/shard_map/ppermute | solution.py:423
  5.0 8.5 %collective-permute-start.2 = (f32[26,32,128]{2,1,0:T(8,128)S(1)}, f32[26,32,128]{2,1,0:T(8,128)S(1)}, u32[]{:S(2)}, u32[]{:S(2)}) collective-permute-start(f32[26,32,128]{2,1,0:T(8,128)S(1)} %get-tuple-element.29), channel_id=1, source_target_pairs={{0,4},{1,5},{2,6},{3,7},{4,0},{5,1},{6,2},{7,3},{8,12},{9,13},{10,... | collective-permute-start | bytes 1277960 | tf_op jit(solution)/shard_map/ppermute | solution.py:423
  5.6 9.3 %collective-permute-start.4 = (f32[26,32,128]{2,1,0:T(8,128)S(1)}, f32[26,32,128]{2,1,0:T(8,128)S(1)}, u32[]{:S(2)}, u32[]{:S(2)}) collective-permute-start(f32[26,32,128]{2,1,0:T(8,128)S(1)} %get-tuple-element.34), channel_id=1, source_target_pairs={{0,1},{1,3},{2,0},{3,2},{4,8},{5,9},{6,10},{7,11},{8,4},{9,5},{10,... | collective-permute-start | bytes 1277960 | tf_op jit(solution)/shard_map/ppermute | solution.py:423
  9.5 4.1 %collective-permute-start.3 = (f32[7,4,8,128]{3,2,1,0:T(8,128)S(1)}, f32[7,4,8,128]{3,2,1,0:T(8,128)S(1)}, u32[]{:S(2)}, u32[]{:S(2)}) collective-permute-start(f32[7,4,8,128]{3,2,1,0:T(8,128)S(1)} %get-tuple-element.32), channel_id=1, source_target_pairs={{0,4},{1,5},{2,6},{3,7},{4,0},{5,1},{6,2},{7,3},{8,12},{9,13},{10,... | collective-permute-start | bytes 344072 | tf_op jit(solution)/shard_map/ppermute | solution.py:423
  9.5 6.3 %collective-permute-start.5 = (f32[7,4,8,128]{3,2,1,0:T(8,128)S(1)}, f32[7,4,8,128]{3,2,1,0:T(8,128)S(1)}, u32[]{:S(2)}, u32[]{:S(2)}) collective-permute-start(f32[7,4,8,128]{3,2,1,0:T(8,128)S(1)} %get-tuple-element.35), channel_id=1, source_target_pairs={{0,1},{1,3},{2,0},{3,2},{4,8},{5,9},{6,10},{7,11},{8,4},{9,5},{10,... | collective-permute-start | bytes 344072 | tf_op jit(solution)/shard_map/ppermute | solution.py:423
  16.9 1.4 %collective-permute-start.6 = (f32[8,32,128]{2,1,0:T(8,128)S(1)}, f32[8,32,128]{2,1,0:T(8,128)S(1)}, u32[]{:S(2)}, u32[]{:S(2)}) collective-permute-start(f32[8,32,128]{2,1,0:T(8,128)S(1)} %get-tuple-element.38.own), channel_id=1, source_target_pairs={{0,4},{1,5},{2,6},{3,7},{4,0},{5,1},{6,2},{7,3},{8,12},{9,13},{10,... | collective-permute-start | bytes 393224 | tf_op jit(solution)/shard_map/ppermute | solution.py:423
  17.1 5.9 %collective-permute-start.7 = (f32[8,32,128]{2,1,0:T(8,128)S(1)}, f32[8,32,128]{2,1,0:T(8,128)S(1)}, u32[]{:S(2)}, u32[]{:S(2)}) collective-permute-start(f32[8,32,128]{2,1,0:T(8,128)S(1)} %band_hop.2), channel_id=1, source_target_pairs={{0,4},{1,5},{2,6},{3,7},{4,12},{5,13},{6,14},{7,15},{8,0},{9,1},{1... | collective-permute-start | bytes 393224 | tf_op jit(solution)/shard_map/ppermute | solution.py:423
  18.5 4.5 %collective-permute-start.8 = (f32[8,32,128]{2,1,0:T(8,128)S(1)}, f32[8,32,128]{2,1,0:T(8,128)S(1)}, u32[]{:S(2)}, u32[]{:S(2)}) collective-permute-start(f32[8,32,128]{2,1,0:T(8,128)S(1)} %band_hop.3), channel_id=1, source_target_pairs={{0,8},{1,9},{2,10},{3,11},{4,0},{5,1},{6,2},{7,3},{8,16},{9,17},{1... | collective-permute-start | bytes 393224 | tf_op jit(solution)/shard_map/ppermute | solution.py:423

commit v5 on v4

--- a/solution.py
+++ b/solution.py
@@ -59,7 +59,7 @@
         core = lambda x, y: (x ^ 1, y)
         self.core = make(core, None)
         self.out_x = make(out_partner, around)
-        self.side_a = make(lambda x, y: (x, y ^ 1), None)
+        self.side_a = [make(lambda x, y: (x, y ^ 1) if y // 2 % 2 == n else None, core) for n in range(2)]
         self.side_b = make(b_partner, core)
         self.ring_1 = make(lambda x, y: ring(x, y, 1), None)
         self.ring_0 = make(lambda x, y: ring(x, y, 0), None)
@@ -95,7 +95,7 @@
     return at_x, at_y, lax.rem(at_x, 2), lax.rem(at_y, 2)
 
 
-def pack_y(margin, fields, perm, ext, side_a, side_b, sems):
+def pack_y(margin, fields, perm, ext, side_a0, side_b, side_a1, sems):
     width, rows, lanes = perm.shape
     _, _, _, odd = position()
     low = low_half(lanes)
@@ -111,7 +111,7 @@
             return edge_tile(low, ext[k, margin + x, where], ext[k, margin + x + width // 2, where], upper)
 
         for j in range(width // 2):
-            side_a[k, j] = edge(j, 1 - odd)
+            side_a0[k, j] = side_a1[k, j] = edge(j, 1 - odd)
             side_b[k, j] = edge(j, odd)
 
 
@@ -134,16 +134,18 @@
     return jnp.where(core == 0, at_x > 0, at_x < count_x - 1)
 
 
-def join_y(margin, count_y, ext_in, side_a, side_b, ext, outer):
+def join_y(margin, count_y, ext_in, side_a0, side_b, side_a1, ext, outer):
     del ext_in
     width, rows, lanes = ext.shape[1] - 2 * margin, ext.shape[2] - SUB, ext.shape[3]
     _, at_y, core, odd = position()
     low = low_half(lanes)
     valid = valid_rows(low, at_y, count_y)
+    in_first = lax.rem(at_y // 2, 2) == 0
     for k in range(7):
         for x in range(width):
             j, upper = x % (width // 2), x // (width // 2)
-            tile = tail_tile(low, odd, side_a[k, j], side_b[k, j], upper)
+            side_a = jnp.where(in_first, side_a0[k, j], side_a1[k, j])
+            tile = tail_tile(low, odd, side_a, side_b[k, j], upper)
             ext[k, margin + x, rows:] = jnp.where(valid, tile, 1.0 if k == 6 else 0.0)
         for j in range(margin):
             outer[k, j] = ext[k, margin + core * (width - margin) + j, rows:]
@@ -425,11 +427,11 @@
     def from_hbm(*values):
         return [pltpu.with_memory_space_constraint(value, pltpu.HBM) for value in values]
 
-    cells, side_a, side_b = pl.pallas_call(
+    cells, side_a0, side_b, side_a1 = pl.pallas_call(
         functools.partial(pack_y, margin),
-        out_shape=(ext, edge, edge),
+        out_shape=(ext, edge, edge, edge),
         in_specs=[hbm] * 2,
-        out_specs=(vmem,) * 3,
+        out_specs=(vmem,) * 4,
         scratch_shapes=[pltpu.SemaphoreType.DMA((7,))],
         compiler_params=params,
         name="pack_y",
@@ -442,8 +444,9 @@
         compiler_params=params,
         name="pack_x",
     )(cells)
+    side_a0 = move(side_a0, routes.side_a[0])
     side_b = move(side_b, routes.side_b)
-    side_a = move(side_a, routes.side_a)
+    side_a1 = move(side_a1, routes.side_a[1])
     in_x = move(in_x, routes.core)
     out_x = move(out_x, routes.out_x)
     cells, forward_e, design_mask, weights = pl.pallas_call(
@@ -463,13 +466,13 @@
     cells, outer = pl.pallas_call(
         functools.partial(join_y, margin, routes.count_y),
         out_shape=(ext, corner),
-        in_specs=[vmem] * 3,
+        in_specs=[vmem] * 4,
         out_specs=(vmem,) * 2,
         input_output_aliases={0: 0},
         compiler_params=params,
         cost_estimate=cost(JOIN_Y_US),
         name="join_y",
-    )(cells, side_a, side_b)
+    )(cells, side_a0, side_b, side_a1)
     outer = move(outer, routes.out_x)
     cells, inner = pl.pallas_call(
         functools.partial(join_inner, margin, routes.count_y),

time: 23.8 us -> 23 us (0.966)
  starting transfers between devices: 11.5 us -> 10.1 us
  waiting for transfers between devices: 4.54 us -> 5.2 us
    ppermute x9 -> x10, starting transfers between devices: 11.5 us -> 10.1 us  [move(): return lax.ppermute(value, BOTH, pairs)]
    ppermute x9 -> x10, waiting for transfers between devices: 4.54 us -> 5.2 us  [move(): return lax.ppermute(value, BOTH, pairs)]
  transfers between devices with their start and end apart: 9 -> 10, of which waited for: 3 -> 5; matrix products, arithmetic and copies ran while one was open for 0% -> 0% of each run, Pallas kernels for 16% -> 16%
where the time goes in v5:
time: 23 us; the launch traced here: 22.8 us
  starting transfers between devices  10.1 us (44%)
  Pallas kernels  6.77 us (29%)
  waiting for transfers between devices  5.2 us (23%)
  between operations  0.74 us (3%)
    ppermute x10, starting transfers between devices, move(): return lax.ppermute(value, BOTH, pairs)  10.1 us
    ppermute x10, waiting for transfers between devices, move(): return lax.ppermute(value, BOTH, pairs)  5.2 us
    pallas_call x1, Pallas kernels, shards(): pl.pallas_call(functools.partial(pack_y, margin), out_shape=(ext, edge, e...  1.31 us
    pallas_call x1, Pallas kernels, shards(): pl.pallas_call(functools.partial(early_steps, margin, routes.count_y), ou...  1.31 us
    pallas_call x1, Pallas kernels, shards(): pl.pallas_call(load_rest, out_shape=(ext, pltpu.VMEM(forward_e.shape, for...  1.18 us
    pallas_call x1, Pallas kernels, shards(): pl.pallas_call(functools.partial(late_steps, margin), out_shape=(ext, blo...  1 us
    pallas_call x1, Pallas kernels, shards(): pl.pallas_call(functools.partial(band_own, reach), out_shape=(block, shap...  0.75 us
    pallas_call x1, Pallas kernels, shards(): pl.pallas_call(functools.partial(band_end, routes.count_x), out_shape=blo...  0.69 us
  transfers between devices with their start and end apart: 10, of which 5 were waited for; matrix products, arithmetic and copies ran while one was open for 0% of the time, Pallas kernels for 16%

profile of v5, /device:TPU:0, one launch (start us, length us, event | category | flops | bytes accessed | tf_op | source)
XLA Modules:
  0.0 22.8 jit_solution(7122791384469855963)
XLA Ops:
  0.6 1.3 %pack_y.1 = (f32[7,16,40,128]{3,2,1,0:T(8,128)S(1)}, f32[7,4,8,128]{3,2,1,0:T(8,128)S(1)}, f32[7,4,8,128]{3,2,1,0:T(8,128)S(1)}, f32[7,4,8,128]{3,2,1,0:T(8,128)S(1)}) custom-call(f32[6,8,32,128]{3,2,1,0:T(8,128)} %fields.1, f32[8,32,128]{2,1,0:T(8,128)} %perm.1), custom_call_target="tpu_custom_call" | custom-call | tf_op jit(solution)/shard_map/pack_y/pallas_call | solution.py:430
  2.0 3.0 %collective-permute-start = (f32[7,4,8,128]{3,2,1,0:T(8,128)S(1)}, f32[7,4,8,128]{3,2,1,0:T(8,128)S(1)}, u32[]{:S(2)}, u32[]{:S(2)}) collective-permute-start(f32[7,4,8,128]{3,2,1,0:T(8,128)S(1)} %get-tuple-element.26), channel_id=1, source_target_pairs={{0,1},{1,0},{2,6},{3,7},{4,5},{5,4},{6,2},{7,3},{8,9},{9,8},{10,14... | collective-permute-start | bytes 344072 | tf_op jit(solution)/shard_map/ppermute | solution.py:425
  5.0 0.5 %collective-permute-start.2 = (f32[7,4,8,128]{3,2,1,0:T(8,128)S(1)}, f32[7,4,8,128]{3,2,1,0:T(8,128)S(1)}, u32[]{:S(2)}, u32[]{:S(2)}) collective-permute-start(f32[7,4,8,128]{3,2,1,0:T(8,128)S(1)} %get-tuple-element.28), channel_id=1, source_target_pairs={{0,4},{1,5},{2,3},{3,2},{4,0},{5,1},{6,7},{7,6},{8,12},{9,13},{10,... | collective-permute-start | bytes 344072 | tf_op jit(solution)/shard_map/ppermute | solution.py:425
  5.5 0.1 pack_x.1
  5.5 0.1 collective-permute-start.3
  5.6 1.6 %collective-permute-start.5 = (f32[26,32,128]{2,1,0:T(8,128)S(1)}, f32[26,32,128]{2,1,0:T(8,128)S(1)}, u32[]{:S(2)}, u32[]{:S(2)}) collective-permute-start(f32[26,32,128]{2,1,0:T(8,128)S(1)} %get-tuple-element.36), channel_id=1, source_target_pairs={{0,1},{1,3},{2,0},{3,2},{4,8},{5,9},{6,10},{7,11},{8,4},{9,5},{10,... | collective-permute-start | bytes 1277960 | tf_op jit(solution)/shard_map/ppermute | solution.py:425
  7.2 1.2 %load_rest.1 = (f32[7,16,40,128]{3,2,1,0:T(8,128)S(1)}, bf16[4,3,8,32,128]{4,3,2,1,0:T(8,128)(2,1)S(1)}, s32[8,32,128]{2,1,0:T(8,128)S(1)}, f32[64,128]{1,0:T(8,128)S(1)}) custom-call(f32[7,16,40,128]{3,2,1,0:T(8,128)S(1)} %get-tuple-element.23.ext_in.ext, bf16[4,3,8,32,128]{4,3,2,1,0:T(8,128)(2,1)} %forward.1, ...), custom_call_target="tpu_custom_call", output_to_operand_aliasing={{0}: (0, {})} | custom-call | flops 50000000 | bytes 180000 | tf_op jit(solution)/shard_map/load_rest/pallas_call | solution.py:452
  8.3 0.3 %collective-permute-done.side_a0 = f32[7,4,8,128]{3,2,1,0:T(8,128)S(1)} collective-permute-done((f32[7,4,8,128]{3,2,1,0:T(8,128)S(1)}, f32[7,4,8,128]{3,2,1,0:T(8,128)S(1)}, u32[]{:S(2)}, u32[]{:S(2)}) %collective-permute-start) | collective-permute-done | bytes 114720 | tf_op jit(solution)/shard_map/ppermute | solution.py:425
  8.7 0.1 join_y.1
  8.8 0.1 collective-permute-start.4
  8.9 3.4 %collective-permute-start.6 = (f32[7,4,8,128]{3,2,1,0:T(8,128)S(1)}, f32[7,4,8,128]{3,2,1,0:T(8,128)S(1)}, u32[]{:S(2)}, u32[]{:S(2)}) collective-permute-start(f32[7,4,8,128]{3,2,1,0:T(8,128)S(1)} %get-tuple-element.37), channel_id=1, source_target_pairs={{0,1},{1,3},{2,0},{3,2},{4,8},{5,9},{6,10},{7,11},{8,4},{9,5},{10,... | collective-permute-start | bytes 344072 | tf_op jit(solution)/shard_map/ppermute | solution.py:425
  12.3 1.3 %early_steps.1 = (f32[7,16,40,128]{3,2,1,0:T(8,128)S(1)}, f32[8,32,128]{2,1,0:T(8,128)S(1)}, f32[3,8,32,128]{3,2,1,0:T(8,128)S(1)}) custom-call(f32[7,16,40,128]{3,2,1,0:T(8,128)S(1)} %join_core.1.ext_in, bf16[4,3,8,32,128]{4,3,2,1,0:T(8,128)(2,1)S(1)} %get-tuple-element.32.forward, ...), custom_call_target="tpu_custom_call", output_to_operand_aliasing={{0}: (0, {})} | custom-call | flops 50000000 | bytes 180000 | tf_op jit(solution)/shard_map/early_steps/pallas_call | solution.py:499
  13.6 0.2 collective-permute-done.5.out_x
  13.8 1.2 %collective-permute-done.6.outer = f32[7,4,8,128]{3,2,1,0:T(8,128)S(1)} collective-permute-done((f32[7,4,8,128]{3,2,1,0:T(8,128)S(1)}, f32[7,4,8,128]{3,2,1,0:T(8,128)S(1)}, u32[]{:S(2)}, u32[]{:S(2)}) %collective-permute-start.6) | collective-permute-done | bytes 114720 | tf_op jit(solution)/shard_map/ppermute | solution.py:425
  15.1 1.0 %late_steps.1 = (f32[7,16,40,128]{3,2,1,0:T(8,128)S(1)}, f32[8,32,128]{2,1,0:T(8,128)S(1)}, f32[3,8,32,128]{3,2,1,0:T(8,128)S(1)}) custom-call(f32[7,16,40,128]{3,2,1,0:T(8,128)S(1)} %join_corner.1.ext_in, f32[8,32,128]{2,1,0:T(8,128)S(1)} %get-tuple-element.38.masked_in, ...), custom_call_target="tpu_custom_call", output_to_operand_aliasing={{0}: (0, {}), {1}: (1, {}), {2}: (2, {})} | custom-call | flops 50000000 | bytes 180000 | tf_op jit(solution)/shard_map/late_steps/pallas_call | solution.py:529
  16.1 0.1 collective-permute-start.7
  16.2 0.1 band_hop.2
  16.3 0.5 %collective-permute-start.8 = (f32[8,32,128]{2,1,0:T(8,128)S(1)}, f32[8,32,128]{2,1,0:T(8,128)S(1)}, u32[]{:S(2)}, u32[]{:S(2)}) collective-permute-start(f32[8,32,128]{2,1,0:T(8,128)S(1)} %band_hop.2), channel_id=1, source_target_pairs={{0,4},{1,5},{2,6},{3,7},{4,12},{5,13},{6,14},{7,15},{8,0},{9,1},{1... | collective-permute-start | bytes 393224 | tf_op jit(solution)/shard_map/ppermute | solution.py:425
  16.8 0.7 %collective-permute-done.7.other.refs_0_ = f32[8,32,128]{2,1,0:T(8,128)S(1)} collective-permute-done((f32[8,32,128]{2,1,0:T(8,128)S(1)}, f32[8,32,128]{2,1,0:T(8,128)S(1)}, u32[]{:S(2)}, u32[]{:S(2)}) %collective-permute-start.7) | collective-permute-done | bytes 131104 | tf_op jit(solution)/shard_map/ppermute | solution.py:425
  17.5 0.2 band_hop.3
  17.7 1.0 %collective-permute-start.9 = (f32[8,32,128]{2,1,0:T(8,128)S(1)}, f32[8,32,128]{2,1,0:T(8,128)S(1)}, u32[]{:S(2)}, u32[]{:S(2)}) collective-permute-start(f32[8,32,128]{2,1,0:T(8,128)S(1)} %band_hop.3), channel_id=1, source_target_pairs={{0,8},{1,9},{2,10},{3,11},{4,0},{5,1},{6,2},{7,3},{8,16},{9,17},{1... | collective-permute-start | bytes 393224 | tf_op jit(solution)/shard_map/ppermute | solution.py:425
  18.7 0.8 %band_own.1 = (f32[8,32,128]{2,1,0:T(8,128)S(1)}, f32[3,8,32,128]{3,2,1,0:T(8,128)}) custom-call(f32[64,128]{1,0:T(8,128)S(1)} %get-tuple-element.24.weights, f32[8,32,128]{2,1,0:T(8,128)S(1)} %get-tuple-element.40.own, f32[8,32,128]{2,1,0:T(8,128)S(1)} %collective-permute-done.7.other.refs_0_, f32[3,8,32,128]{3,2,1,0:T(8,128)S(1)} %get-tuple-element.41.final), custom_call_target="tpu_custom_call" | custom-call | flops 2000000000 | bytes 7200000 | tf_op jit(solution)/shard_map/band_own/pallas_call | solution.py:558
  19.4 2.7 %collective-permute-done.8.via_1 = f32[8,32,128]{2,1,0:T(8,128)S(1)} collective-permute-done((f32[8,32,128]{2,1,0:T(8,128)S(1)}, f32[8,32,128]{2,1,0:T(8,128)S(1)}, u32[]{:S(2)}, u32[]{:S(2)}) %collective-permute-start.8) | collective-permute-done | bytes 131104 | tf_op jit(solution)/shard_map/ppermute | solution.py:425
  22.2 0.7 %band_end.1 = f32[8,32,128]{2,1,0:T(8,128)} custom-call(f32[8,32,128]{2,1,0:T(8,128)S(1)} %get-tuple-element.42.base, f32[8,32,128]{2,1,0:T(8,128)S(1)} %collective-permute-done.8.via_1, f32[8,32,128]{2,1,0:T(8,128)S(1)} %collective-permute-done.9.via_0), custom_call_target="tpu_custom_call" | custom-call | tf_op jit(solution)/shard_map/band_end/pallas_call | solution.py:568
  (10 shorter events, 0.2 us)
Async XLA Ops:
  2.0 6.7 %collective-permute-start = (f32[7,4,8,128]{3,2,1,0:T(8,128)S(1)}, f32[7,4,8,128]{3,2,1,0:T(8,128)S(1)}, u32[]{:S(2)}, u32[]{:S(2)}) collective-permute-start(f32[7,4,8,128]{3,2,1,0:T(8,128)S(1)} %get-tuple-element.26), channel_id=1, source_target_pairs={{0,1},{1,0},{2,6},{3,7},{4,5},{5,4},{6,2},{7,3},{8,9},{9,8},{10,14... | collective-permute-start | bytes 344072 | tf_op jit(solution)/shard_map/ppermute | solution.py:425
  5.0 3.7 %collective-permute-start.1 = (f32[7,4,8,128]{3,2,1,0:T(8,128)S(1)}, f32[7,4,8,128]{3,2,1,0:T(8,128)S(1)}, u32[]{:S(2)}, u32[]{:S(2)}) collective-permute-start(f32[7,4,8,128]{3,2,1,0:T(8,128)S(1)} %get-tuple-element.27), channel_id=1, source_target_pairs={{0,4},{1,2},{2,1},{3,7},{4,0},{5,6},{6,5},{7,3},{8,12},{9,10},{10,... | collective-permute-start | bytes 344072 | tf_op jit(solution)/shard_map/ppermute | solution.py:425
  5.0 3.7 %collective-permute-start.2 = (f32[7,4,8,128]{3,2,1,0:T(8,128)S(1)}, f32[7,4,8,128]{3,2,1,0:T(8,128)S(1)}, u32[]{:S(2)}, u32[]{:S(2)}) collective-permute-start(f32[7,4,8,128]{3,2,1,0:T(8,128)S(1)} %get-tuple-element.28), channel_id=1, source_target_pairs={{0,4},{1,5},{2,3},{3,2},{4,0},{5,1},{6,7},{7,6},{8,12},{9,13},{10,... | collective-permute-start | bytes 344072 | tf_op jit(solution)/shard_map/ppermute | solution.py:425
  5.5 6.7 %collective-permute-start.3 = (f32[26,32,128]{2,1,0:T(8,128)S(1)}, f32[26,32,128]{2,1,0:T(8,128)S(1)}, u32[]{:S(2)}, u32[]{:S(2)}) collective-permute-start(f32[26,32,128]{2,1,0:T(8,128)S(1)} %get-tuple-element.31), channel_id=1, source_target_pairs={{0,4},{1,5},{2,6},{3,7},{4,0},{5,1},{6,2},{7,3},{8,12},{9,13},{10,... | collective-permute-start | bytes 1277960 | tf_op jit(solution)/shard_map/ppermute | solution.py:425
  5.6 8.2 %collective-permute-start.5 = (f32[26,32,128]{2,1,0:T(8,128)S(1)}, f32[26,32,128]{2,1,0:T(8,128)S(1)}, u32[]{:S(2)}, u32[]{:S(2)}) collective-permute-start(f32[26,32,128]{2,1,0:T(8,128)S(1)} %get-tuple-element.36), channel_id=1, source_target_pairs={{0,1},{1,3},{2,0},{3,2},{4,8},{5,9},{6,10},{7,11},{8,4},{9,5},{10,... | collective-permute-start | bytes 1277960 | tf_op jit(solution)/shard_map/ppermute | solution.py:425
  8.8 3.5 %collective-permute-start.4 = (f32[7,4,8,128]{3,2,1,0:T(8,128)S(1)}, f32[7,4,8,128]{3,2,1,0:T(8,128)S(1)}, u32[]{:S(2)}, u32[]{:S(2)}) collective-permute-start(f32[7,4,8,128]{3,2,1,0:T(8,128)S(1)} %get-tuple-element.34), channel_id=1, source_target_pairs={{0,4},{1,5},{2,6},{3,7},{4,0},{5,1},{6,2},{7,3},{8,12},{9,13},{10,... | collective-permute-start | bytes 344072 | tf_op jit(solution)/shard_map/ppermute | solution.py:425
  8.9 6.2 %collective-permute-start.6 = (f32[7,4,8,128]{3,2,1,0:T(8,128)S(1)}, f32[7,4,8,128]{3,2,1,0:T(8,128)S(1)}, u32[]{:S(2)}, u32[]{:S(2)}) collective-permute-start(f32[7,4,8,128]{3,2,1,0:T(8,128)S(1)} %get-tuple-element.37), channel_id=1, source_target_pairs={{0,1},{1,3},{2,0},{3,2},{4,8},{5,9},{6,10},{7,11},{8,4},{9,5},{10,... | collective-permute-start | bytes 344072 | tf_op jit(solution)/shard_map/ppermute | solution.py:425
  16.1 1.4 %collective-permute-start.7 = (f32[8,32,128]{2,1,0:T(8,128)S(1)}, f32[8,32,128]{2,1,0:T(8,128)S(1)}, u32[]{:S(2)}, u32[]{:S(2)}) collective-permute-start(f32[8,32,128]{2,1,0:T(8,128)S(1)} %get-tuple-element.40.own), channel_id=1, source_target_pairs={{0,4},{1,5},{2,6},{3,7},{4,0},{5,1},{6,2},{7,3},{8,12},{9,13},{10,... | collective-permute-start | bytes 393224 | tf_op jit(solution)/shard_map/ppermute | solution.py:425
  16.3 5.9 %collective-permute-start.8 = (f32[8,32,128]{2,1,0:T(8,128)S(1)}, f32[8,32,128]{2,1,0:T(8,128)S(1)}, u32[]{:S(2)}, u32[]{:S(2)}) collective-permute-start(f32[8,32,128]{2,1,0:T(8,128)S(1)} %band_hop.2), channel_id=1, source_target_pairs={{0,4},{1,5},{2,6},{3,7},{4,12},{5,13},{6,14},{7,15},{8,0},{9,1},{1... | collective-permute-start | bytes 393224 | tf_op jit(solution)/shard_map/ppermute | solution.py:425
  17.7 4.5 %collective-permute-start.9 = (f32[8,32,128]{2,1,0:T(8,128)S(1)}, f32[8,32,128]{2,1,0:T(8,128)S(1)}, u32[]{:S(2)}, u32[]{:S(2)}) collective-permute-start(f32[8,32,128]{2,1,0:T(8,128)S(1)} %band_hop.3), channel_id=1, source_target_pairs={{0,8},{1,9},{2,10},{3,11},{4,0},{5,1},{6,2},{7,3},{8,16},{9,17},{1... | collective-permute-start | bytes 393224 | tf_op jit(solution)/shard_map/ppermute | solution.py:425

commit v6 on v5

--- a/solution.py
+++ b/solution.py
@@ -86,6 +86,20 @@
     return jnp.where(low, after, before)
 
 
+SHORT = (4, 6)
+LONG = (0, 1, 2, 3, 5)
+
+
+def short_places(width, depth):
+    for n, (k, x) in enumerate((k, x) for k in SHORT for x in range(width)):
+        yield k, x, n * depth // SUB, n * depth % SUB
+
+
+def side_tiles(width, margin):
+    assert margin * 2 == SUB
+    return len(LONG) * width // 2, -(-len(SHORT) * width * (margin - 1) // SUB)
+
+
 def low_half(lanes):
     return lax.broadcasted_iota(jnp.int32, (SUB, lanes), 0) < SUB // 2
 
@@ -103,16 +117,33 @@
     loads = [pltpu.make_async_copy(fields.at[k] if k < 6 else perm, ext.at[(k, *own)], sems.at[k]) for k in range(7)]
     for load in loads:
         load.start()
+
+    def rows_of(k, x, upper):
+        return ext[k, margin + x, pl.ds(pl.multiple_of(upper * (rows - SUB), SUB), SUB)]
+
     for k in range(7):
         loads[k].wait()
-
-        def edge(x, upper):
-            where = pl.ds(pl.multiple_of(upper * (rows - SUB), SUB), SUB)
-            return edge_tile(low, ext[k, margin + x, where], ext[k, margin + x + width // 2, where], upper)
-
-        for j in range(width // 2):
-            side_a0[k, j] = side_a1[k, j] = edge(j, 1 - odd)
-            side_b[k, j] = edge(j, odd)
+        if k in LONG:
+            for j in range(width // 2):
+                for upper, to in ((1 - odd, (side_a0, side_a1)), (odd, (side_b,))):
+                    tile = edge_tile(low, rows_of(k, j, upper), rows_of(k, j + width // 2, upper), upper)
+                    for ref in to:
+                        ref[LONG.index(k) * (width // 2) + j] = tile
+    long_tiles, _ = side_tiles(width, margin)
+    depth = margin - 1
+    sub = lax.broadcasted_iota(jnp.int32, (SUB, lanes), 0)
+    for upper, to in ((1 - odd, (side_a0, side_a1)), (odd, (side_b,))):
+        tiles = {}
+        for k, x, t, at in short_places(width, depth):
+            rows_kx = rows_of(k, x, upper)
+            rows_kx = jnp.where(upper == 1, pltpu.roll(rows_kx, depth, 0), rows_kx)
+            rows_kx = pltpu.roll(rows_kx, at, 0) if at else rows_kx
+            tiles[t] = jnp.where(sub >= at, rows_kx, tiles[t]) if t in tiles else rows_kx
+            if at + depth > SUB:
+                tiles[t + 1] = rows_kx
+        for t, tile in tiles.items():
+            for ref in to:
+                ref[long_tiles + t] = tile
 
 
 def pack_x(margin, ext, out_x, in_x):
@@ -139,14 +170,39 @@
     width, rows, lanes = ext.shape[1] - 2 * margin, ext.shape[2] - SUB, ext.shape[3]
     _, at_y, core, odd = position()
     low = low_half(lanes)
+    has_after, has_before = at_y < count_y - 1, at_y > 0
     valid = valid_rows(low, at_y, count_y)
     in_first = lax.rem(at_y // 2, 2) == 0
+    long_tiles, short_tiles = side_tiles(width, margin)
+    depth = margin - 1
+    sub = lax.broadcasted_iota(jnp.int32, (SUB, lanes), 0)
+
+    def from_sides(t):
+        side_a = jnp.where(in_first, side_a0[t], side_a1[t])
+        return side_a, side_b[t]
+
+    after, before = [], []
+    for t in range(short_tiles):
+        from_a, from_b = from_sides(long_tiles + t)
+        after.append(jnp.where(odd == 0, from_a, from_b))
+        before.append(jnp.where(odd == 0, from_b, from_a))
+
+    def short_rows(tiles, t, at, to):
+        tile = tiles[t]
+        if at + depth > SUB:
+            tile = jnp.where(sub >= at, tile, tiles[t + 1])
+        return pltpu.roll(tile, (to - at) % SUB, 0) if (to - at) % SUB else tile
+
+    for k, x, t, at in short_places(width, depth):
+        blank = 1.0 if k == 6 else 0.0
+        tile = jnp.where((sub < depth) & jnp.broadcast_to(has_after, (SUB, lanes)), short_rows(after, t, at, 0), blank)
+        upper_rows = (sub >= SUB - depth) & jnp.broadcast_to(has_before, (SUB, lanes))
+        ext[k, margin + x, rows:] = jnp.where(upper_rows, short_rows(before, t, at, SUB - depth), tile)
     for k in range(7):
-        for x in range(width):
+        for x in range(width if k in LONG else 0):
             j, upper = x % (width // 2), x // (width // 2)
-            side_a = jnp.where(in_first, side_a0[k, j], side_a1[k, j])
-            tile = tail_tile(low, odd, side_a, side_b[k, j], upper)
-            ext[k, margin + x, rows:] = jnp.where(valid, tile, 1.0 if k == 6 else 0.0)
+            tile = tail_tile(low, odd, *from_sides(LONG.index(k) * (width // 2) + j), upper)
+            ext[k, margin + x, rows:] = jnp.where(valid, tile, 0.0)
         for j in range(margin):
             outer[k, j] = ext[k, margin + core * (width - margin) + j, rows:]
 
@@ -225,13 +281,13 @@
             ext[k, out_at + j, rows:] = tile
 
 
-def steps(margin, ranges, ext, forward, mask, masked, final):
+def steps(margin, ranges, product, ext, forward, mask, masked, final):
     width, rows, lanes = mask.shape
     high = rows + SUB
     at_x, at_y, _, _ = position()
     low = low_half(lanes)
     lane = lax.broadcasted_iota(jnp.int32, (high, lanes), 1)
-    first_lane = lane == 0
+    first_lane, last_lane = lane == 0, lane == lanes - 1
     before_rows = jnp.where(low | jnp.broadcast_to(at_y > 0, (SUB, lanes)), 1.0, 0.0)
     before_x = jnp.where(at_x > 0, 1.0, 0.0)
 
@@ -239,8 +295,8 @@
     ahead = jnp.where(gap == 1, 1.0, 0.0) - jnp.where(gap == 0, 1.0, 0.0)
     ahead = jnp.concatenate([ahead, ahead], 0).astype(jnp.bfloat16)
 
-    def ahead_z(k, first, end):
-        f = ext[k, first:end].reshape((end - first) * high, lanes)
+    def ahead_z(first, end):
+        f = ext[0:2, first:end].reshape(2 * (end - first) * high, lanes)
         main = f.astype(jnp.bfloat16)
         rest = (f - main.astype(jnp.float32)).astype(jnp.bfloat16)
         return jnp.dot(jnp.concatenate([main, rest], 1), ahead, preferred_element_type=jnp.float32)
@@ -251,12 +307,16 @@
     def last_y(f):
         return pltpu.roll(f, 1, 0)
 
+    def next_z(f):
+        return jnp.where(last_lane, 0.0, pltpu.roll(f, lanes - 1, 1))
+
     def last_z(f):
         return jnp.where(first_lane, 0.0, pltpu.roll(f, 1, 1))
 
     for turn, (first, first_e, end_h, end_e) in enumerate(ranges):
         last = turn == margin - 1
-        ahead_x, ahead_y = ahead_z(0, first, end_h), ahead_z(1, first, end_h)
+        if product:
+            both = ahead_z(first, end_h)
         held_y = held_z = None
         for i in range(first, end_e):
             ex, ey, ez = ext[0, i], ext[1, i], ext[2, i]
@@ -265,9 +325,12 @@
                 ey_x, ez_x = ext[1, i + 1], ext[2, i + 1]
                 if turn == 0:
                     hx, hy, hz = hx * (1 / COURANT), hy * (1 / COURANT), hz * (1 / COURANT)
-                here = slice((i - first) * high, (i - first + 1) * high)
-                hx = hx - ((next_y(ez) - ez) - ahead_y[here])
-                hy = hy - (ahead_x[here] - (ez_x - ez))
+                if product:
+                    ahead_x, ahead_y = (both[n * high : (n + 1) * high] for n in (i - first, i - first + end_h - first))
+                else:
+                    ahead_x, ahead_y = next_z(ex) - ex, next_z(ey) - ey
+                hx = hx - ((next_y(ez) - ez) - ahead_y)
+                hy = hy - (ahead_x - (ez_x - ez))
                 hz = hz - ((ey_x - ey) - (next_y(ex) - ex))
 
                 def clear(h):
@@ -327,16 +390,17 @@
     for c in range(2):
         @pl.when(core == c)
         def _():
-            steps(margin, inner_ranges(margin, width, c), ext, forward, mask, masked, final)
-
-
-def late_steps(margin, ext_in, masked_in, final_in, forward, mask, ext, masked, final):
+            steps(margin, inner_ranges(margin, width, c), True, ext, forward, mask, masked, final)
+
+
+def late_steps(margin, reach, rounds, ext_in, masked_in, final_in, forward, mask, weights, ext, masked, final, send):
     del ext_in, masked_in, final_in
     _, _, core, _ = position()
     for c in range(2):
         @pl.when(core == c)
         def _():
-            steps(margin, outer_ranges(margin, mask.shape[0], c), ext, forward, mask, masked, final)
+            steps(margin, outer_ranges(margin, mask.shape[0], c), False, ext, forward, mask, masked, final)
+    band_hop(reach, rounds, None, 1, True, weights, masked, send)
 
 
 def band_sum(reach, hop, sign, alone, weights, own, other, where, sums):
@@ -412,7 +476,7 @@
     block = shape((width, rows, lanes), f32)
     ext = shape((7, width + 2 * margin, rows + SUB, lanes), f32)
     strip = shape((planes, rows, lanes), f32)
-    edge = shape((7, width // 2, SUB, lanes), f32)
+    edge = shape((sum(side_tiles(width, margin)), SUB, lanes), f32)
     corner = shape((7, margin, SUB, lanes), f32)
     reach = width * routes.count_x // 4
     rounds = -(-reach // (2 * width))
@@ -526,16 +590,16 @@
         cost_estimate=cost(JOIN_X_US),
         name="join_corner",
     )(cells, outer)
-    _, masked, final = pl.pallas_call(
-        functools.partial(late_steps, margin),
-        out_shape=(ext, block, fields),
-        in_specs=[vmem] * 5,
-        out_specs=(vmem,) * 3,
+    _, masked, final, send_1 = pl.pallas_call(
+        functools.partial(late_steps, margin, reach, rounds),
+        out_shape=(ext, block, fields, block),
+        in_specs=[vmem] * 6,
+        out_specs=(vmem,) * 4,
         input_output_aliases={0: 0, 1: 1, 2: 2},
         compiler_params=params,
         cost_estimate=cost(JOIN_X_US),
         name="late_steps",
-    )(cells, masked, final, forward_e, design_mask)
+    )(cells, masked, final, forward_e, design_mask, weights)
 
     other = move(masked, routes.core)
     via = []
@@ -552,7 +616,8 @@
         )(*operands)
 
     for hop in range(rounds, 0, -1):
-        send_1 = hop_kernel(hop, 1, hop == rounds)
+        if hop < rounds:
+            send_1 = hop_kernel(hop, 1, False)
         send_0 = hop_kernel(hop, 0, False)
         via = [move(send_1, routes.ring_1), move(send_0, routes.ring_0)]
     base, final = pl.pallas_call(

time: 23 us -> 22.7 us (0.987)
  waiting for transfers between devices: 5.2 us -> 4.88 us
    ppermute x10, waiting for transfers between devices: 5.2 us -> 4.88 us  [move(): return lax.ppermute(value, BOTH, pairs)]
  transfers between devices with their start and end apart: 10 -> 10, of which waited for: 5 -> 4; matrix products, arithmetic and copies ran while one was open for 0% -> 0% of each run, Pallas kernels for 16% -> 16%
where the time goes in v6:
time: 22.7 us; the launch traced here: 22.6 us
  starting transfers between devices  10.3 us (45%)
  Pallas kernels  6.68 us (29%)
  waiting for transfers between devices  4.88 us (21%)
  between operations  0.75 us (3%)
    ppermute x10, starting transfers between devices, move(): return lax.ppermute(value, BOTH, pairs)  10.3 us
    ppermute x10, waiting for transfers between devices, move(): return lax.ppermute(value, BOTH, pairs)  4.88 us
    pallas_call x1, Pallas kernels, shards(): pl.pallas_call(functools.partial(pack_y, margin), out_shape=(ext, edge, e...  1.32 us
    pallas_call x1, Pallas kernels, shards(): pl.pallas_call(functools.partial(early_steps, margin, routes.count_y), ou...  1.29 us
    pallas_call x1, Pallas kernels, shards(): pl.pallas_call(load_rest, out_shape=(ext, pltpu.VMEM(forward_e.shape, for...  1.18 us
    pallas_call x1, Pallas kernels, shards(): pl.pallas_call(functools.partial(late_steps, margin, reach, rounds), out_...  0.97 us
    pallas_call x1, Pallas kernels, shards(): pl.pallas_call(functools.partial(band_own, reach), out_shape=(block, shap...  0.75 us
    pallas_call x1, Pallas kernels, shards(): pl.pallas_call(functools.partial(band_end, routes.count_x), out_shape=blo...  0.7 us
  transfers between devices with their start and end apart: 10, of which 4 were waited for; matrix products, arithmetic and copies ran while one was open for 0% of the time, Pallas kernels for 16%

profile of v6, /device:TPU:0, one launch (start us, length us, event | category | flops | bytes accessed | tf_op | source)
XLA Modules:
  0.0 22.6 jit_solution(5211532789642353857)
XLA Ops:
  0.6 1.3 %pack_y.1 = (f32[7,16,40,128]{3,2,1,0:T(8,128)S(1)}, f32[26,8,128]{2,1,0:T(8,128)S(1)}, f32[26,8,128]{2,1,0:T(8,128)S(1)}, f32[26,8,128]{2,1,0:T(8,128)S(1)}) custom-call(f32[6,8,32,128]{3,2,1,0:T(8,128)} %fields.1, f32[8,32,128]{2,1,0:T(8,128)} %perm.1), custom_call_target="tpu_custom_call" | custom-call | tf_op jit(solution)/shard_map/pack_y/pallas_call | solution.py:494
  2.0 3.0 %collective-permute-start = (f32[26,8,128]{2,1,0:T(8,128)S(1)}, f32[26,8,128]{2,1,0:T(8,128)S(1)}, u32[]{:S(2)}, u32[]{:S(2)}) collective-permute-start(f32[26,8,128]{2,1,0:T(8,128)S(1)} %get-tuple-element.27), channel_id=1, source_target_pairs={{0,1},{1,0},{2,6},{3,7},{4,5},{5,4},{6,2},{7,3},{8,9},{9,8},{10,14... | collective-permute-start | bytes 319496 | tf_op jit(solution)/shard_map/ppermute | solution.py:489
  5.0 0.5 %collective-permute-start.2 = (f32[26,8,128]{2,1,0:T(8,128)S(1)}, f32[26,8,128]{2,1,0:T(8,128)S(1)}, u32[]{:S(2)}, u32[]{:S(2)}) collective-permute-start(f32[26,8,128]{2,1,0:T(8,128)S(1)} %get-tuple-element.29), channel_id=1, source_target_pairs={{0,4},{1,5},{2,3},{3,2},{4,0},{5,1},{6,7},{7,6},{8,12},{9,13},{10,... | collective-permute-start | bytes 319496 | tf_op jit(solution)/shard_map/ppermute | solution.py:489
  5.5 0.1 pack_x.1
  5.5 0.1 collective-permute-start.3
  5.6 1.6 %collective-permute-start.5 = (f32[26,32,128]{2,1,0:T(8,128)S(1)}, f32[26,32,128]{2,1,0:T(8,128)S(1)}, u32[]{:S(2)}, u32[]{:S(2)}) collective-permute-start(f32[26,32,128]{2,1,0:T(8,128)S(1)} %get-tuple-element.37), channel_id=1, source_target_pairs={{0,1},{1,3},{2,0},{3,2},{4,8},{5,9},{6,10},{7,11},{8,4},{9,5},{10,... | collective-permute-start | bytes 1277960 | tf_op jit(solution)/shard_map/ppermute | solution.py:489
  7.2 1.2 %load_rest.1 = (f32[7,16,40,128]{3,2,1,0:T(8,128)S(1)}, bf16[4,3,8,32,128]{4,3,2,1,0:T(8,128)(2,1)S(1)}, s32[8,32,128]{2,1,0:T(8,128)S(1)}, f32[64,128]{1,0:T(8,128)S(1)}) custom-call(f32[7,16,40,128]{3,2,1,0:T(8,128)S(1)} %get-tuple-element.24.ext_in.ext, bf16[4,3,8,32,128]{4,3,2,1,0:T(8,128)(2,1)} %forward.1, ...), custom_call_target="tpu_custom_call", output_to_operand_aliasing={{0}: (0, {})} | custom-call | flops 50000000 | bytes 180000 | tf_op jit(solution)/shard_map/load_rest/pallas_call | solution.py:516
  8.4 0.0 collective-permute-done.side_a0
  8.4 0.1 join_y.1
  8.5 0.2 %collective-permute-start.4 = (f32[7,4,8,128]{3,2,1,0:T(8,128)S(1)}, f32[7,4,8,128]{3,2,1,0:T(8,128)S(1)}, u32[]{:S(2)}, u32[]{:S(2)}) collective-permute-start(f32[7,4,8,128]{3,2,1,0:T(8,128)S(1)} %get-tuple-element.35), channel_id=1, source_target_pairs={{0,4},{1,5},{2,6},{3,7},{4,0},{5,1},{6,2},{7,3},{8,12},{9,13},{10,... | collective-permute-start | bytes 344072 | tf_op jit(solution)/shard_map/ppermute | solution.py:489
  8.8 3.3 %collective-permute-start.6 = (f32[7,4,8,128]{3,2,1,0:T(8,128)S(1)}, f32[7,4,8,128]{3,2,1,0:T(8,128)S(1)}, u32[]{:S(2)}, u32[]{:S(2)}) collective-permute-start(f32[7,4,8,128]{3,2,1,0:T(8,128)S(1)} %get-tuple-element.38), channel_id=1, source_target_pairs={{0,1},{1,3},{2,0},{3,2},{4,8},{5,9},{6,10},{7,11},{8,4},{9,5},{10,... | collective-permute-start | bytes 344072 | tf_op jit(solution)/shard_map/ppermute | solution.py:489
  12.1 1.3 %early_steps.1 = (f32[7,16,40,128]{3,2,1,0:T(8,128)S(1)}, f32[8,32,128]{2,1,0:T(8,128)S(1)}, f32[3,8,32,128]{3,2,1,0:T(8,128)S(1)}) custom-call(f32[7,16,40,128]{3,2,1,0:T(8,128)S(1)} %join_core.1.ext_in, bf16[4,3,8,32,128]{4,3,2,1,0:T(8,128)(2,1)S(1)} %get-tuple-element.33.forward, ...), custom_call_target="tpu_custom_call", output_to_operand_aliasing={{0}: (0, {})} | custom-call | flops 50000000 | bytes 180000 | tf_op jit(solution)/shard_map/early_steps/pallas_call | solution.py:563
  13.4 0.4 %collective-permute-done.5.out_x = f32[26,32,128]{2,1,0:T(8,128)S(1)} collective-permute-done((f32[26,32,128]{2,1,0:T(8,128)S(1)}, f32[26,32,128]{2,1,0:T(8,128)S(1)}, u32[]{:S(2)}, u32[]{:S(2)}) %collective-permute-start.5) | collective-permute-done | bytes 426016 | tf_op jit(solution)/shard_map/ppermute | solution.py:489
  13.8 0.1 join_outer.1.ext_in
  13.8 1.2 %collective-permute-done.6.outer = f32[7,4,8,128]{3,2,1,0:T(8,128)S(1)} collective-permute-done((f32[7,4,8,128]{3,2,1,0:T(8,128)S(1)}, f32[7,4,8,128]{3,2,1,0:T(8,128)S(1)}, u32[]{:S(2)}, u32[]{:S(2)}) %collective-permute-start.6) | collective-permute-done | bytes 114720 | tf_op jit(solution)/shard_map/ppermute | solution.py:489
  15.0 1.0 %late_steps.1 = (f32[7,16,40,128]{3,2,1,0:T(8,128)S(1)}, f32[8,32,128]{2,1,0:T(8,128)S(1)}, f32[3,8,32,128]{3,2,1,0:T(8,128)S(1)}, f32[8,32,128]{2,1,0:T(8,128)S(1)}) custom-call(f32[7,16,40,128]{3,2,1,0:T(8,128)S(1)} %join_corner.1.ext_in, ...), custom_call_target="tpu_custom_call", output_to_operand_aliasing={{0}: (0, {}), {1}: (1, {}), {2}: (2, {})} | custom-call | flops 50000000 | bytes 180000 | tf_op jit(solution)/shard_map/late_steps/pallas_call | solution.py:593
  16.0 0.1 collective-permute-start.7
  16.1 0.5 %collective-permute-start.8 = (f32[8,32,128]{2,1,0:T(8,128)S(1)}, f32[8,32,128]{2,1,0:T(8,128)S(1)}, u32[]{:S(2)}, u32[]{:S(2)}) collective-permute-start(f32[8,32,128]{2,1,0:T(8,128)S(1)} %get-tuple-element.44), channel_id=1, source_target_pairs={{0,4},{1,5},{2,6},{3,7},{4,12},{5,13},{6,14},{7,15},{8,0},{9,1},{1... | collective-permute-start | bytes 393224 | tf_op jit(solution)/shard_map/ppermute | solution.py:489
  16.6 0.8 %collective-permute-done.7.other.refs_0_ = f32[8,32,128]{2,1,0:T(8,128)S(1)} collective-permute-done((f32[8,32,128]{2,1,0:T(8,128)S(1)}, f32[8,32,128]{2,1,0:T(8,128)S(1)}, u32[]{:S(2)}, u32[]{:S(2)}) %collective-permute-start.7) | collective-permute-done | bytes 131104 | tf_op jit(solution)/shard_map/ppermute | solution.py:489
  17.4 0.2 band_hop.1
  17.6 1.0 %collective-permute-start.9 = (f32[8,32,128]{2,1,0:T(8,128)S(1)}, f32[8,32,128]{2,1,0:T(8,128)S(1)}, u32[]{:S(2)}, u32[]{:S(2)}) collective-permute-start(f32[8,32,128]{2,1,0:T(8,128)S(1)} %band_hop.1), channel_id=1, source_target_pairs={{0,8},{1,9},{2,10},{3,11},{4,0},{5,1},{6,2},{7,3},{8,16},{9,17},{1... | collective-permute-start | bytes 393224 | tf_op jit(solution)/shard_map/ppermute | solution.py:489
  18.6 0.8 %band_own.1 = (f32[8,32,128]{2,1,0:T(8,128)S(1)}, f32[3,8,32,128]{3,2,1,0:T(8,128)}) custom-call(f32[64,128]{1,0:T(8,128)S(1)} %get-tuple-element.25.weights, f32[8,32,128]{2,1,0:T(8,128)S(1)} %get-tuple-element.41.own, f32[8,32,128]{2,1,0:T(8,128)S(1)} %collective-permute-done.7.other.refs_0_, f32[3,8,32,128]{3,2,1,0:T(8,128)S(1)} %get-tuple-element.42.final), custom_call_target="tpu_custom_call" | custom-call | flops 2000000000 | bytes 7200000 | tf_op jit(solution)/shard_map/band_own/pallas_call | solution.py:623
  19.4 2.5 %collective-permute-done.8.via_1 = f32[8,32,128]{2,1,0:T(8,128)S(1)} collective-permute-done((f32[8,32,128]{2,1,0:T(8,128)S(1)}, f32[8,32,128]{2,1,0:T(8,128)S(1)}, u32[]{:S(2)}, u32[]{:S(2)}) %collective-permute-start.8) | collective-permute-done | bytes 131104 | tf_op jit(solution)/shard_map/ppermute | solution.py:489
  21.9 0.7 %band_end.1 = f32[8,32,128]{2,1,0:T(8,128)} custom-call(f32[8,32,128]{2,1,0:T(8,128)S(1)} %get-tuple-element.43.base, f32[8,32,128]{2,1,0:T(8,128)S(1)} %collective-permute-done.8.via_1, f32[8,32,128]{2,1,0:T(8,128)S(1)} %collective-permute-done.9.via_0), custom_call_target="tpu_custom_call" | custom-call | tf_op jit(solution)/shard_map/band_end/pallas_call | solution.py:633
  (9 shorter events, 0.1 us)
Async XLA Ops:
  2.0 6.4 %collective-permute-start = (f32[26,8,128]{2,1,0:T(8,128)S(1)}, f32[26,8,128]{2,1,0:T(8,128)S(1)}, u32[]{:S(2)}, u32[]{:S(2)}) collective-permute-start(f32[26,8,128]{2,1,0:T(8,128)S(1)} %get-tuple-element.27), channel_id=1, source_target_pairs={{0,1},{1,0},{2,6},{3,7},{4,5},{5,4},{6,2},{7,3},{8,9},{9,8},{10,14... | collective-permute-start | bytes 319496 | tf_op jit(solution)/shard_map/ppermute | solution.py:489
  5.0 3.4 %collective-permute-start.1 = (f32[26,8,128]{2,1,0:T(8,128)S(1)}, f32[26,8,128]{2,1,0:T(8,128)S(1)}, u32[]{:S(2)}, u32[]{:S(2)}) collective-permute-start(f32[26,8,128]{2,1,0:T(8,128)S(1)} %get-tuple-element.28), channel_id=1, source_target_pairs={{0,4},{1,2},{2,1},{3,7},{4,0},{5,6},{6,5},{7,3},{8,12},{9,10},{10,... | collective-permute-start | bytes 319496 | tf_op jit(solution)/shard_map/ppermute | solution.py:489
  5.0 3.4 %collective-permute-start.2 = (f32[26,8,128]{2,1,0:T(8,128)S(1)}, f32[26,8,128]{2,1,0:T(8,128)S(1)}, u32[]{:S(2)}, u32[]{:S(2)}) collective-permute-start(f32[26,8,128]{2,1,0:T(8,128)S(1)} %get-tuple-element.29), channel_id=1, source_target_pairs={{0,4},{1,5},{2,3},{3,2},{4,0},{5,1},{6,7},{7,6},{8,12},{9,13},{10,... | collective-permute-start | bytes 319496 | tf_op jit(solution)/shard_map/ppermute | solution.py:489
  5.5 6.5 %collective-permute-start.3 = (f32[26,32,128]{2,1,0:T(8,128)S(1)}, f32[26,32,128]{2,1,0:T(8,128)S(1)}, u32[]{:S(2)}, u32[]{:S(2)}) collective-permute-start(f32[26,32,128]{2,1,0:T(8,128)S(1)} %get-tuple-element.32), channel_id=1, source_target_pairs={{0,4},{1,5},{2,6},{3,7},{4,0},{5,1},{6,2},{7,3},{8,12},{9,13},{10,... | collective-permute-start | bytes 1277960 | tf_op jit(solution)/shard_map/ppermute | solution.py:489
  5.6 8.2 %collective-permute-start.5 = (f32[26,32,128]{2,1,0:T(8,128)S(1)}, f32[26,32,128]{2,1,0:T(8,128)S(1)}, u32[]{:S(2)}, u32[]{:S(2)}) collective-permute-start(f32[26,32,128]{2,1,0:T(8,128)S(1)} %get-tuple-element.37), channel_id=1, source_target_pairs={{0,1},{1,3},{2,0},{3,2},{4,8},{5,9},{6,10},{7,11},{8,4},{9,5},{10,... | collective-permute-start | bytes 1277960 | tf_op jit(solution)/shard_map/ppermute | solution.py:489
  8.5 3.6 %collective-permute-start.4 = (f32[7,4,8,128]{3,2,1,0:T(8,128)S(1)}, f32[7,4,8,128]{3,2,1,0:T(8,128)S(1)}, u32[]{:S(2)}, u32[]{:S(2)}) collective-permute-start(f32[7,4,8,128]{3,2,1,0:T(8,128)S(1)} %get-tuple-element.35), channel_id=1, source_target_pairs={{0,4},{1,5},{2,6},{3,7},{4,0},{5,1},{6,2},{7,3},{8,12},{9,13},{10,... | collective-permute-start | bytes 344072 | tf_op jit(solution)/shard_map/ppermute | solution.py:489
  8.8 6.2 %collective-permute-start.6 = (f32[7,4,8,128]{3,2,1,0:T(8,128)S(1)}, f32[7,4,8,128]{3,2,1,0:T(8,128)S(1)}, u32[]{:S(2)}, u32[]{:S(2)}) collective-permute-start(f32[7,4,8,128]{3,2,1,0:T(8,128)S(1)} %get-tuple-element.38), channel_id=1, source_target_pairs={{0,1},{1,3},{2,0},{3,2},{4,8},{5,9},{6,10},{7,11},{8,4},{9,5},{10,... | collective-permute-start | bytes 344072 | tf_op jit(solution)/shard_map/ppermute | solution.py:489
  16.0 1.4 %collective-permute-start.7 = (f32[8,32,128]{2,1,0:T(8,128)S(1)}, f32[8,32,128]{2,1,0:T(8,128)S(1)}, u32[]{:S(2)}, u32[]{:S(2)}) collective-permute-start(f32[8,32,128]{2,1,0:T(8,128)S(1)} %get-tuple-element.41.own), channel_id=1, source_target_pairs={{0,4},{1,5},{2,6},{3,7},{4,0},{5,1},{6,2},{7,3},{8,12},{9,13},{10,... | collective-permute-start | bytes 393224 | tf_op jit(solution)/shard_map/ppermute | solution.py:489
  16.1 5.8 %collective-permute-start.8 = (f32[8,32,128]{2,1,0:T(8,128)S(1)}, f32[8,32,128]{2,1,0:T(8,128)S(1)}, u32[]{:S(2)}, u32[]{:S(2)}) collective-permute-start(f32[8,32,128]{2,1,0:T(8,128)S(1)} %get-tuple-element.44), channel_id=1, source_target_pairs={{0,4},{1,5},{2,6},{3,7},{4,12},{5,13},{6,14},{7,15},{8,0},{9,1},{1... | collective-permute-start | bytes 393224 | tf_op jit(solution)/shard_map/ppermute | solution.py:489
  17.6 4.3 %collective-permute-start.9 = (f32[8,32,128]{2,1,0:T(8,128)S(1)}, f32[8,32,128]{2,1,0:T(8,128)S(1)}, u32[]{:S(2)}, u32[]{:S(2)}) collective-permute-start(f32[8,32,128]{2,1,0:T(8,128)S(1)} %band_hop.1), channel_id=1, source_target_pairs={{0,8},{1,9},{2,10},{3,11},{4,0},{5,1},{6,2},{7,3},{8,16},{9,17},{1... | collective-permute-start | bytes 393224 | tf_op jit(solution)/shard_map/ppermute | solution.py:489

commit v7 on v6

--- a/solution.py
+++ b/solution.py
@@ -203,8 +203,11 @@
             j, upper = x % (width // 2), x // (width // 2)
             tile = tail_tile(low, odd, *from_sides(LONG.index(k) * (width // 2) + j), upper)
             ext[k, margin + x, rows:] = jnp.where(valid, tile, 0.0)
-        for j in range(margin):
-            outer[k, j] = ext[k, margin + core * (width - margin) + j, rows:]
+    at = 0
+    for k, depth in enumerate(depths(margin)):
+        for j in range(depth):
+            outer[at + j] = ext[k, margin + core * (width - depth) + j, rows:]
+        at += depth
 
 
 def join_inner(margin, count_y, ext_in, ext, inner):
@@ -212,9 +215,11 @@
     width, rows, lanes = ext.shape[1] - 2 * margin, ext.shape[2] - SUB, ext.shape[3]
     _, at_y, core, _ = position()
     valid = valid_rows(low_half(lanes), at_y, count_y)
-    for k in range(7):
-        for j in range(margin):
-            inner[k, j] = ext[k, margin + (1 - core) * (width - margin) + j, rows:]
+    at = 0
+    for k, depth in enumerate(depths(margin)):
+        for j in range(depth):
+            inner[at + j] = ext[k, margin + (1 - core) * (width - depth) + j, rows:]
+        at += depth
     scale = COURANT * COURANT
     for x in range(margin, margin + width):
         ext[6, x, 0:rows] = scale / ext[6, x, 0:rows]
@@ -274,11 +279,13 @@
     has_out = has_outward(at_x, core, count_x)
     valid = valid_rows(low_half(lanes), at_y, count_y) & jnp.broadcast_to(has_out, (SUB, lanes))
     out_at = core * (width + margin)
-    for k in range(7):
-        for j in range(margin):
-            tile = outer[k, j]
+    at = 0
+    for k, depth in enumerate(depths(margin)):
+        for j in range(depth):
+            tile = outer[at + j]
             tile = jnp.where(valid, COURANT * COURANT / tile, 0.0) if k == 6 else jnp.where(has_out, tile, 0.0)
-            ext[k, out_at + j, rows:] = tile
+            ext[k, out_at + (1 - core) * (margin - depth) + j, rows:] = tile
+        at += depth
 
 
 def steps(margin, ranges, product, ext, forward, mask, masked, final):
@@ -383,10 +390,13 @@
     _, at_y, core, _ = position()
     valid = valid_rows(low_half(lanes), at_y, count_y)
     in_at = (1 - core) * (width + margin)
-    for k in range(7):
-        for j in range(margin):
-            tile = inner[k, j]
-            ext[k, in_at + j, rows:] = jnp.where(valid, COURANT * COURANT / tile, 0.0) if k == 6 else tile
+    at = 0
+    for k, depth in enumerate(depths(margin)):
+        for j in range(depth):
+            tile = inner[at + j]
+            place = in_at + core * (margin - depth) + j
+            ext[k, place, rows:] = jnp.where(valid, COURANT * COURANT / tile, 0.0) if k == 6 else tile
+        at += depth
     for c in range(2):
         @pl.when(core == c)
         def _():
@@ -477,7 +487,7 @@
     ext = shape((7, width + 2 * margin, rows + SUB, lanes), f32)
     strip = shape((planes, rows, lanes), f32)
     edge = shape((sum(side_tiles(width, margin)), SUB, lanes), f32)
-    corner = shape((7, margin, SUB, lanes), f32)
+    corner = shape((planes, SUB, lanes), f32)
     reach = width * routes.count_x // 4
     rounds = -(-reach // (2 * width))
     distances = shape((4 * (rounds + 1) * width, lanes), f32)

time: 22.7 us -> 22.6 us (level)
  no operation moved by 1% of the time
where the time goes in v7:
time: 22.6 us; the launch traced here: 22.5 us
  starting transfers between devices  10.3 us (46%)
  Pallas kernels  6.65 us (29%)
  waiting for transfers between devices  4.8 us (21%)
  between operations  0.76 us (3%)
    ppermute x10, starting transfers between devices, move(): return lax.ppermute(value, BOTH, pairs)  10.3 us
    ppermute x10, waiting for transfers between devices, move(): return lax.ppermute(value, BOTH, pairs)  4.8 us
    pallas_call x1, Pallas kernels, shards(): pl.pallas_call(functools.partial(pack_y, margin), out_shape=(ext, edge, e...  1.32 us
    pallas_call x1, Pallas kernels, shards(): pl.pallas_call(functools.partial(early_steps, margin, routes.count_y), ou...  1.29 us
    pallas_call x1, Pallas kernels, shards(): pl.pallas_call(load_rest, out_shape=(ext, pltpu.VMEM(forward_e.shape, for...  1.18 us
    pallas_call x1, Pallas kernels, shards(): pl.pallas_call(functools.partial(late_steps, margin, reach, rounds), out_...  0.96 us
    pallas_call x1, Pallas kernels, shards(): pl.pallas_call(functools.partial(band_own, reach), out_shape=(block, shap...  0.75 us
    pallas_call x1, Pallas kernels, shards(): pl.pallas_call(functools.partial(band_end, routes.count_x), out_shape=blo...  0.69 us
  transfers between devices with their start and end apart: 10, of which 4 were waited for; matrix products, arithmetic and copies ran while one was open for 0% of the time, Pallas kernels for 16%

profile of v7, /device:TPU:0, one launch (start us, length us, event | category | flops | bytes accessed | tf_op | source)
XLA Modules:
  0.0 22.5 jit_solution(8719222175432050261)
XLA Ops:
  0.6 1.3 %pack_y.1 = (f32[7,16,40,128]{3,2,1,0:T(8,128)S(1)}, f32[26,8,128]{2,1,0:T(8,128)S(1)}, f32[26,8,128]{2,1,0:T(8,128)S(1)}, f32[26,8,128]{2,1,0:T(8,128)S(1)}) custom-call(f32[6,8,32,128]{3,2,1,0:T(8,128)} %fields.1, f32[8,32,128]{2,1,0:T(8,128)} %perm.1), custom_call_target="tpu_custom_call" | custom-call | tf_op jit(solution)/shard_map/pack_y/pallas_call | solution.py:504
  2.0 3.0 %collective-permute-start = (f32[26,8,128]{2,1,0:T(8,128)S(1)}, f32[26,8,128]{2,1,0:T(8,128)S(1)}, u32[]{:S(2)}, u32[]{:S(2)}) collective-permute-start(f32[26,8,128]{2,1,0:T(8,128)S(1)} %get-tuple-element.27), channel_id=1, source_target_pairs={{0,1},{1,0},{2,6},{3,7},{4,5},{5,4},{6,2},{7,3},{8,9},{9,8},{10,14... | collective-permute-start | bytes 319496 | tf_op jit(solution)/shard_map/ppermute | solution.py:499
  5.0 0.0 collective-permute-start.1
  5.0 0.5 %collective-permute-start.2 = (f32[26,8,128]{2,1,0:T(8,128)S(1)}, f32[26,8,128]{2,1,0:T(8,128)S(1)}, u32[]{:S(2)}, u32[]{:S(2)}) collective-permute-start(f32[26,8,128]{2,1,0:T(8,128)S(1)} %get-tuple-element.29), channel_id=1, source_target_pairs={{0,4},{1,5},{2,3},{3,2},{4,0},{5,1},{6,7},{7,6},{8,12},{9,13},{10,... | collective-permute-start | bytes 319496 | tf_op jit(solution)/shard_map/ppermute | solution.py:499
  5.5 0.1 pack_x.1
  5.5 0.1 collective-permute-start.3
  5.6 1.6 %collective-permute-start.5 = (f32[26,32,128]{2,1,0:T(8,128)S(1)}, f32[26,32,128]{2,1,0:T(8,128)S(1)}, u32[]{:S(2)}, u32[]{:S(2)}) collective-permute-start(f32[26,32,128]{2,1,0:T(8,128)S(1)} %get-tuple-element.37), channel_id=1, source_target_pairs={{0,1},{1,3},{2,0},{3,2},{4,8},{5,9},{6,10},{7,11},{8,4},{9,5},{10,... | collective-permute-start | bytes 1277960 | tf_op jit(solution)/shard_map/ppermute | solution.py:499
  7.2 1.2 %load_rest.1 = (f32[7,16,40,128]{3,2,1,0:T(8,128)S(1)}, bf16[4,3,8,32,128]{4,3,2,1,0:T(8,128)(2,1)S(1)}, s32[8,32,128]{2,1,0:T(8,128)S(1)}, f32[64,128]{1,0:T(8,128)S(1)}) custom-call(f32[7,16,40,128]{3,2,1,0:T(8,128)S(1)} %get-tuple-element.24.ext_in.ext, bf16[4,3,8,32,128]{4,3,2,1,0:T(8,128)(2,1)} %forward.1, ...), custom_call_target="tpu_custom_call", output_to_operand_aliasing={{0}: (0, {})} | custom-call | flops 50000000 | bytes 180000 | tf_op jit(solution)/shard_map/load_rest/pallas_call | solution.py:526
  8.4 0.1 join_y.1
  8.5 0.2 %collective-permute-start.4 = (f32[26,8,128]{2,1,0:T(8,128)S(1)}, f32[26,8,128]{2,1,0:T(8,128)S(1)}, u32[]{:S(2)}, u32[]{:S(2)}) collective-permute-start(f32[26,8,128]{2,1,0:T(8,128)S(1)} %get-tuple-element.35), channel_id=1, source_target_pairs={{0,4},{1,5},{2,6},{3,7},{4,0},{5,1},{6,2},{7,3},{8,12},{9,13},{10,... | collective-permute-start | bytes 319496 | tf_op jit(solution)/shard_map/ppermute | solution.py:499
  8.8 3.3 %collective-permute-start.6 = (f32[26,8,128]{2,1,0:T(8,128)S(1)}, f32[26,8,128]{2,1,0:T(8,128)S(1)}, u32[]{:S(2)}, u32[]{:S(2)}) collective-permute-start(f32[26,8,128]{2,1,0:T(8,128)S(1)} %get-tuple-element.38), channel_id=1, source_target_pairs={{0,1},{1,3},{2,0},{3,2},{4,8},{5,9},{6,10},{7,11},{8,4},{9,5},{10,... | collective-permute-start | bytes 319496 | tf_op jit(solution)/shard_map/ppermute | solution.py:499
  12.1 1.3 %early_steps.1 = (f32[7,16,40,128]{3,2,1,0:T(8,128)S(1)}, f32[8,32,128]{2,1,0:T(8,128)S(1)}, f32[3,8,32,128]{3,2,1,0:T(8,128)S(1)}) custom-call(f32[7,16,40,128]{3,2,1,0:T(8,128)S(1)} %join_core.1.ext_in, bf16[4,3,8,32,128]{4,3,2,1,0:T(8,128)(2,1)S(1)} %get-tuple-element.33.forward, ...), custom_call_target="tpu_custom_call", output_to_operand_aliasing={{0}: (0, {})} | custom-call | flops 50000000 | bytes 180000 | tf_op jit(solution)/shard_map/early_steps/pallas_call | solution.py:573
  13.4 0.4 %collective-permute-done.5.out_x = f32[26,32,128]{2,1,0:T(8,128)S(1)} collective-permute-done((f32[26,32,128]{2,1,0:T(8,128)S(1)}, f32[26,32,128]{2,1,0:T(8,128)S(1)}, u32[]{:S(2)}, u32[]{:S(2)}) %collective-permute-start.5) | collective-permute-done | bytes 426016 | tf_op jit(solution)/shard_map/ppermute | solution.py:499
  13.8 0.1 join_outer.1.ext_in
  13.8 1.1 %collective-permute-done.6.outer = f32[26,8,128]{2,1,0:T(8,128)S(1)} collective-permute-done((f32[26,8,128]{2,1,0:T(8,128)S(1)}, f32[26,8,128]{2,1,0:T(8,128)S(1)}, u32[]{:S(2)}, u32[]{:S(2)}) %collective-permute-start.6) | collective-permute-done | bytes 106528 | tf_op jit(solution)/shard_map/ppermute | solution.py:499
  15.0 1.0 %late_steps.1 = (f32[7,16,40,128]{3,2,1,0:T(8,128)S(1)}, f32[8,32,128]{2,1,0:T(8,128)S(1)}, f32[3,8,32,128]{3,2,1,0:T(8,128)S(1)}, f32[8,32,128]{2,1,0:T(8,128)S(1)}) custom-call(f32[7,16,40,128]{3,2,1,0:T(8,128)S(1)} %join_corner.1.ext_in, ...), custom_call_target="tpu_custom_call", output_to_operand_aliasing={{0}: (0, {}), {1}: (1, {}), {2}: (2, {})} | custom-call | flops 50000000 | bytes 180000 | tf_op jit(solution)/shard_map/late_steps/pallas_call | solution.py:603
  15.9 0.1 collective-permute-start.7
  16.0 0.5 %collective-permute-start.8 = (f32[8,32,128]{2,1,0:T(8,128)S(1)}, f32[8,32,128]{2,1,0:T(8,128)S(1)}, u32[]{:S(2)}, u32[]{:S(2)}) collective-permute-start(f32[8,32,128]{2,1,0:T(8,128)S(1)} %get-tuple-element.44), channel_id=1, source_target_pairs={{0,4},{1,5},{2,6},{3,7},{4,12},{5,13},{6,14},{7,15},{8,0},{9,1},{1... | collective-permute-start | bytes 393224 | tf_op jit(solution)/shard_map/ppermute | solution.py:499
  16.5 0.8 %collective-permute-done.7.other.refs_0_ = f32[8,32,128]{2,1,0:T(8,128)S(1)} collective-permute-done((f32[8,32,128]{2,1,0:T(8,128)S(1)}, f32[8,32,128]{2,1,0:T(8,128)S(1)}, u32[]{:S(2)}, u32[]{:S(2)}) %collective-permute-start.7) | collective-permute-done | bytes 131104 | tf_op jit(solution)/shard_map/ppermute | solution.py:499
  17.3 0.2 band_hop.1
  17.5 1.0 %collective-permute-start.9 = (f32[8,32,128]{2,1,0:T(8,128)S(1)}, f32[8,32,128]{2,1,0:T(8,128)S(1)}, u32[]{:S(2)}, u32[]{:S(2)}) collective-permute-start(f32[8,32,128]{2,1,0:T(8,128)S(1)} %band_hop.1), channel_id=1, source_target_pairs={{0,8},{1,9},{2,10},{3,11},{4,0},{5,1},{6,2},{7,3},{8,16},{9,17},{1... | collective-permute-start | bytes 393224 | tf_op jit(solution)/shard_map/ppermute | solution.py:499
  18.5 0.8 %band_own.1 = (f32[8,32,128]{2,1,0:T(8,128)S(1)}, f32[3,8,32,128]{3,2,1,0:T(8,128)}) custom-call(f32[64,128]{1,0:T(8,128)S(1)} %get-tuple-element.25.weights, f32[8,32,128]{2,1,0:T(8,128)S(1)} %get-tuple-element.41.own, f32[8,32,128]{2,1,0:T(8,128)S(1)} %collective-permute-done.7.other.refs_0_, f32[3,8,32,128]{3,2,1,0:T(8,128)S(1)} %get-tuple-element.42.final), custom_call_target="tpu_custom_call" | custom-call | flops 2000000000 | bytes 7200000 | tf_op jit(solution)/shard_map/band_own/pallas_call | solution.py:633
  19.3 2.5 %collective-permute-done.8.via_1 = f32[8,32,128]{2,1,0:T(8,128)S(1)} collective-permute-done((f32[8,32,128]{2,1,0:T(8,128)S(1)}, f32[8,32,128]{2,1,0:T(8,128)S(1)}, u32[]{:S(2)}, u32[]{:S(2)}) %collective-permute-start.8) | collective-permute-done | bytes 131104 | tf_op jit(solution)/shard_map/ppermute | solution.py:499
  21.8 0.7 %band_end.1 = f32[8,32,128]{2,1,0:T(8,128)} custom-call(f32[8,32,128]{2,1,0:T(8,128)S(1)} %get-tuple-element.43.base, f32[8,32,128]{2,1,0:T(8,128)S(1)} %collective-permute-done.8.via_1, f32[8,32,128]{2,1,0:T(8,128)S(1)} %collective-permute-done.9.via_0), custom_call_target="tpu_custom_call" | custom-call | tf_op jit(solution)/shard_map/band_end/pallas_call | solution.py:643
  (9 shorter events, 0.1 us)
Async XLA Ops:
  2.0 6.4 %collective-permute-start = (f32[26,8,128]{2,1,0:T(8,128)S(1)}, f32[26,8,128]{2,1,0:T(8,128)S(1)}, u32[]{:S(2)}, u32[]{:S(2)}) collective-permute-start(f32[26,8,128]{2,1,0:T(8,128)S(1)} %get-tuple-element.27), channel_id=1, source_target_pairs={{0,1},{1,0},{2,6},{3,7},{4,5},{5,4},{6,2},{7,3},{8,9},{9,8},{10,14... | collective-permute-start | bytes 319496 | tf_op jit(solution)/shard_map/ppermute | solution.py:499
  5.0 3.4 %collective-permute-start.1 = (f32[26,8,128]{2,1,0:T(8,128)S(1)}, f32[26,8,128]{2,1,0:T(8,128)S(1)}, u32[]{:S(2)}, u32[]{:S(2)}) collective-permute-start(f32[26,8,128]{2,1,0:T(8,128)S(1)} %get-tuple-element.28), channel_id=1, source_target_pairs={{0,4},{1,2},{2,1},{3,7},{4,0},{5,6},{6,5},{7,3},{8,12},{9,10},{10,... | collective-permute-start | bytes 319496 | tf_op jit(solution)/shard_map/ppermute | solution.py:499
  5.0 3.4 %collective-permute-start.2 = (f32[26,8,128]{2,1,0:T(8,128)S(1)}, f32[26,8,128]{2,1,0:T(8,128)S(1)}, u32[]{:S(2)}, u32[]{:S(2)}) collective-permute-start(f32[26,8,128]{2,1,0:T(8,128)S(1)} %get-tuple-element.29), channel_id=1, source_target_pairs={{0,4},{1,5},{2,3},{3,2},{4,0},{5,1},{6,7},{7,6},{8,12},{9,13},{10,... | collective-permute-start | bytes 319496 | tf_op jit(solution)/shard_map/ppermute | solution.py:499
  5.5 6.5 %collective-permute-start.3 = (f32[26,32,128]{2,1,0:T(8,128)S(1)}, f32[26,32,128]{2,1,0:T(8,128)S(1)}, u32[]{:S(2)}, u32[]{:S(2)}) collective-permute-start(f32[26,32,128]{2,1,0:T(8,128)S(1)} %get-tuple-element.32), channel_id=1, source_target_pairs={{0,4},{1,5},{2,6},{3,7},{4,0},{5,1},{6,2},{7,3},{8,12},{9,13},{10,... | collective-permute-start | bytes 1277960 | tf_op jit(solution)/shard_map/ppermute | solution.py:499
  5.6 8.2 %collective-permute-start.5 = (f32[26,32,128]{2,1,0:T(8,128)S(1)}, f32[26,32,128]{2,1,0:T(8,128)S(1)}, u32[]{:S(2)}, u32[]{:S(2)}) collective-permute-start(f32[26,32,128]{2,1,0:T(8,128)S(1)} %get-tuple-element.37), channel_id=1, source_target_pairs={{0,1},{1,3},{2,0},{3,2},{4,8},{5,9},{6,10},{7,11},{8,4},{9,5},{10,... | collective-permute-start | bytes 1277960 | tf_op jit(solution)/shard_map/ppermute | solution.py:499
  8.5 3.6 %collective-permute-start.4 = (f32[26,8,128]{2,1,0:T(8,128)S(1)}, f32[26,8,128]{2,1,0:T(8,128)S(1)}, u32[]{:S(2)}, u32[]{:S(2)}) collective-permute-start(f32[26,8,128]{2,1,0:T(8,128)S(1)} %get-tuple-element.35), channel_id=1, source_target_pairs={{0,4},{1,5},{2,6},{3,7},{4,0},{5,1},{6,2},{7,3},{8,12},{9,13},{10,... | collective-permute-start | bytes 319496 | tf_op jit(solution)/shard_map/ppermute | solution.py:499
  8.8 6.2 %collective-permute-start.6 = (f32[26,8,128]{2,1,0:T(8,128)S(1)}, f32[26,8,128]{2,1,0:T(8,128)S(1)}, u32[]{:S(2)}, u32[]{:S(2)}) collective-permute-start(f32[26,8,128]{2,1,0:T(8,128)S(1)} %get-tuple-element.38), channel_id=1, source_target_pairs={{0,1},{1,3},{2,0},{3,2},{4,8},{5,9},{6,10},{7,11},{8,4},{9,5},{10,... | collective-permute-start | bytes 319496 | tf_op jit(solution)/shard_map/ppermute | solution.py:499
  15.9 1.4 %collective-permute-start.7 = (f32[8,32,128]{2,1,0:T(8,128)S(1)}, f32[8,32,128]{2,1,0:T(8,128)S(1)}, u32[]{:S(2)}, u32[]{:S(2)}) collective-permute-start(f32[8,32,128]{2,1,0:T(8,128)S(1)} %get-tuple-element.41.own), channel_id=1, source_target_pairs={{0,4},{1,5},{2,6},{3,7},{4,0},{5,1},{6,2},{7,3},{8,12},{9,13},{10,... | collective-permute-start | bytes 393224 | tf_op jit(solution)/shard_map/ppermute | solution.py:499
  16.0 5.8 %collective-permute-start.8 = (f32[8,32,128]{2,1,0:T(8,128)S(1)}, f32[8,32,128]{2,1,0:T(8,128)S(1)}, u32[]{:S(2)}, u32[]{:S(2)}) collective-permute-start(f32[8,32,128]{2,1,0:T(8,128)S(1)} %get-tuple-element.44), channel_id=1, source_target_pairs={{0,4},{1,5},{2,6},{3,7},{4,12},{5,13},{6,14},{7,15},{8,0},{9,1},{1... | collective-permute-start | bytes 393224 | tf_op jit(solution)/shard_map/ppermute | solution.py:499
  17.5 4.3 %collective-permute-start.9 = (f32[8,32,128]{2,1,0:T(8,128)S(1)}, f32[8,32,128]{2,1,0:T(8,128)S(1)}, u32[]{:S(2)}, u32[]{:S(2)}) collective-permute-start(f32[8,32,128]{2,1,0:T(8,128)S(1)} %band_hop.1), channel_id=1, source_target_pairs={{0,8},{1,9},{2,10},{3,11},{4,0},{5,1},{6,2},{7,3},{8,16},{9,17},{1... | collective-permute-start | bytes 393224 | tf_op jit(solution)/shard_map/ppermute | solution.py:499

commit v8 on v7

--- a/solution.py
+++ b/solution.py
@@ -403,9 +403,10 @@
             steps(margin, inner_ranges(margin, width, c), True, ext, forward, mask, masked, final)
 
 
-def late_steps(margin, reach, rounds, ext_in, masked_in, final_in, forward, mask, weights, ext, masked, final, send):
-    del ext_in, masked_in, final_in
+def late_steps(margin, reach, rounds, count_x, count_y, ext_in, masked_in, final_in, outer, forward, mask, weights, ext, masked, final, send):
+    del masked_in, final_in
     _, _, core, _ = position()
+    join_corner(margin, count_x, count_y, ext_in, outer, ext)
     for c in range(2):
         @pl.when(core == c)
         def _():
@@ -590,26 +591,16 @@
         cost_estimate=cost(JOIN_X_US),
         name="join_outer",
     )(cells, out_x)
-    cells = pl.pallas_call(
-        functools.partial(join_corner, margin, routes.count_x, routes.count_y),
-        out_shape=ext,
-        in_specs=[vmem] * 2,
-        out_specs=vmem,
-        input_output_aliases={0: 0},
-        compiler_params=params,
-        cost_estimate=cost(JOIN_X_US),
-        name="join_corner",
-    )(cells, outer)
     _, masked, final, send_1 = pl.pallas_call(
-        functools.partial(late_steps, margin, reach, rounds),
+        functools.partial(late_steps, margin, reach, rounds, routes.count_x, routes.count_y),
         out_shape=(ext, block, fields, block),
-        in_specs=[vmem] * 6,
+        in_specs=[vmem] * 7,
         out_specs=(vmem,) * 4,
         input_output_aliases={0: 0, 1: 1, 2: 2},
         compiler_params=params,
         cost_estimate=cost(JOIN_X_US),
         name="late_steps",
-    )(cells, masked, final, forward_e, design_mask, weights)
+    )(cells, masked, final, outer, forward_e, design_mask, weights)
 
     other = move(masked, routes.core)
     via = []

time: 22.6 us -> 22.7 us (level)
    pallas_call x2 -> x1, Pallas kernels: 0.98 us -> 1.01 us  [shards(): pl.pallas_call(functools.partial(late_steps, margin, reach, rounds, route...]
  transfers between devices with their start and end apart: 10 -> 10, of which waited for: 4 -> 4; matrix products, arithmetic and copies ran while one was open for 0% -> 0% of each run, Pallas kernels for 16% -> 17%
where the time goes in v8:
time: 22.7 us; the launch traced here: 22.5 us
  starting transfers between devices  10.3 us (45%)
  Pallas kernels  6.78 us (30%)
  waiting for transfers between devices  4.69 us (21%)
  between operations  0.75 us (3%)
    ppermute x10, starting transfers between devices, move(): return lax.ppermute(value, BOTH, pairs)  10.3 us
    ppermute x10, waiting for transfers between devices, move(): return lax.ppermute(value, BOTH, pairs)  4.69 us
    pallas_call x1, Pallas kernels, shards(): pl.pallas_call(functools.partial(early_steps, margin, routes.count_y), ou...  1.39 us
    pallas_call x1, Pallas kernels, shards(): pl.pallas_call(functools.partial(pack_y, margin), out_shape=(ext, edge, e...  1.32 us
    pallas_call x1, Pallas kernels, shards(): pl.pallas_call(load_rest, out_shape=(ext, pltpu.VMEM(forward_e.shape, for...  1.18 us
    pallas_call x1, Pallas kernels, shards(): pl.pallas_call(functools.partial(late_steps, margin, reach, rounds, route...  1.01 us
    pallas_call x1, Pallas kernels, shards(): pl.pallas_call(functools.partial(band_own, reach), out_shape=(block, shap...  0.75 us
    pallas_call x1, Pallas kernels, shards(): pl.pallas_call(functools.partial(band_end, routes.count_x), out_shape=blo...  0.69 us
  transfers between devices with their start and end apart: 10, of which 4 were waited for; matrix products, arithmetic and copies ran while one was open for 0% of the time, Pallas kernels for 17%

profile of v8, /device:TPU:0, one launch (start us, length us, event | category | flops | bytes accessed | tf_op | source)
XLA Modules:
  0.0 22.5 jit_solution(4961113176214237212)
XLA Ops:
  0.6 1.3 %pack_y.1 = (f32[7,16,40,128]{3,2,1,0:T(8,128)S(1)}, f32[26,8,128]{2,1,0:T(8,128)S(1)}, f32[26,8,128]{2,1,0:T(8,128)S(1)}, f32[26,8,128]{2,1,0:T(8,128)S(1)}) custom-call(f32[6,8,32,128]{3,2,1,0:T(8,128)} %fields.1, f32[8,32,128]{2,1,0:T(8,128)} %perm.1), custom_call_target="tpu_custom_call" | custom-call | tf_op jit(solution)/shard_map/pack_y/pallas_call | solution.py:505
  2.0 3.0 %collective-permute-start = (f32[26,8,128]{2,1,0:T(8,128)S(1)}, f32[26,8,128]{2,1,0:T(8,128)S(1)}, u32[]{:S(2)}, u32[]{:S(2)}) collective-permute-start(f32[26,8,128]{2,1,0:T(8,128)S(1)} %get-tuple-element.27), channel_id=1, source_target_pairs={{0,1},{1,0},{2,6},{3,7},{4,5},{5,4},{6,2},{7,3},{8,9},{9,8},{10,14... | collective-permute-start | bytes 319496 | tf_op jit(solution)/shard_map/ppermute | solution.py:500
  5.0 0.0 collective-permute-start.1
  5.0 0.5 %collective-permute-start.2 = (f32[26,8,128]{2,1,0:T(8,128)S(1)}, f32[26,8,128]{2,1,0:T(8,128)S(1)}, u32[]{:S(2)}, u32[]{:S(2)}) collective-permute-start(f32[26,8,128]{2,1,0:T(8,128)S(1)} %get-tuple-element.29), channel_id=1, source_target_pairs={{0,4},{1,5},{2,3},{3,2},{4,0},{5,1},{6,7},{7,6},{8,12},{9,13},{10,... | collective-permute-start | bytes 319496 | tf_op jit(solution)/shard_map/ppermute | solution.py:500
  5.5 0.1 pack_x.1
  5.5 0.1 collective-permute-start.3
  5.6 1.6 %collective-permute-start.5 = (f32[26,32,128]{2,1,0:T(8,128)S(1)}, f32[26,32,128]{2,1,0:T(8,128)S(1)}, u32[]{:S(2)}, u32[]{:S(2)}) collective-permute-start(f32[26,32,128]{2,1,0:T(8,128)S(1)} %get-tuple-element.37), channel_id=1, source_target_pairs={{0,1},{1,3},{2,0},{3,2},{4,8},{5,9},{6,10},{7,11},{8,4},{9,5},{10,... | collective-permute-start | bytes 1277960 | tf_op jit(solution)/shard_map/ppermute | solution.py:500
  7.2 1.2 %load_rest.1 = (f32[7,16,40,128]{3,2,1,0:T(8,128)S(1)}, bf16[4,3,8,32,128]{4,3,2,1,0:T(8,128)(2,1)S(1)}, s32[8,32,128]{2,1,0:T(8,128)S(1)}, f32[64,128]{1,0:T(8,128)S(1)}) custom-call(f32[7,16,40,128]{3,2,1,0:T(8,128)S(1)} %get-tuple-element.24.ext_in.ext, bf16[4,3,8,32,128]{4,3,2,1,0:T(8,128)(2,1)} %forward.1, ...), custom_call_target="tpu_custom_call", output_to_operand_aliasing={{0}: (0, {})} | custom-call | flops 50000000 | bytes 180000 | tf_op jit(solution)/shard_map/load_rest/pallas_call | solution.py:527
  8.4 0.1 join_y.1
  8.5 0.2 %collective-permute-start.4 = (f32[26,8,128]{2,1,0:T(8,128)S(1)}, f32[26,8,128]{2,1,0:T(8,128)S(1)}, u32[]{:S(2)}, u32[]{:S(2)}) collective-permute-start(f32[26,8,128]{2,1,0:T(8,128)S(1)} %get-tuple-element.35), channel_id=1, source_target_pairs={{0,4},{1,5},{2,6},{3,7},{4,0},{5,1},{6,2},{7,3},{8,12},{9,13},{10,... | collective-permute-start | bytes 319496 | tf_op jit(solution)/shard_map/ppermute | solution.py:500
  8.8 3.3 %collective-permute-start.6 = (f32[26,8,128]{2,1,0:T(8,128)S(1)}, f32[26,8,128]{2,1,0:T(8,128)S(1)}, u32[]{:S(2)}, u32[]{:S(2)}) collective-permute-start(f32[26,8,128]{2,1,0:T(8,128)S(1)} %get-tuple-element.40), channel_id=1, source_target_pairs={{0,1},{1,3},{2,0},{3,2},{4,8},{5,9},{6,10},{7,11},{8,4},{9,5},{10,... | collective-permute-start | bytes 319496 | tf_op jit(solution)/shard_map/ppermute | solution.py:500
  12.1 1.4 %early_steps.1 = (f32[7,16,40,128]{3,2,1,0:T(8,128)S(1)}, f32[8,32,128]{2,1,0:T(8,128)S(1)}, f32[3,8,32,128]{3,2,1,0:T(8,128)S(1)}) custom-call(f32[7,16,40,128]{3,2,1,0:T(8,128)S(1)} %join_core.1.ext_in, bf16[4,3,8,32,128]{4,3,2,1,0:T(8,128)(2,1)S(1)} %get-tuple-element.33.forward, ...), custom_call_target="tpu_custom_call", output_to_operand_aliasing={{0}: (0, {})} | custom-call | flops 50000000 | bytes 180000 | tf_op jit(solution)/shard_map/early_steps/pallas_call | solution.py:574
  13.5 0.3 %collective-permute-done.5.out_x = f32[26,32,128]{2,1,0:T(8,128)S(1)} collective-permute-done((f32[26,32,128]{2,1,0:T(8,128)S(1)}, f32[26,32,128]{2,1,0:T(8,128)S(1)}, u32[]{:S(2)}, u32[]{:S(2)}) %collective-permute-start.5) | collective-permute-done | bytes 426016 | tf_op jit(solution)/shard_map/ppermute | solution.py:500
  13.8 0.1 join_outer.1.ext_in
  13.8 1.1 %collective-permute-done.6.outer = f32[26,8,128]{2,1,0:T(8,128)S(1)} collective-permute-done((f32[26,8,128]{2,1,0:T(8,128)S(1)}, f32[26,8,128]{2,1,0:T(8,128)S(1)}, u32[]{:S(2)}, u32[]{:S(2)}) %collective-permute-start.6) | collective-permute-done | bytes 106528 | tf_op jit(solution)/shard_map/ppermute | solution.py:500
  14.9 1.0 %late_steps.1 = (f32[7,16,40,128]{3,2,1,0:T(8,128)S(1)}, f32[8,32,128]{2,1,0:T(8,128)S(1)}, f32[3,8,32,128]{3,2,1,0:T(8,128)S(1)}, f32[8,32,128]{2,1,0:T(8,128)S(1)}) custom-call(f32[7,16,40,128]{3,2,1,0:T(8,128)S(1)} %join_outer.1.ext_in, f32[8,32,128]{2,1,0:T(8,128)S(1)} %get-tuple-element.38.masked_in, ...), custom_call_target="tpu_custom_call", output_to_operand_aliasing={{0}: (0, {}), {1}: (1, {}), {2}: (2, {})} | custom-call | flops 50000000 | bytes 180000 | tf_op jit(solution)/shard_map/late_steps/pallas_call | solution.py:594
  15.9 0.1 collective-permute-start.7
  16.0 0.5 %collective-permute-start.8 = (f32[8,32,128]{2,1,0:T(8,128)S(1)}, f32[8,32,128]{2,1,0:T(8,128)S(1)}, u32[]{:S(2)}, u32[]{:S(2)}) collective-permute-start(f32[8,32,128]{2,1,0:T(8,128)S(1)} %get-tuple-element.44), channel_id=1, source_target_pairs={{0,4},{1,5},{2,6},{3,7},{4,12},{5,13},{6,14},{7,15},{8,0},{9,1},{1... | collective-permute-start | bytes 393224 | tf_op jit(solution)/shard_map/ppermute | solution.py:500
  16.5 0.8 %collective-permute-done.7.other.refs_0_ = f32[8,32,128]{2,1,0:T(8,128)S(1)} collective-permute-done((f32[8,32,128]{2,1,0:T(8,128)S(1)}, f32[8,32,128]{2,1,0:T(8,128)S(1)}, u32[]{:S(2)}, u32[]{:S(2)}) %collective-permute-start.7) | collective-permute-done | bytes 131104 | tf_op jit(solution)/shard_map/ppermute | solution.py:500
  17.4 0.2 band_hop.1
  17.5 1.0 %collective-permute-start.9 = (f32[8,32,128]{2,1,0:T(8,128)S(1)}, f32[8,32,128]{2,1,0:T(8,128)S(1)}, u32[]{:S(2)}, u32[]{:S(2)}) collective-permute-start(f32[8,32,128]{2,1,0:T(8,128)S(1)} %band_hop.1), channel_id=1, source_target_pairs={{0,8},{1,9},{2,10},{3,11},{4,0},{5,1},{6,2},{7,3},{8,16},{9,17},{1... | collective-permute-start | bytes 393224 | tf_op jit(solution)/shard_map/ppermute | solution.py:500
  18.5 0.8 %band_own.1 = (f32[8,32,128]{2,1,0:T(8,128)S(1)}, f32[3,8,32,128]{3,2,1,0:T(8,128)}) custom-call(f32[64,128]{1,0:T(8,128)S(1)} %get-tuple-element.25.weights, f32[8,32,128]{2,1,0:T(8,128)S(1)} %get-tuple-element.41.own, f32[8,32,128]{2,1,0:T(8,128)S(1)} %collective-permute-done.7.other.refs_0_, f32[3,8,32,128]{3,2,1,0:T(8,128)S(1)} %get-tuple-element.42.final), custom_call_target="tpu_custom_call" | custom-call | flops 2000000000 | bytes 7200000 | tf_op jit(solution)/shard_map/band_own/pallas_call | solution.py:624
  19.3 2.5 %collective-permute-done.8.via_1 = f32[8,32,128]{2,1,0:T(8,128)S(1)} collective-permute-done((f32[8,32,128]{2,1,0:T(8,128)S(1)}, f32[8,32,128]{2,1,0:T(8,128)S(1)}, u32[]{:S(2)}, u32[]{:S(2)}) %collective-permute-start.8) | collective-permute-done | bytes 131104 | tf_op jit(solution)/shard_map/ppermute | solution.py:500
  21.8 0.7 %band_end.1 = f32[8,32,128]{2,1,0:T(8,128)} custom-call(f32[8,32,128]{2,1,0:T(8,128)S(1)} %get-tuple-element.43.base, f32[8,32,128]{2,1,0:T(8,128)S(1)} %collective-permute-done.8.via_1, f32[8,32,128]{2,1,0:T(8,128)S(1)} %collective-permute-done.9.via_0), custom_call_target="tpu_custom_call" | custom-call | tf_op jit(solution)/shard_map/band_end/pallas_call | solution.py:634
  (8 shorter events, 0.1 us)
Async XLA Ops:
  2.0 6.4 %collective-permute-start = (f32[26,8,128]{2,1,0:T(8,128)S(1)}, f32[26,8,128]{2,1,0:T(8,128)S(1)}, u32[]{:S(2)}, u32[]{:S(2)}) collective-permute-start(f32[26,8,128]{2,1,0:T(8,128)S(1)} %get-tuple-element.27), channel_id=1, source_target_pairs={{0,1},{1,0},{2,6},{3,7},{4,5},{5,4},{6,2},{7,3},{8,9},{9,8},{10,14... | collective-permute-start | bytes 319496 | tf_op jit(solution)/shard_map/ppermute | solution.py:500
  5.0 3.4 %collective-permute-start.1 = (f32[26,8,128]{2,1,0:T(8,128)S(1)}, f32[26,8,128]{2,1,0:T(8,128)S(1)}, u32[]{:S(2)}, u32[]{:S(2)}) collective-permute-start(f32[26,8,128]{2,1,0:T(8,128)S(1)} %get-tuple-element.28), channel_id=1, source_target_pairs={{0,4},{1,2},{2,1},{3,7},{4,0},{5,6},{6,5},{7,3},{8,12},{9,10},{10,... | collective-permute-start | bytes 319496 | tf_op jit(solution)/shard_map/ppermute | solution.py:500
  5.0 3.4 %collective-permute-start.2 = (f32[26,8,128]{2,1,0:T(8,128)S(1)}, f32[26,8,128]{2,1,0:T(8,128)S(1)}, u32[]{:S(2)}, u32[]{:S(2)}) collective-permute-start(f32[26,8,128]{2,1,0:T(8,128)S(1)} %get-tuple-element.29), channel_id=1, source_target_pairs={{0,4},{1,5},{2,3},{3,2},{4,0},{5,1},{6,7},{7,6},{8,12},{9,13},{10,... | collective-permute-start | bytes 319496 | tf_op jit(solution)/shard_map/ppermute | solution.py:500
  5.5 6.5 %collective-permute-start.3 = (f32[26,32,128]{2,1,0:T(8,128)S(1)}, f32[26,32,128]{2,1,0:T(8,128)S(1)}, u32[]{:S(2)}, u32[]{:S(2)}) collective-permute-start(f32[26,32,128]{2,1,0:T(8,128)S(1)} %get-tuple-element.32), channel_id=1, source_target_pairs={{0,4},{1,5},{2,6},{3,7},{4,0},{5,1},{6,2},{7,3},{8,12},{9,13},{10,... | collective-permute-start | bytes 1277960 | tf_op jit(solution)/shard_map/ppermute | solution.py:500
  5.6 8.2 %collective-permute-start.5 = (f32[26,32,128]{2,1,0:T(8,128)S(1)}, f32[26,32,128]{2,1,0:T(8,128)S(1)}, u32[]{:S(2)}, u32[]{:S(2)}) collective-permute-start(f32[26,32,128]{2,1,0:T(8,128)S(1)} %get-tuple-element.37), channel_id=1, source_target_pairs={{0,1},{1,3},{2,0},{3,2},{4,8},{5,9},{6,10},{7,11},{8,4},{9,5},{10,... | collective-permute-start | bytes 1277960 | tf_op jit(solution)/shard_map/ppermute | solution.py:500
  8.5 3.6 %collective-permute-start.4 = (f32[26,8,128]{2,1,0:T(8,128)S(1)}, f32[26,8,128]{2,1,0:T(8,128)S(1)}, u32[]{:S(2)}, u32[]{:S(2)}) collective-permute-start(f32[26,8,128]{2,1,0:T(8,128)S(1)} %get-tuple-element.35), channel_id=1, source_target_pairs={{0,4},{1,5},{2,6},{3,7},{4,0},{5,1},{6,2},{7,3},{8,12},{9,13},{10,... | collective-permute-start | bytes 319496 | tf_op jit(solution)/shard_map/ppermute | solution.py:500
  8.8 6.2 %collective-permute-start.6 = (f32[26,8,128]{2,1,0:T(8,128)S(1)}, f32[26,8,128]{2,1,0:T(8,128)S(1)}, u32[]{:S(2)}, u32[]{:S(2)}) collective-permute-start(f32[26,8,128]{2,1,0:T(8,128)S(1)} %get-tuple-element.40), channel_id=1, source_target_pairs={{0,1},{1,3},{2,0},{3,2},{4,8},{5,9},{6,10},{7,11},{8,4},{9,5},{10,... | collective-permute-start | bytes 319496 | tf_op jit(solution)/shard_map/ppermute | solution.py:500
  15.9 1.4 %collective-permute-start.7 = (f32[8,32,128]{2,1,0:T(8,128)S(1)}, f32[8,32,128]{2,1,0:T(8,128)S(1)}, u32[]{:S(2)}, u32[]{:S(2)}) collective-permute-start(f32[8,32,128]{2,1,0:T(8,128)S(1)} %get-tuple-element.41.own), channel_id=1, source_target_pairs={{0,4},{1,5},{2,6},{3,7},{4,0},{5,1},{6,2},{7,3},{8,12},{9,13},{10,... | collective-permute-start | bytes 393224 | tf_op jit(solution)/shard_map/ppermute | solution.py:500
  16.0 5.8 %collective-permute-start.8 = (f32[8,32,128]{2,1,0:T(8,128)S(1)}, f32[8,32,128]{2,1,0:T(8,128)S(1)}, u32[]{:S(2)}, u32[]{:S(2)}) collective-permute-start(f32[8,32,128]{2,1,0:T(8,128)S(1)} %get-tuple-element.44), channel_id=1, source_target_pairs={{0,4},{1,5},{2,6},{3,7},{4,12},{5,13},{6,14},{7,15},{8,0},{9,1},{1... | collective-permute-start | bytes 393224 | tf_op jit(solution)/shard_map/ppermute | solution.py:500
  17.5 4.3 %collective-permute-start.9 = (f32[8,32,128]{2,1,0:T(8,128)S(1)}, f32[8,32,128]{2,1,0:T(8,128)S(1)}, u32[]{:S(2)}, u32[]{:S(2)}) collective-permute-start(f32[8,32,128]{2,1,0:T(8,128)S(1)} %band_hop.1), channel_id=1, source_target_pairs={{0,8},{1,9},{2,10},{3,11},{4,0},{5,1},{6,2},{7,3},{8,16},{9,17},{1... | collective-permute-start | bytes 393224 | tf_op jit(solution)/shard_map/ppermute | solution.py:500
